TPU v7x, 32 devices: a whole 2x2x4 slice. The times are simulated.
32 devices in a mesh: groups: 2 (over x), row: 16 (over z, y, core).
Axes of the slice: x: 2, y: 2, z: 4, core: 2. Of those that a mesh axis runs over, the one named last changes fastest.
Arguments:
- pair_acts: bfloat16 [96, 48, 128], P(('groups', 'row')), parts along dimension 0, may hold values from -6 to 6
- res_mask: int32 [96], P('groups'), parts along dimension 0, may hold values 0 or 1
- chain_id: int32 [96], P('groups'), parts along dimension 0, may hold values from 0 to 3, never falling along the last dimension, each value on 1 to 24 neighbouring positions
- in_gain: float32 [128], replicated, may hold values from 0.1 to 1.9
- w_left: bfloat16 [128, 256], replicated, may hold values from -0.5 to 0.5
- w_right: bfloat16 [128, 256], replicated, may hold values from -0.5 to 0.5
- w_mult_gate: bfloat16 [128, 128], replicated, may hold values from -0.5 to 0.5
- mult_gain: float32 [128], replicated, may hold values from 0.1 to 1.9
- w_mult_out: bfloat16 [128, 128], replicated, may hold values from -0.5 to 0.5
- att_gain: float32 [128], replicated, may hold values from 0.1 to 1.9
- w_att: bfloat16 [128, 512], replicated, may hold values from -0.5 to 0.5
- w_pair_bias: bfloat16 [128, 4], replicated, may hold values from -0.5 to 0.5
- cross_bias: float32 [4], replicated, may hold values from -2 to 2
- w_att_out: bfloat16 [128, 128], replicated, may hold values from -0.5 to 0.5
Outputs:
- pair_out: bfloat16 [96, 48, 128], P(('groups', 'row')), parts along dimension 0
There are 2 independent parts, one for each index of `groups`. A program takes and returns all parts, laid end to end along the dimension named above; an argument that names none is the same for every part. Nothing has to cross between parts.
Inputs may be any that keep to these rules, and one draw needn't show every extreme that they name: `res_mask`: 1 marks a residue that is present, 0 a padded or missing one. `chain_id`: chains are contiguous runs of residues numbered from 0 in order; each has 1 to 24 residues and every number below 4 occurs.
All inputs are finite; a program needn't handle non-finite values.
Results may differ from a plain program's by a relative error of at most 0.0085.
Values may be sent and summed in bfloat16 or wider, within the bound.
No kernel may reach another device: no remote copies, remote signals or barrier semaphores. Data moves between devices by JAX's collectives and lax.ppermute only.
A program may use at most 64 MiB of HBM per device.

v0:
```python
import jax
import jax.numpy as jnp
from jax import lax
from jax.sharding import PartitionSpec as P

norm_eps = 1e-05


def layer_norm(tensor, norm_axis):
    tensor = tensor.astype(jnp.float32)
    average = jnp.mean(tensor, axis=norm_axis, keepdims=True)
    spread = jnp.mean(jnp.square(tensor - average), axis=norm_axis, keepdims=True)
    return (tensor - average) * lax.rsqrt(spread + norm_eps)


def edges_of(normed, weight, row_mask, mult_width):
    gate_part = jnp.einsum(
        "ikc,cm->mik", normed, weight[:, :mult_width], preferred_element_type=jnp.float32
    )
    value_part = jnp.einsum(
        "ikc,cm->mik", normed, weight[:, mult_width:], preferred_element_type=jnp.float32
    )
    return (row_mask[None] * jax.nn.sigmoid(gate_part) * value_part).astype(jnp.bfloat16)


def attend(normed_cols, bias_table, mask_float, chain_id, cross_bias, w_att, first_col):
    residues, col_count, _ = normed_cols.shape
    inner_dim = w_att.shape[1] // 4
    head_count = cross_bias.shape[0]
    head_dim = inner_dim // head_count

    def project(slot_idx):
        return jnp.einsum(
            "ijc,ce->ije",
            normed_cols,
            w_att[:, slot_idx * inner_dim : (slot_idx + 1) * inner_dim],
            preferred_element_type=jnp.float32,
        )

    query_all = (
        (project(0) * head_dim ** (-0.5))
        .astype(jnp.bfloat16)
        .reshape(residues, col_count, head_count, head_dim)
    )
    key_all = project(1).astype(jnp.bfloat16).reshape(residues, col_count, head_count, head_dim)
    value_all = project(2).astype(jnp.bfloat16).reshape(residues, col_count, head_count, head_dim)
    gate_att = jax.nn.sigmoid(project(3))
    crossing = (chain_id[:, None] != chain_id[None, :]).astype(jnp.float32)
    half_rows = residues // 2

    def column(col_index):
        query = lax.dynamic_index_in_dim(query_all, col_index, 1, keepdims=False)
        key_col = lax.dynamic_index_in_dim(key_all, col_index, 1, keepdims=False)
        value_col = lax.dynamic_index_in_dim(value_all, col_index, 1, keepdims=False)
        own_live = lax.dynamic_index_in_dim(mask_float, first_col + col_index, 0, keepdims=False)
        key_live = mask_float * own_live > 0
        pieces_out = []
        for block_idx in range(2):
            lower_row = block_idx * half_rows
            query_block = query[lower_row : lower_row + half_rows]
            scores = jnp.einsum(
                "ihd,khd->hki", query_block, key_col, preferred_element_type=jnp.float32
            )
            scores = scores + (
                bias_table[:, :, lower_row : lower_row + half_rows].astype(jnp.float32)
                + cross_bias[:, None, None] * crossing[None, :, lower_row : lower_row + half_rows]
            )
            scores = jnp.where(key_live[None, :, None], scores, -1000000000.0)
            weights = jax.nn.softmax(scores, axis=1).astype(jnp.bfloat16)
            pieces_out.append(
                jnp.einsum("hki,khd->ihd", weights, value_col, preferred_element_type=jnp.float32)
            )
        return jnp.concatenate(pieces_out, 0)

    outputs = lax.map(column, jnp.arange(col_count, dtype=jnp.int32))
    outputs = jnp.transpose(outputs, (1, 0, 2, 3)).reshape(residues, col_count, inner_dim)
    return (outputs * gate_att).astype(jnp.bfloat16)


def shards(
    pair_acts,
    res_mask,
    chain_id,
    in_gain,
    w_left,
    w_right,
    w_mult_gate,
    mult_gain,
    w_mult_out,
    att_gain,
    w_att,
    w_pair_bias,
    cross_bias,
    w_att_out,
):
    row_count = pair_acts.shape[0]
    mult_width = w_left.shape[1] // 2
    first_row = lax.axis_index("row") * row_count
    mask_float = res_mask.astype(jnp.float32)
    own_mask = lax.dynamic_slice_in_dim(mask_float, first_row, row_count)
    row_mask = own_mask[:, None] * mask_float[None, :]
    normed = (layer_norm(pair_acts, -1) * in_gain).astype(jnp.bfloat16)
    left_edges = edges_of(normed, w_left, row_mask, mult_width)
    right_edges = edges_of(normed, w_right, row_mask, mult_width)
    left_chan, right_chan = (
        lax.all_to_all(left_edges, "row", split_axis=0, concat_axis=1, tiled=True),
        lax.all_to_all(right_edges, "row", split_axis=0, concat_axis=1, tiled=True),
    )
    product = jnp.einsum(
        "cik,cjk->cij", left_chan, right_chan, preferred_element_type=jnp.float32
    ).astype(jnp.bfloat16)
    product_own = lax.all_to_all(product, "row", split_axis=1, concat_axis=0, tiled=True)
    product_norm = (layer_norm(product_own, 0) * mult_gain[:, None, None]).astype(jnp.bfloat16)
    gate_mult = jax.nn.sigmoid(
        jnp.einsum("ijc,cd->ijd", normed, w_mult_gate, preferred_element_type=jnp.float32)
    )
    update = jnp.einsum("mij,mc->ijc", product_norm, w_mult_out, preferred_element_type=jnp.float32)
    pair_mid = (pair_acts.astype(jnp.float32) + gate_mult * update).astype(jnp.bfloat16)
    normed_mid = (layer_norm(pair_mid, -1) * att_gain).astype(jnp.bfloat16)
    bias_piece = jnp.einsum(
        "kic,ch->hki", normed_mid, w_pair_bias, preferred_element_type=jnp.float32
    ).astype(jnp.bfloat16)
    bias_table = lax.all_gather(bias_piece, "row", axis=1, tiled=True)
    normed_cols = lax.all_to_all(normed_mid, "row", split_axis=1, concat_axis=0, tiled=True)
    gated = attend(normed_cols, bias_table, mask_float, chain_id, cross_bias, w_att, first_row)
    gated_rows = lax.all_to_all(gated, "row", split_axis=0, concat_axis=1, tiled=True)
    pair_out = pair_mid.astype(jnp.float32) + jnp.einsum(
        "ije,ec->ijc", gated_rows, w_att_out, preferred_element_type=jnp.float32
    )
    return pair_out.astype(jnp.bfloat16)


def solution(mesh):
    placed = (
        P(("groups", "row"), None, None),
        P("groups"),
        P("groups"),
        P(),
        P(),
        P(),
        P(),
        P(),
        P(),
        P(),
        P(),
        P(),
        P(),
        P(),
    )
    return jax.shard_map(
        shards,
        mesh=mesh,
        in_specs=placed,
        out_specs=P(("groups", "row"), None, None),
        check_vma=False,
    )
```

profile of v0, /device:TPU:0, one launch (start us, length us, event | category | flops | bytes accessed | tf_op | source)
XLA Modules:
  0.0 101.6 jit_solution(9254026986416031045)
XLA Ops:
  0.0 0.7 convert_element_type.88
  0.7 0.9 convert_reduce_fusion
  1.9 0.7 copy-done.7
  3.2 0.8 reshape.120
  3.9 7.5 %all-to-all-start = ((bf16[16,2,576]{2,1,0:T(2,128)(2,1)}), bf16[16,2,576]{2,1,0:T(2,128)(2,1)S(1)}, u32[]{:S(2)}, u32[]{:S(2)}) async-start(bf16[16,2,576]{2,1,0:T(2,128)(2,1)} %reshape.120), calls=%async_computation | async-start | bytes 81920 | tf_op jit(solution)/shard_map/all_to_all | solution.py:106
  12.1 0.8 reshape.118
  12.9 5.3 %all-to-all-done = bf16[16,2,576]{2,1,0:T(2,128)(2,1)S(1)} async-done(((bf16[16,2,576]{2,1,0:T(2,128)(2,1)}), bf16[16,2,576]{2,1,0:T(2,128)(2,1)S(1)}, u32[]{:S(2)}, u32[]{:S(2)}) %all-to-all-start) | async-done | bytes 36896 | tf_op jit(solution)/shard_map/all_to_all | solution.py:106
  18.2 3.5 %all-to-all-start.1 = ((bf16[16,2,576]{2,1,0:T(2,128)(2,1)}), bf16[16,2,576]{2,1,0:T(2,128)(2,1)S(1)}, u32[]{:S(2)}, u32[]{:S(2)}) async-start(bf16[16,2,576]{2,1,0:T(2,128)(2,1)} %reshape.118), calls=%async_computation.1 | async-start | bytes 81920 | tf_op jit(solution)/shard_map/all_to_all | solution.py:107
  22.2 6.2 %all-to-all-done.1 = bf16[16,2,576]{2,1,0:T(2,128)(2,1)S(1)} async-done(((bf16[16,2,576]{2,1,0:T(2,128)(2,1)}), bf16[16,2,576]{2,1,0:T(2,128)(2,1)S(1)}, u32[]{:S(2)}, u32[]{:S(2)}) %all-to-all-start.1) | async-done | bytes 36896 | tf_op jit(solution)/shard_map/all_to_all | solution.py:107
  28.8 0.8 reshape.122
  29.6 3.6 %all-to-all-start.2 = ((bf16[16,2,576]{2,1,0:T(2,128)(2,1)}), bf16[16,2,576]{2,1,0:T(2,128)(2,1)S(1)}, u32[]{:S(2)}, u32[]{:S(2)}) async-start(bf16[16,2,576]{2,1,0:T(2,128)(2,1)} %reshape.122), calls=%async_computation.2 | async-start | bytes 81920 | tf_op jit(solution)/shard_map/all_to_all | solution.py:112
  33.3 6.6 %all-to-all-done.2 = bf16[16,2,576]{2,1,0:T(2,128)(2,1)S(1)} async-done(((bf16[16,2,576]{2,1,0:T(2,128)(2,1)}), bf16[16,2,576]{2,1,0:T(2,128)(2,1)S(1)}, u32[]{:S(2)}, u32[]{:S(2)}) %all-to-all-start.2) | async-done | bytes 36896 | tf_op jit(solution)/shard_map/all_to_all | solution.py:112
  40.1 0.6 copy-done.12
  41.3 0.6 copy-done.10
  42.1 0.6 copy.54
  42.7 3.6 %all-to-all-start.3 = ((bf16[3,48,128]{2,0,1:T(4,128)(2,1)}), bf16[3,48,128]{2,0,1:T(4,128)(2,1)S(1)}, u32[]{:S(2)}, u32[]{:S(2)}) async-start(bf16[3,48,128]{2,0,1:T(4,128)(2,1)} %copy.54), calls=%async_computation.3 | async-start | bytes 98304 | tf_op jit(solution)/shard_map/all_to_all | solution.py:124
  46.5 21.8 %all_gather.3 = bf16[4,48,48]{2,0,1:T(4,128)(2,1)S(1)} all-gather(bf16[4,3,48]{2,0,1:T(4,128)(2,1)S(1)} %fusion.60), channel_id=1, replica_groups=mesh['groups'=2,'row'=16] {'row'}, dimensions={1}, use_global_device_ids=true | all-gather | bytes 19584 | tf_op jit(solution)/shard_map/all_gather | solution.py:123
  68.5 0.7 copy-done.2
  70.1 0.6 copy-done.3
  70.8 19.4 %while.10 = (s32[]{:T(128)}, f32[3,48,4,32]{3,1,2,0:T(8,128)S(1)}, s32[3]{0:T(128)S(1)}, bf16[48,3,4,32]{0,3,2,1:T(8,128)(2,1)S(1)}, s32[]{:T(128)}, /*index=5*/...) while((s32[]{:T(128)}, f32[3,48,4,32]{3,1,2,0:T(8,128)S(1)}, ...), condition=%wide.region_11.12_spmd, body=%wide.region_6.11_spmd.sunk | while | flops 1914342 | bytes 962825 | solution.py:75
  70.8 0.7 dynamic_slice.60
  72.1 0.6 dynamic_slice.61
  72.7 0.6 multiply_compare_fusion.2
  77.2 0.7 dynamic_slice.60
  78.6 0.6 dynamic_slice.61
  79.2 0.6 multiply_compare_fusion.2
  83.7 0.7 dynamic_slice.60
  85.1 0.6 dynamic_slice.61
  85.7 0.6 multiply_compare_fusion.2
  90.7 9.3 %all_to_all.81 = bf16[48,3,128]{2,1,0:T(4,128)(2,1)S(1)} all-to-all(bf16[48,3,128]{2,1,0:T(4,128)(2,1)S(1)} %copy.64), channel_id=1, replica_groups=mesh['groups'=2,'row'=16] {'row'}, dimensions={0} | all-to-all | bytes 73728 | tf_op jit(solution)/shard_map/all_to_all | solution.py:126
  100.1 0.7 copy-done.4
  100.8 0.8 fusion.57
  (93 shorter events, 10.5 us)
Async XLA Ops:
  0.0 40.1 %copy-start = (bf16[128,128]{1,0:T(8,128)(2,1)S(1)}, bf16[128,128]{1,0:T(8,128)(2,1)}, u32[]{:S(2)}) copy-start(bf16[128,128]{1,0:T(8,128)(2,1)} %param.24) | copy-start | bytes 98308
  0.0 1.6 %copy-start.1 = (bf16[3,48,128]{2,1,0:T(8,128)(2,1)S(1)}, bf16[3,48,128]{2,1,0:T(8,128)(2,1)}, u32[]{:S(2)}) copy-start(bf16[3,48,128]{2,1,0:T(8,128)(2,1)} %param.16) | copy-start | bytes 110596
  0.0 1.9 %copy-start.5 = (bf16[128,256]{1,0:T(8,128)(2,1)S(1)}, bf16[128,256]{1,0:T(8,128)(2,1)}, u32[]{:S(2)}) copy-start(bf16[128,256]{1,0:T(8,128)(2,1)} %param.20) | copy-start | bytes 196612
  1.9 0.7 copy-start.7
  3.9 7.5 %copy-start.6 = (bf16[128,256]{1,0:T(8,128)(2,1)S(1)}, bf16[128,256]{1,0:T(8,128)(2,1)}, u32[]{:S(2)}) copy-start(bf16[128,256]{1,0:T(8,128)(2,1)} %param.21) | copy-start | bytes 196612
  3.9 14.2 %all-to-all-start = ((bf16[16,2,576]{2,1,0:T(2,128)(2,1)}), bf16[16,2,576]{2,1,0:T(2,128)(2,1)S(1)}, u32[]{:S(2)}, u32[]{:S(2)}) async-start(bf16[16,2,576]{2,1,0:T(2,128)(2,1)} %reshape.120), calls=%async_computation | async-start | bytes 81920 | tf_op jit(solution)/shard_map/all_to_all | solution.py:106
  12.9 8.8 %copy-start.11 = (bf16[128,128]{1,0:T(8,128)(2,1)S(1)}, bf16[128,128]{1,0:T(8,128)(2,1)}, u32[]{:S(2)}) copy-start(bf16[128,128]{1,0:T(8,128)(2,1)} %param.22) | copy-start | bytes 98308
  18.2 10.2 %all-to-all-start.1 = ((bf16[16,2,576]{2,1,0:T(2,128)(2,1)}), bf16[16,2,576]{2,1,0:T(2,128)(2,1)S(1)}, u32[]{:S(2)}, u32[]{:S(2)}) async-start(bf16[16,2,576]{2,1,0:T(2,128)(2,1)} %reshape.118), calls=%async_computation.1 | async-start | bytes 81920 | tf_op jit(solution)/shard_map/all_to_all | solution.py:107
  29.6 3.6 %copy-start.8 = (s32[48]{0:T(128)S(1)}, s32[48]{0:T(128)}, u32[]{:S(2)}) copy-start(s32[48]{0:T(128)} %param.18) | copy-start | bytes 580
  29.6 10.3 %all-to-all-start.2 = ((bf16[16,2,576]{2,1,0:T(2,128)(2,1)}), bf16[16,2,576]{2,1,0:T(2,128)(2,1)S(1)}, u32[]{:S(2)}, u32[]{:S(2)}) async-start(bf16[16,2,576]{2,1,0:T(2,128)(2,1)} %reshape.122), calls=%async_computation.2 | async-start | bytes 81920 | tf_op jit(solution)/shard_map/all_to_all | solution.py:112
  40.1 0.7 copy-start.12
  41.3 0.7 copy-start.10
  42.7 3.6 %copy-start.9 = (bf16[128,4]{0,1:T(4,128)(2,1)S(1)}, bf16[128,4]{0,1:T(4,128)(2,1)}, u32[]{:S(2)}) copy-start(bf16[128,4]{0,1:T(4,128)(2,1)} %param.27) | copy-start | bytes 3076
  42.7 25.7 %all-to-all-start.3 = ((bf16[3,48,128]{2,0,1:T(4,128)(2,1)}), bf16[3,48,128]{2,0,1:T(4,128)(2,1)S(1)}, u32[]{:S(2)}, u32[]{:S(2)}) async-start(bf16[3,48,128]{2,0,1:T(4,128)(2,1)} %copy.54), calls=%async_computation.3 | async-start | bytes 98304 | tf_op jit(solution)/shard_map/all_to_all | solution.py:124
  68.3 0.9 copy-start.2
  70.1 0.7 copy-start.3
  100.0 0.8 copy-start.4
where the time goes:
time: 102 us
  blocking collectives  31.1 us (30%)
  starting transfers between devices  18.3 us (18%)
  waiting for transfers between devices  18.1 us (18%)
  local copies, waits for them, and re-layouts  12.5 us (12%)
  matrix products  8.73 us (9%)
  loops' own time  8.47 us (8%)
  other arithmetic  3.97 us (4%)
    all_gather x1, blocking collectives, shards(): bias_table = lax.all_gather(bias_piece, 'row', axis=1, tiled=True)  21.8 us
    all_to_all x1, blocking collectives, shards(): lax.all_to_all(gated, 'row', split_axis=0, concat_axis=1, tiled=True)  9.34 us
    another operation x1, loops' own time, attend(): outputs = lax.map(column, jnp.arange(col_count, dtype=jnp.int32))  8.47 us
    all_to_all x1, starting transfers between devices, shards(): lax.all_to_all(left_edges, 'row', split_axis=0, concat_axis=1, tiled=True)  7.52 us
    unnamed x32, local copies, waits for them, and re-layouts  6.83 us
    all_to_all x1, waiting for transfers between devices, shards(): lax.all_to_all(product, 'row', split_axis=1, concat_axis=0, tiled=True)  6.58 us
    all_to_all x1, waiting for transfers between devices, shards(): lax.all_to_all(right_edges, 'row', split_axis=0, concat_axis=1, tiled=True)  6.18 us
    all_to_all x1, waiting for transfers between devices, shards(): lax.all_to_all(left_edges, 'row', split_axis=0, concat_axis=1, tiled=True)  5.29 us
  transfers between devices with their start and end apart: 4, of which 3 were waited for; matrix products, arithmetic and copies ran while one was open for 2% of the time, Pallas kernels for 0%

commit v1 on v0

--- a/solution.py
+++ b/solution.py
@@ -1,9 +1,14 @@
+import functools
+
 import jax
 import jax.numpy as jnp
 from jax import lax
+from jax.experimental import pallas as pl
+from jax.experimental.pallas import tpu as pltpu
 from jax.sharding import PartitionSpec as P
 
 norm_eps = 1e-05
+vmem_share = 4 * 2**20
 
 
 def layer_norm(tensor, norm_axis):
@@ -130,6 +135,323 @@
     return pair_out.astype(jnp.bfloat16)
 
 
+def dot(a, b):
+    return jnp.dot(a, b, preferred_element_type=jnp.float32)
+
+
+def dot_t(a, b):
+    return lax.dot_general(a, b, (((1,), (1,)), ((), ())), preferred_element_type=jnp.float32)
+
+
+def sigmoid(x):
+    return 1.0 / (1.0 + jnp.exp(-x))
+
+
+def norm_rows(x, gain):
+    average = jnp.mean(x, axis=-1, keepdims=True)
+    centred = x - average
+    spread = jnp.mean(centred * centred, axis=-1, keepdims=True)
+    return centred * lax.rsqrt(spread + norm_eps) * gain
+
+
+def right_kernel(offsets, row_count, me_ref, live_ref, held_ref, come_ref, gain_ref, w_ref, acts_ref, normed_ref, right_ref):
+    residues = come_ref.shape[1]
+    width = w_ref.shape[1] // 2
+    pieces = len(offsets) // 2
+    for t, offset in enumerate(offsets):
+        source, at = (held_ref, t) if t < pieces else (come_ref, t - pieces)
+        place = jnp.bitwise_xor(me_ref[0], offset) // 2
+        acts_ref[pl.ds(place * row_count, row_count)] = source[at * row_count : (at + 1) * row_count]
+
+    own_count = acts_ref.shape[0]
+    step_rows = row_count
+    core = me_ref[0] % 2
+    live_all = live_ref[...]
+    for chip in range(own_count // row_count):
+        lower = chip * row_count
+        x = acts_ref[lower : lower + row_count].astype(jnp.float32)
+        normed = norm_rows(x, gain_ref[...])
+        rows = []
+        for r in range(row_count):
+            live = me_ref[1 + (2 * chip + core) * row_count + r].astype(jnp.float32)
+            rows.append(normed[r] * (live_all * live))
+        normed = jnp.concatenate(rows, 0).astype(jnp.bfloat16)
+        normed_ref[lower * residues : (lower + row_count) * residues] = normed
+        both = dot(normed, w_ref[...])
+        edges = (sigmoid(both[:, :width]) * both[:, width:]).astype(jnp.bfloat16)
+        right_ref[lower * residues : (lower + row_count) * residues] = edges
+
+
+def left_kernel(step_rows, normed_ref, w_left_ref, w_gate_ref, left_ref, gate_ref):
+    width = w_left_ref.shape[1] // 2
+    for lower in range(0, normed_ref.shape[0], step_rows):
+        normed = normed_ref[lower : lower + step_rows]
+        both = dot(normed, w_left_ref[...])
+        edges = sigmoid(both[:, :width]) * both[:, width:]
+        left_ref[lower : lower + step_rows] = edges.astype(jnp.bfloat16).astype(jnp.float32)
+        gate_ref[lower : lower + step_rows] = sigmoid(dot(normed, w_gate_ref[...]))
+
+
+def product_kernel(
+    row_count,
+    me_ref,
+    left_ref,
+    right_ref,
+    other_ref,
+    gate_ref,
+    acts_ref,
+    mult_gain_ref,
+    w_out_ref,
+    att_gain_ref,
+    mid_ref,
+    normed_mid_ref,
+    turned_ref,
+    product_ref,
+):
+    own_count, residues, _ = acts_ref.shape
+    core = me_ref[0] % 2
+    for source, side in ((right_ref, core), (other_ref, 1 - core)):
+        for local in range(own_count):
+            spot = (2 * (local // row_count) + side) * row_count + local % row_count
+            turned_ref[pl.ds(spot, residues, stride=residues), :] = source[
+                local * residues : (local + 1) * residues
+            ].astype(jnp.float32)
+
+    row_block, tile = 4, 8
+    tiles = residues // tile
+
+    def rows_of(block, carry):
+        first = block * row_block
+
+        def add(k, totals):
+            ahead = [
+                turned_ref[pl.ds(pl.multiple_of(k * residues + t * tile, tile), tile), :]
+                for t in range(tiles)
+            ]
+            out = []
+            for a in range(row_block):
+                one = left_ref[pl.ds((first + a) * residues + k, 1), :]
+                out.extend(totals[a * tiles + t] + one * ahead[t] for t in range(tiles))
+            return tuple(out)
+
+        totals = lax.fori_loop(
+            0,
+            residues,
+            add,
+            tuple(jnp.zeros((tile, left_ref.shape[1]), jnp.float32) for _ in range(row_block * tiles)),
+            unroll=8,
+        )
+        for a in range(row_block):
+            for t in range(tiles):
+                product_ref[pl.ds(pl.multiple_of((first + a) * residues + t * tile, tile), tile), :] = (
+                    totals[a * tiles + t]
+                )
+        return carry
+
+    lax.fori_loop(0, own_count // row_block, rows_of, 0)
+
+    for local in range(0, own_count, row_count):
+        at = slice(local * residues, (local + row_count) * residues)
+        product = product_ref[at].astype(jnp.bfloat16).astype(jnp.float32)
+        product = norm_rows(product, mult_gain_ref[...]).astype(jnp.bfloat16)
+        update = gate_ref[at] * dot(product, w_out_ref[...])
+        acts = acts_ref[local : local + row_count].astype(jnp.float32).reshape(update.shape)
+        mid = (acts + update).astype(jnp.bfloat16)
+        mid_ref[at] = mid
+        normed_mid_ref[at] = norm_rows(mid.astype(jnp.float32), att_gain_ref[...]).astype(jnp.bfloat16)
+
+
+def attend_kernel(
+    row_count,
+    me_ref,
+    cross_ref,
+    mid_ref,
+    own_ref,
+    other_ref,
+    crossing_ref,
+    keep_ref,
+    w_att_ref,
+    w_bias_ref,
+    w_out_ref,
+    out_ref,
+    pair_ref,
+    query_ref,
+    context_ref,
+):
+    residues = pair_ref.shape[1]
+    heads = w_bias_ref.shape[0]
+    inner = w_out_ref.shape[0]
+    head_dim = inner // heads
+    channels = pair_ref.shape[2]
+    core = me_ref[0] % 2
+    chip = me_ref[0] // 2
+    own_count = residues // 2
+    for source, side in ((own_ref, core), (other_ref, 1 - core)):
+        for local in range(own_count):
+            spot = (2 * (local // row_count) + side) * row_count + local % row_count
+            pair_ref[pl.ds(spot, 1)] = source[local * residues : (local + 1) * residues].astype(jnp.float32)[None]
+
+    first = me_ref[0] * row_count
+    mine = pair_ref[pl.ds(first, row_count)].reshape(row_count * residues, channels).astype(jnp.bfloat16)
+    query = (dot(mine, w_att_ref[:, :inner]) * head_dim ** (-0.5)).astype(jnp.bfloat16)
+    gate = sigmoid(dot(mine, w_att_ref[:, 3 * inner :]))
+    head_of = lax.broadcasted_iota(jnp.int32, (1, inner), 1) // head_dim
+    for h in range(heads):
+        w_key = jnp.where(head_of == h, w_att_ref[:, inner : 2 * inner], 0)
+        query_ref[h] = dot_t(query, w_key).reshape(row_count, residues, channels)
+
+    tile = 8
+    wide = residues * tile
+    pieces = []
+    for i in range(row_count):
+        column = pair_ref[:, pl.ds(first + i, 1), :]
+        spread = jnp.broadcast_to(column, (residues, tile, channels)).reshape(wide, channels)
+        bias = dot_t(w_bias_ref[...], spread.astype(jnp.bfloat16)).astype(jnp.bfloat16).astype(jnp.float32)
+        crossing = crossing_ref[i : i + 1, :]
+        pieces.append([bias[h : h + 1] + cross_ref[h] * crossing for h in range(heads)])
+    extra = jnp.concatenate(
+        [jnp.broadcast_to(pieces[i][h], (tile, wide)) for h in range(heads) for i in range(row_count)], 0
+    )
+    total_rows = heads * row_count * tile
+    same = (
+        lax.broadcasted_iota(jnp.int32, (total_rows, wide), 0) % tile
+        == lax.broadcasted_iota(jnp.int32, (total_rows, wide), 1) % tile
+    )
+    for g in range(residues // tile):
+        keys = pair_ref[:, g * tile : (g + 1) * tile, :].reshape(wide, channels).astype(jnp.bfloat16)
+        asked = query_ref[:, :, g * tile : (g + 1) * tile, :].reshape(total_rows, channels).astype(jnp.bfloat16)
+        scores = dot_t(asked, keys) + extra
+        scores = jnp.where(keep_ref[g : g + 1, :] > 0, scores, -1000000000.0)
+        scores = jnp.where(same, scores, -1e30)
+        scores = jnp.exp(scores - jnp.max(scores, axis=-1, keepdims=True))
+        weights = (scores / jnp.sum(scores, axis=-1, keepdims=True)).astype(jnp.bfloat16)
+        context_ref[:, :, g * tile : (g + 1) * tile, :] = dot(weights, keys).reshape(
+            heads, row_count, tile, channels
+        )
+
+    values = jnp.zeros((row_count * residues, inner), jnp.float32)
+    for h in range(heads):
+        w_value = jnp.where(head_of == h, w_att_ref[:, 2 * inner : 3 * inner], 0)
+        context = context_ref[h].reshape(row_count * residues, channels).astype(jnp.bfloat16)
+        values = values + dot(context, w_value)
+    gated = (values * gate).astype(jnp.bfloat16)
+    mid = mid_ref[pl.ds(chip * row_count, row_count)].astype(jnp.float32)
+    update = dot(gated, w_out_ref[...]).reshape(mid.shape)
+    out_ref[...] = (mid + update).astype(jnp.bfloat16)
+
+
+def call(body, args, scalars, outs, scratch, flops, name):
+    return pl.pallas_call(
+        body,
+        out_shape=[jax.ShapeDtypeStruct(shape, dtype) for shape, dtype in outs],
+        in_specs=[pl.BlockSpec(memory_space=pltpu.SMEM)] * len(scalars)
+        + [pl.BlockSpec(memory_space=pltpu.VMEM)] * len(args),
+        out_specs=[pl.BlockSpec(memory_space=pltpu.VMEM)] * len(outs),
+        scratch_shapes=scratch,
+        compiler_params=pltpu.CompilerParams(vmem_limit_bytes=24 * 2**20),
+        cost_estimate=pl.CostEstimate(flops=flops, bytes_accessed=2**20, transcendentals=2**18),
+        name=name,
+    )(*scalars, *args)
+
+
+def gathered(
+    row_devices,
+    pair_acts,
+    res_mask,
+    chain_id,
+    in_gain,
+    w_left,
+    w_right,
+    w_mult_gate,
+    mult_gain,
+    w_mult_out,
+    att_gain,
+    w_att,
+    w_pair_bias,
+    cross_bias,
+    w_att_out,
+):
+    row_count, residues, channels = pair_acts.shape
+    width = w_left.shape[1] // 2
+    heads = w_pair_bias.shape[1]
+    own_count = residues // 2
+    pairs = own_count * residues
+    me = lax.axis_index("row")
+    tile = 8
+
+    def swap(x, shift):
+        return lax.ppermute(x, "row", [(i, i ^ shift) for i in range(row_devices)])
+
+    held, offsets, shift = pair_acts, [0], row_devices // 2
+    while shift > 2:
+        held = jnp.concatenate([held, swap(held, shift)], 0)
+        offsets = offsets + [o ^ shift for o in offsets]
+        shift //= 2
+    come = swap(held, 2)
+    offsets = offsets + [o ^ 2 for o in offsets]
+
+    place = jnp.concatenate([me[None].astype(jnp.int32), res_mask])
+    mask_float = res_mask.astype(jnp.float32)
+    live = jnp.broadcast_to(mask_float[:, None], (residues, channels))
+    own_chain = lax.dynamic_slice_in_dim(chain_id, me * row_count, row_count)
+    crossing = (own_chain[:, None] != jnp.repeat(chain_id, tile)[None, :]).astype(jnp.float32)
+    keep = (mask_float.reshape(-1, 1, tile) * mask_float[None, :, None]).reshape(-1, residues * tile)
+
+    bf16, f32 = jnp.bfloat16, jnp.float32
+    acts, normed, right = call(
+        functools.partial(right_kernel, offsets, row_count),
+        [live, held, come, in_gain[None], w_right],
+        [place],
+        [((own_count, residues, channels), bf16), ((pairs, channels), bf16), ((pairs, width), bf16)],
+        [],
+        2 * pairs * channels * 2 * width,
+        "right_edges",
+    )
+    other = swap(right, 1)
+    left, gate = call(
+        functools.partial(left_kernel, row_count * residues),
+        [normed, w_left, w_mult_gate],
+        [],
+        [((pairs, width), f32), ((pairs, channels), f32)],
+        [],
+        2 * pairs * channels * 3 * width,
+        "left_edges",
+    )
+    mid, normed_mid = call(
+        functools.partial(product_kernel, row_count),
+        [left, right, other, gate, acts, mult_gain[None], w_mult_out, att_gain[None]],
+        [place],
+        [((pairs, channels), bf16), ((pairs, channels), bf16)],
+        [pltpu.VMEM((residues * residues, width), f32), pltpu.VMEM((pairs, width), f32)],
+        2 * pairs * residues * width,
+        "product",
+    )
+    normed_other = swap(normed_mid, 1)
+    (out,) = call(
+        functools.partial(attend_kernel, row_count),
+        [
+            mid.reshape(own_count, residues, channels),
+            normed_mid,
+            normed_other,
+            crossing,
+            keep,
+            w_att,
+            w_pair_bias.T,
+            w_att_out,
+        ],
+        [place, cross_bias],
+        [((row_count, residues, channels), bf16)],
+        [
+            pltpu.VMEM((residues, residues, channels), f32),
+            pltpu.VMEM((heads, row_count, residues, channels), f32),
+            pltpu.VMEM((heads, row_count, residues, channels), f32),
+        ],
+        2 * pairs * channels * 4 * channels,
+        "attend",
+    )
+    return out
+
+
 def solution(mesh):
     placed = (
         P(("groups", "row"), None, None),
@@ -147,8 +469,18 @@
         P(),
         P(),
     )
+    row_devices = mesh.shape["row"]
+
+    def whole(pair_acts, *others):
+        row_count, residues, channels = pair_acts.shape
+        in_vmem = 4 * residues * residues * channels <= vmem_share
+        paired = row_devices >= 4 and row_devices & (row_devices - 1) == 0 and residues % 8 == 0
+        if in_vmem and paired:
+            return gathered(row_devices, pair_acts, *others)
+        return shards(pair_acts, *others)
+
     return jax.shard_map(
-        shards,
+        whole,
         mesh=mesh,
         in_specs=placed,
         out_specs=P(("groups", "row"), None, None),

time: 102 us -> 31.6 us (0.31)
  blocking collectives: 31.1 us -> 0 us
  starting transfers between devices: 18.3 us -> 7.56 us
  Pallas kernels: 0 us -> 10.1 us
  waiting for transfers between devices: 18.1 us -> 8.82 us
  matrix products: 8.73 us -> 0 us
  loops' own time: 8.47 us -> 0 us
  local copies, waits for them, and re-layouts: 12.5 us -> 4.59 us
  other arithmetic: 3.97 us -> 0.16 us
    all_gather x1 -> x0, blocking collectives: 21.8 us -> none  [shards(): bias_table = lax.all_gather(bias_piece, 'row', axis=1, tiled=True)]
    all_to_all x4 -> x0, starting transfers between devices: 18.3 us -> none  [the longest x1 7.52 us: shards(): lax.all_to_all(left_edges, 'row', split_axis=0, concat_axis=1, tiled=True)]
    all_to_all x4 -> x0, waiting for transfers between devices: 18.1 us -> none  [the longest x1 6.58 us: shards(): lax.all_to_all(product, 'row', split_axis=1, concat_axis=0, tiled=True)]
    pallas_call x0 -> x4, Pallas kernels: none -> 10.1 us  [call(): pl.pallas_call(body, out_shape=[jax.ShapeDtypeStruct(shape, dtype) for sh...]
    all_to_all x1 -> x0, blocking collectives: 9.34 us -> none  [shards(): lax.all_to_all(gated, 'row', split_axis=0, concat_axis=1, tiled=True)]
    ppermute x0 -> x5, waiting for transfers between devices: none -> 8.82 us  [swap(): return lax.ppermute(x, 'row', [(i, i ^ shift) for i in range(row_devices)])]
    another operation x1 -> x0, loops' own time: 8.47 us -> none  [attend(): outputs = lax.map(column, jnp.arange(col_count, dtype=jnp.int32))]
    ppermute x0 -> x5, starting transfers between devices: none -> 7.56 us  [swap(): return lax.ppermute(x, 'row', [(i, i ^ shift) for i in range(row_devices)])]
  transfers between devices with their start and end apart: 4 -> 5, of which waited for: 3 -> 5; matrix products, arithmetic and copies ran while one was open for 2% -> 5% of each run, Pallas kernels for 0% -> 2%
where the time goes in v1:
time: 31.6 us; the launch traced here: 31.3 us
  Pallas kernels  10.1 us (32%)
  waiting for transfers between devices  8.82 us (28%)
  starting transfers between devices  7.56 us (24%)
  local copies, waits for them, and re-layouts  4.59 us (15%)
    pallas_call x4, Pallas kernels, call(): pl.pallas_call(body, out_shape=[jax.ShapeDtypeStruct(shape, dtype) for sh...  10.1 us
    ppermute x5, waiting for transfers between devices, swap(): return lax.ppermute(x, 'row', [(i, i ^ shift) for i in range(row_devices)])  8.82 us
    ppermute x5, starting transfers between devices, swap(): return lax.ppermute(x, 'row', [(i, i ^ shift) for i in range(row_devices)])  7.56 us
    unnamed x30, local copies, waits for them, and re-layouts  3.9 us
  transfers between devices with their start and end apart: 5, of which 5 were waited for; matrix products, arithmetic and copies ran while one was open for 5% of the time, Pallas kernels for 2%

profile of v1, /device:TPU:0, one launch (start us, length us, event | category | flops | bytes accessed | tf_op | source)
XLA Modules:
  0.0 31.3 jit_solution(1344185820224372728)
XLA Ops:
  0.0 4.0 %collective-permute-start = (bf16[3,48,128]{2,1,0:T(8,128)(2,1)}, bf16[3,48,128]{2,1,0:T(8,128)(2,1)S(1)}, u32[]{:S(2)}, u32[]{:S(2)}) collective-permute-start(bf16[3,48,128]{2,1,0:T(8,128)(2,1)} %param.14), channel_id=1, source_target_pairs={{0,8},{1,9},{2,10},{3,11},{4,12},{5,13},{6,14},{7,15},{8,0},{9,1},... | collective-permute-start | bytes 110600 | tf_op jit(solution)/shard_map/ppermute | solution.py:383
  4.0 0.8 %constant_dynamic-update-slice_fusion.2 = bf16[12,48,128]{2,1,0:T(8,128)(2,1)S(1)} fusion(bf16[3,48,128]{2,1,0:T(8,128)(2,1)} %param.14), kind=kLoop, calls=%fused_computation.3 | loop fusion | bytes 73728
  4.8 1.8 %collective-permute-done = bf16[3,48,128]{2,1,0:T(8,128)(2,1)S(1)} collective-permute-done((bf16[3,48,128]{2,1,0:T(8,128)(2,1)}, bf16[3,48,128]{2,1,0:T(8,128)(2,1)S(1)}, u32[]{:S(2)}, u32[]{:S(2)}) %collective-permute-start) | collective-permute-done | bytes 36896 | tf_op jit(solution)/shard_map/ppermute | solution.py:383
  6.7 1.5 %collective-permute-start.1 = (bf16[6,48,128]{2,1,0:T(8,128)(2,1)S(1)}, bf16[6,48,128]{2,1,0:T(8,128)(2,1)S(1)}, u32[]{:S(2)}, u32[]{:S(2)}) collective-permute-start(bf16[6,48,128]{2,1,0:T(8,128)(2,1)S(1)} %pad_maximum_fusion), channel_id=1, source_target_pairs={{0,4},{1,5},{2,6},{3,7},{4,0},{5,1},{6,2},{7,3},{8,12},{9,13},{10,... | collective-permute-start | bytes 221192 | tf_op jit(solution)/shard_map/ppermute | solution.py:383
  8.2 2.9 %collective-permute-done.1 = bf16[6,48,128]{2,1,0:T(8,128)(2,1)S(1)} collective-permute-done((bf16[6,48,128]{2,1,0:T(8,128)(2,1)S(1)}, bf16[6,48,128]{2,1,0:T(8,128)(2,1)S(1)}, u32[]{:S(2)}, u32[]{:S(2)}) %collective-permute-start.1) | collective-permute-done | bytes 73760 | tf_op jit(solution)/shard_map/ppermute | solution.py:383
  11.1 1.7 %collective-permute-start.2 = (bf16[12,48,128]{2,1,0:T(8,128)(2,1)S(1)}, bf16[12,48,128]{2,1,0:T(8,128)(2,1)S(1)}, u32[]{:S(2)}, u32[]{:S(2)}) collective-permute-start(bf16[12,48,128]{2,1,0:T(8,128)(2,1)S(1)} %constant_dynamic-update-slice_fusion.held_ref), channel_id=1, source_target_pairs={{0,2},{1,3},{2,0},{3,1},{4,6},{5,7},{6,4},{7,5},{8,10},{9,11},{10,... | collective-permute-start | bytes 442376 | tf_op jit(solution)/shard_map/ppermute | solution.py:383
  12.8 0.7 %copy-done.13 = s32[48]{0:T(128)S(1)} copy-done((s32[48]{0:T(128)S(1)}, s32[48]{0:T(128)}, u32[]{:S(2)}) %copy-start.13) | copy-done | bytes 216
  13.5 0.1 pad_add_fusion.me_ref
  13.6 2.7 %collective-permute-done.2.come_ref = bf16[12,48,128]{2,1,0:T(8,128)(2,1)S(1)} collective-permute-done((bf16[12,48,128]{2,1,0:T(8,128)(2,1)S(1)}, bf16[12,48,128]{2,1,0:T(8,128)(2,1)S(1)}, u32[]{:S(2)}, u32[]{:S(2)}) %collective-permute-start.2) | collective-permute-done | bytes 147488 | tf_op jit(solution)/shard_map/ppermute | solution.py:383
  16.3 0.1 broadcast_in_dim.24.live_ref
  16.4 0.7 %copy-done.10 = f32[128]{0:T(128)S(1)} copy-done((f32[128]{0:T(128)S(1)}, f32[128]{0:T(128)}, u32[]{:S(2)}) %copy-start.10) | copy-done | bytes 536
  17.0 1.2 %right_edges.1 = (bf16[24,48,128]{2,1,0:T(8,128)(2,1)S(1)}, bf16[1152,128]{1,0:T(8,128)(2,1)S(1)}, bf16[1152,128]{1,0:T(8,128)(2,1)S(1)}) custom-call(s32[49]{0:T(128)S(1)} %pad_add_fusion.me_ref, f32[48,128]{1,0:T(8,128)S(1)} %broadcast_in_dim.24.live_ref, bf16[12,48,128]{2,1,0:T(8,128)(2,1)S(1)} %constant_dynamic-update-slice_fusion.held_ref, ...), custom_call_target="tpu_custom_call" | custom-call | flops 75497472 | bytes 1048576 | tf_op jit(solution)/shard_map/right_edges/pallas_call | solution.py:344
  18.3 0.1 collective-permute-start.3
  18.3 0.1 dynamic_slice.3
  18.4 0.1 broadcast_in_dim.28
  18.5 0.1 ne.16
  18.6 0.4 %copy-done.9 = bf16[128,128]{1,0:T(8,128)(2,1)S(1)} copy-done((bf16[128,128]{1,0:T(8,128)(2,1)S(1)}, bf16[128,128]{1,0:T(8,128)(2,1)}, u32[]{:S(2)}) %copy-start.9) | copy-done | bytes 32792
  19.0 0.5 %left_edges.1 = (f32[1152,128]{1,0:T(8,128)S(1)}, f32[1152,128]{1,0:T(8,128)S(1)}) custom-call(bf16[1152,128]{1,0:T(8,128)(2,1)S(1)} %get-tuple-element.12.normed_ref, bf16[128,256]{1,0:T(8,128)(2,1)S(1)} %copy-done.8, bf16[128,128]{1,0:T(8,128)(2,1)S(1)} %copy-done.9), custom_call_target="tpu_custom_call" | custom-call | flops 113246208 | bytes 1048576 | tf_op jit(solution)/shard_map/left_edges/pallas_call | solution.py:344
  19.5 0.4 %collective-permute-done.3.other_ref = bf16[1152,128]{1,0:T(8,128)(2,1)S(1)} collective-permute-done((bf16[1152,128]{1,0:T(8,128)(2,1)S(1)}, bf16[1152,128]{1,0:T(8,128)(2,1)S(1)}, u32[]{:S(2)}, u32[]{:S(2)}) %collective-permute-start.3) | collective-permute-done | bytes 294944 | tf_op jit(solution)/shard_map/ppermute | solution.py:383
  19.9 0.6 %copy-done.4 = f32[128]{0:T(128)S(1)} copy-done((f32[128]{0:T(128)S(1)}, f32[128]{0:T(128)}, u32[]{:S(2)}) %copy-start.4) | copy-done | bytes 536
  20.6 0.0 copy-done.5
  20.6 4.3 %product.1 = (bf16[1152,128]{1,0:T(8,128)(2,1)S(1)}, bf16[1152,128]{1,0:T(8,128)(2,1)S(1)}) custom-call(s32[49]{0:T(128)S(1)} %pad_add_fusion.me_ref, f32[1152,128]{1,0:T(8,128)S(1)} %get-tuple-element.13.left_ref, bf16[1152,128]{1,0:T(8,128)(2,1)S(1)} %get-tuple-element.14.right_ref, bf16[1152,128]{1,0:T(8,128)(2,1)S(1)} %collective-permute-done.3.other_ref, ...), custom_call_target="tpu_custom_call" | custom-call | flops 14155776 | bytes 1048576 | tf_op jit(solution)/shard_map/product/pallas_call | solution.py:344
  24.9 0.2 collective-permute-start.4
  25.1 0.1 compare_convert_fusion.crossing_ref
  25.2 0.1 mul.26
  25.3 0.0 copy-start
  25.3 0.1 mul.28
  25.4 0.1 mul.29
  25.5 0.1 mul.30
  25.6 1.0 %collective-permute-done.4.other_ref = bf16[1152,128]{1,0:T(8,128)(2,1)S(1)} collective-permute-done((bf16[1152,128]{1,0:T(8,128)(2,1)S(1)}, bf16[1152,128]{1,0:T(8,128)(2,1)S(1)}, u32[]{:S(2)}, u32[]{:S(2)}) %collective-permute-start.4) | collective-permute-done | bytes 294944 | tf_op jit(solution)/shard_map/ppermute | solution.py:383
  26.6 0.7 %copy-done.3 = bf16[128,4]{0,1:T(4,128)(2,1)S(1)} copy-done((bf16[128,4]{0,1:T(4,128)(2,1)S(1)}, bf16[128,4]{0,1:T(4,128)(2,1)}, u32[]{:S(2)}) %copy-start.3) | copy-done | bytes 1048
  27.2 4.1 %attend.1 = bf16[3,48,128]{2,1,0:T(8,128)(2,1)} custom-call(s32[49]{0:T(128)S(1)} %pad_add_fusion.me_ref, f32[4]{0:T(128)S(1)} %copy-done.6, bf16[24,48,128]{2,1,0:T(8,128)(2,1)S(1)} %bitcast.6, bf16[1152,128]{1,0:T(8,128)(2,1)S(1)} %get-tuple-element.18.own_ref, bf16[1152,128]{1,0:T(8,128)(2,1)S(1)} %collective-permute-done.4.other_ref, ...), custom_call_target="tpu_custom_call" | custom-call | flops 150994944 | bytes 1048576 | tf_op jit(solution)/shard_map/attend/pallas_call | solution.py:344
  (27 shorter events, 0.1 us)
Async XLA Ops:
  0.0 6.7 %copy-start.11 = (bf16[3,48,128]{2,1,0:T(8,128)(2,1)S(1)}, bf16[3,48,128]{2,1,0:T(8,128)(2,1)}, u32[]{:S(2)}) copy-start(bf16[3,48,128]{2,1,0:T(8,128)(2,1)} %param.14) | copy-start | bytes 110596
  0.0 6.6 %collective-permute-start = (bf16[3,48,128]{2,1,0:T(8,128)(2,1)}, bf16[3,48,128]{2,1,0:T(8,128)(2,1)S(1)}, u32[]{:S(2)}, u32[]{:S(2)}) collective-permute-start(bf16[3,48,128]{2,1,0:T(8,128)(2,1)} %param.14), channel_id=1, source_target_pairs={{0,8},{1,9},{2,10},{3,11},{4,12},{5,13},{6,14},{7,15},{8,0},{9,1},... | collective-permute-start | bytes 110600 | tf_op jit(solution)/shard_map/ppermute | solution.py:383
  6.7 4.4 %collective-permute-start.1 = (bf16[6,48,128]{2,1,0:T(8,128)(2,1)S(1)}, bf16[6,48,128]{2,1,0:T(8,128)(2,1)S(1)}, u32[]{:S(2)}, u32[]{:S(2)}) collective-permute-start(bf16[6,48,128]{2,1,0:T(8,128)(2,1)S(1)} %pad_maximum_fusion), channel_id=1, source_target_pairs={{0,4},{1,5},{2,6},{3,7},{4,0},{5,1},{6,2},{7,3},{8,12},{9,13},{10,... | collective-permute-start | bytes 221192 | tf_op jit(solution)/shard_map/ppermute | solution.py:383
  8.2 8.2 %copy-start.7 = (bf16[128,256]{1,0:T(8,128)(2,1)S(1)}, bf16[128,256]{1,0:T(8,128)(2,1)}, u32[]{:S(2)}) copy-start(bf16[128,256]{1,0:T(8,128)(2,1)} %w_ref.1) | copy-start | bytes 196612
  11.1 5.2 %collective-permute-start.2 = (bf16[12,48,128]{2,1,0:T(8,128)(2,1)S(1)}, bf16[12,48,128]{2,1,0:T(8,128)(2,1)S(1)}, u32[]{:S(2)}, u32[]{:S(2)}) collective-permute-start(bf16[12,48,128]{2,1,0:T(8,128)(2,1)S(1)} %constant_dynamic-update-slice_fusion.held_ref), channel_id=1, source_target_pairs={{0,2},{1,3},{2,0},{3,1},{4,6},{5,7},{6,4},{7,5},{8,10},{9,11},{10,... | collective-permute-start | bytes 442376 | tf_op jit(solution)/shard_map/ppermute | solution.py:383
  12.8 0.7 %copy-start.13 = (s32[48]{0:T(128)S(1)}, s32[48]{0:T(128)}, u32[]{:S(2)}) copy-start(s32[48]{0:T(128)} %param.15) | copy-start | bytes 580
  16.4 0.7 %copy-start.10 = (f32[128]{0:T(128)S(1)}, f32[128]{0:T(128)}, u32[]{:S(2)}) copy-start(f32[128]{0:T(128)} %param.17) | copy-start | bytes 1540
  17.0 1.3 %copy-start.12 = (s32[48]{0:T(128)S(1)}, s32[48]{0:T(128)}, u32[]{:S(2)}) copy-start(s32[48]{0:T(128)} %param.16) | copy-start | bytes 580
  17.0 1.6 %copy-start.8 = (bf16[128,256]{1,0:T(8,128)(2,1)S(1)}, bf16[128,256]{1,0:T(8,128)(2,1)}, u32[]{:S(2)}) copy-start(bf16[128,256]{1,0:T(8,128)(2,1)} %w_left_ref.1) | copy-start | bytes 196612
  18.2 0.8 %copy-start.9 = (bf16[128,128]{1,0:T(8,128)(2,1)S(1)}, bf16[128,128]{1,0:T(8,128)(2,1)}, u32[]{:S(2)}) copy-start(bf16[128,128]{1,0:T(8,128)(2,1)} %w_gate_ref.1) | copy-start | bytes 98308
  18.3 1.6 %collective-permute-start.3 = (bf16[1152,128]{1,0:T(8,128)(2,1)S(1)}, bf16[1152,128]{1,0:T(8,128)(2,1)S(1)}, u32[]{:S(2)}, u32[]{:S(2)}) collective-permute-start(bf16[1152,128]{1,0:T(8,128)(2,1)S(1)} %get-tuple-element.14.right_ref), channel_id=1, source_target_pairs={{0,1},{1,0},{2,3},{3,2},{4,5},{5,4},{6,7},{7,6},{8,9},{9,8},{10,11... | collective-permute-start | bytes 884744 | tf_op jit(solution)/shard_map/ppermute | solution.py:383
  19.0 0.9 %copy-start.1 = (bf16[128,128]{1,0:T(8,128)(2,1)S(1)}, bf16[128,128]{1,0:T(8,128)(2,1)}, u32[]{:S(2)}) copy-start(bf16[128,128]{1,0:T(8,128)(2,1)} %w_out_ref.2) | copy-start | bytes 98308
  19.9 0.7 %copy-start.4 = (f32[128]{0:T(128)S(1)}, f32[128]{0:T(128)}, u32[]{:S(2)}) copy-start(f32[128]{0:T(128)} %param.21) | copy-start | bytes 1540
  19.9 0.7 %copy-start.5 = (f32[128]{0:T(128)S(1)}, f32[128]{0:T(128)}, u32[]{:S(2)}) copy-start(f32[128]{0:T(128)} %param.23) | copy-start | bytes 1540
  24.9 1.6 %collective-permute-start.4 = (bf16[1152,128]{1,0:T(8,128)(2,1)S(1)}, bf16[1152,128]{1,0:T(8,128)(2,1)S(1)}, u32[]{:S(2)}, u32[]{:S(2)}) collective-permute-start(bf16[1152,128]{1,0:T(8,128)(2,1)S(1)} %get-tuple-element.18.own_ref), channel_id=1, source_target_pairs={{0,1},{1,0},{2,3},{3,2},{4,5},{5,4},{6,7},{7,6},{8,9},{9,8},{10,11... | collective-permute-start | bytes 884744 | tf_op jit(solution)/shard_map/ppermute | solution.py:383
  25.3 1.3 %copy-start = (bf16[128,512]{1,0:T(8,128)(2,1)S(1)}, bf16[128,512]{1,0:T(8,128)(2,1)}, u32[]{:S(2)}) copy-start(bf16[128,512]{1,0:T(8,128)(2,1)} %w_att_ref.1) | copy-start | bytes 393220
  25.5 1.1 %copy-start.2 = (bf16[128,128]{1,0:T(8,128)(2,1)S(1)}, bf16[128,128]{1,0:T(8,128)(2,1)}, u32[]{:S(2)}) copy-start(bf16[128,128]{1,0:T(8,128)(2,1)} %w_out_ref.3) | copy-start | bytes 98308
  26.6 0.7 %copy-start.3 = (bf16[128,4]{0,1:T(4,128)(2,1)S(1)}, bf16[128,4]{0,1:T(4,128)(2,1)}, u32[]{:S(2)}) copy-start(bf16[128,4]{0,1:T(4,128)(2,1)} %param.25) | copy-start | bytes 3076
  26.6 0.7 %copy-start.6 = (f32[4]{0:T(128)S(1)}, f32[4]{0:T(128)}, u32[]{:S(2)}) copy-start(f32[4]{0:T(128)} %cross_ref.1) | copy-start | bytes 52

commit v2 on v0

--- a/solution.py
+++ b/solution.py
@@ -1,9 +1,14 @@
+import functools
+
 import jax
 import jax.numpy as jnp
 from jax import lax
+from jax.experimental import pallas as pl
+from jax.experimental.pallas import tpu as pltpu
 from jax.sharding import PartitionSpec as P
 
 norm_eps = 1e-05
+vmem_share = 4 * 2**20
 
 
 def layer_norm(tensor, norm_axis):
@@ -130,6 +135,463 @@
     return pair_out.astype(jnp.bfloat16)
 
 
+def dot(a, b):
+    return jnp.dot(a, b, preferred_element_type=jnp.float32)
+
+
+def dot_t(a, b):
+    return lax.dot_general(a, b, (((1,), (1,)), ((), ())), preferred_element_type=jnp.float32)
+
+
+def sigmoid(x):
+    return 0.5 * jnp.tanh(0.5 * x) + 0.5
+
+
+def norm_rows(x, gain):
+    average = jnp.mean(x, axis=-1, keepdims=True)
+    centred = x - average
+    spread = jnp.mean(centred * centred, axis=-1, keepdims=True)
+    return centred * lax.rsqrt(spread + norm_eps) * gain
+
+
+def gated_edges(normed, weight):
+    both = dot(normed, weight)
+    width = both.shape[1] // 2
+    return (sigmoid(both[:, :width]) * both[:, width:]).astype(jnp.bfloat16)
+
+
+def stage_kernel(copied, *refs):
+    sources, refs = refs[: copied + 4], refs[copied + 4 :]
+    (live_ref, crossing_ref, keep_ref), copies = refs[:3], refs[3 : copied + 3]
+    *early, done = refs[copied + 3 :]
+    cross_ref, chain_ref, mask_row_ref, chain_row_ref = early
+    moves = [
+        pltpu.make_async_copy(source, target, done.at[at])
+        for at, (source, target) in enumerate(zip(sources, (*early, *copies), strict=True))
+    ]
+    for move in moves:
+        move.start()
+    for move in moves[: len(early)]:
+        move.wait()
+    residues = live_ref.shape[0]
+    blocks, wide = keep_ref.shape
+    tile = wide // residues
+    heads = cross_ref.shape[0]
+    row_count = crossing_ref.shape[0] // heads
+    mask_row = mask_row_ref[...].astype(jnp.float32)
+    chain_row = chain_row_ref[...].astype(jnp.float32)
+
+    line = lax.broadcasted_iota(jnp.int32, (residues, residues), 0)
+    spot = lax.broadcasted_iota(jnp.int32, (residues, residues), 1)
+    diagonal = jnp.where(line == spot, mask_row, 0.0)
+    live_ref[...] = dot(diagonal, jnp.ones((residues, live_ref.shape[1]), jnp.float32))
+
+    line = lax.broadcasted_iota(jnp.int32, (residues, wide), 0)
+    lane = lax.broadcasted_iota(jnp.int32, (residues, wide), 1)
+    by_key = (lane // tile == line).astype(jnp.float32)
+    by_column = (lane % tile == line % tile).astype(jnp.float32)
+    block = lax.broadcasted_iota(jnp.int32, (blocks, residues), 0)
+    spot = lax.broadcasted_iota(jnp.int32, (blocks, residues), 1)
+    column_mask = jnp.where(spot // tile == block, mask_row, 0.0)
+    keep_ref[...] = dot(column_mask, by_column) * dot(mask_row, by_key)
+
+    chain_wide = dot(chain_row, by_key)
+    first = lax.axis_index("row") * row_count
+    for i in range(row_count):
+        crossing = (chain_wide != chain_ref[first + i].astype(jnp.float32)).astype(jnp.float32)
+        for h in range(heads):
+            crossing_ref[h * row_count + i : h * row_count + i + 1, :] = cross_ref[h] * crossing
+    for move in moves[len(early) :]:
+        move.wait()
+
+
+def spot_of(block_rows, place):
+    return pl.ds(pl.multiple_of(place * block_rows, block_rows), block_rows)
+
+
+def take_blocks(pieces, offsets, row_count, residues, live_ref, gain_ref):
+    me = lax.axis_index("row")
+    block_rows = row_count * residues
+    blocks = [(ref, at) for ref in pieces for at in range(ref.shape[0] // row_count)]
+    for (ref, at), offset in zip(blocks, offsets, strict=True):
+        device = jnp.bitwise_xor(me, offset)
+        acts = ref[at * row_count : (at + 1) * row_count]
+        normed = norm_rows(acts.astype(jnp.float32), gain_ref[0:1])
+        live_all = live_ref[...]
+        rows = [normed[r] * (live_all * live_ref[pl.ds(device * row_count + r, 1), :]) for r in range(row_count)]
+        normed = jnp.concatenate(rows, 0).astype(jnp.bfloat16)
+        yield spot_of(block_rows, device // 2), acts.reshape(block_rows, acts.shape[-1]), normed
+
+
+def early_kernel(offsets, row_count, live_ref, gain_ref, w_right_ref, w_left_ref, w_gate_ref, *refs):
+    pieces, (acts_ref, right_ref, left_ref, gate_ref) = refs[:-4], refs[-4:]
+    residues = live_ref.shape[0]
+    for spot, acts, normed in take_blocks(pieces, offsets, row_count, residues, live_ref, gain_ref):
+        acts_ref[spot] = acts
+        right_ref[spot] = gated_edges(normed, w_right_ref[...])
+        left_ref[spot] = gated_edges(normed, w_left_ref[...]).astype(jnp.float32)
+        gate_ref[spot] = sigmoid(dot(normed, w_gate_ref[...]))
+
+
+def right_kernel(offsets, row_count, live_ref, gain_ref, w_right_ref, *refs):
+    pieces, (_, _, acts_ref, right_ref, normed_ref) = refs[:-5], refs[-5:]
+    residues = live_ref.shape[0]
+    block_rows = row_count * residues
+    blocks = take_blocks(pieces, offsets, row_count, residues, live_ref, gain_ref)
+    for t, (spot, acts, normed) in enumerate(blocks):
+        acts_ref[spot] = acts
+        right_ref[spot] = gated_edges(normed, w_right_ref[...])
+        normed_ref[t * block_rows : (t + 1) * block_rows] = normed
+
+
+def turn(source, turned_ref, row_count, residues):
+    chips = source.shape[0] // (row_count * residues)
+    own_count = chips * row_count
+    for chip in range(chips):
+        for r in range(row_count):
+            lower = (chip * row_count + r) * residues
+            turned_ref[pl.ds(r * chips + chip, residues, stride=own_count), :] = source[
+                lower : lower + residues
+            ].astype(jnp.float32)
+
+
+def multiply(left_ref, turned_ref, residues, store):
+    row_block, tile = 8, 8
+    count = turned_ref.shape[0] // residues
+    own_count = left_ref.shape[0] // residues
+    tiles = count // tile
+
+    def rows_of(block, carry):
+        first = block * row_block
+
+        def add(k, totals):
+            ahead = [
+                turned_ref[pl.ds(pl.multiple_of(k * count + t * tile, tile), tile), :] for t in range(tiles)
+            ]
+            out = []
+            for a in range(row_block):
+                one = left_ref[pl.ds((first + a) * residues + k, 1), :]
+                out.extend(totals[a * tiles + t] + one * ahead[t] for t in range(tiles))
+            return tuple(out)
+
+        zeros = tuple(jnp.zeros((tile, left_ref.shape[1]), jnp.float32) for _ in range(row_block * tiles))
+        totals = lax.fori_loop(0, residues, add, zeros, unroll=8)
+        for a in range(row_block):
+            for t in range(tiles):
+                store(first + a, t, totals[a * tiles + t])
+        return carry
+
+    lax.fori_loop(0, own_count // row_block, rows_of, 0)
+
+
+def left_kernel(
+    offsets, row_count, residues, normed_ref, right_ref, w_left_ref, w_gate_ref, _, __, left_ref, gate_ref, near_ref, turned_ref
+):
+    me = lax.axis_index("row")
+    block_rows = row_count * residues
+    for t, offset in enumerate(offsets):
+        spot = spot_of(block_rows, jnp.bitwise_xor(me, offset) // 2)
+        normed = normed_ref[t * block_rows : (t + 1) * block_rows]
+        left_ref[spot] = gated_edges(normed, w_left_ref[...]).astype(jnp.float32)
+        gate_ref[spot] = sigmoid(dot(normed, w_gate_ref[...]))
+    turn(right_ref, turned_ref, row_count, residues)
+    count = turned_ref.shape[0] // residues
+
+    def store(i, t, values):
+        near_ref[pl.ds(pl.multiple_of(i * count + t * 8, 8), 8), :] = values
+
+    multiply(left_ref, turned_ref, residues, store)
+
+
+def product_kernel(
+    row_count,
+    residues,
+    left_ref,
+    other_ref,
+    near_ref,
+    gate_ref,
+    acts_ref,
+    gain_ref,
+    w_out_ref,
+    mid_ref,
+    normed_mid_ref,
+    turned_ref,
+    product_ref,
+):
+    core = lax.axis_index("row") % 2
+    turn(other_ref, turned_ref, row_count, residues)
+    count = turned_ref.shape[0] // residues
+    chips = count // row_count
+    part = chips // 8
+
+    def place(i, t, side):
+        r, eighth = t // part, t % part
+        start = i * residues + (eighth * 16 + side) * row_count + r
+        return pl.ds(start, 8, stride=2 * row_count)
+
+    def store(i, t, values):
+        product_ref[place(i, t, 1 - core), :] = values
+        product_ref[place(i, t, core), :] = near_ref[pl.ds(pl.multiple_of(i * count + t * 8, 8), 8), :]
+
+    multiply(left_ref, turned_ref, residues, store)
+
+    block_rows = row_count * residues
+    for lower in range(0, acts_ref.shape[0], block_rows):
+        at = slice(lower, lower + block_rows)
+        product = product_ref[at].astype(jnp.bfloat16).astype(jnp.float32)
+        product = norm_rows(product, gain_ref[1:2]).astype(jnp.bfloat16)
+        update = gate_ref[at] * dot(product, w_out_ref[...])
+        mid = (acts_ref[at].astype(jnp.float32) + update).astype(jnp.bfloat16)
+        mid_ref[at] = mid
+        normed_mid_ref[at] = norm_rows(mid.astype(jnp.float32), gain_ref[2:3]).astype(jnp.bfloat16)
+
+
+def query_kernel(row_count, residues, heads, own_ref, w_att_ref, asked_ref, gate_ref):
+    block_rows = row_count * residues
+    inner = w_att_ref.shape[1] // 4
+    head_dim = inner // heads
+    tile = 8
+    mine = own_ref[spot_of(block_rows, lax.axis_index("row") // 2)]
+    query = (dot(mine, w_att_ref[:, :inner]) * head_dim ** (-0.5)).astype(jnp.bfloat16)
+    gate_ref[...] = sigmoid(dot(mine, w_att_ref[:, 3 * inner :]))
+    head_of = lax.broadcasted_iota(jnp.int32, (1, inner), 1) // head_dim
+    asked = [
+        dot_t(query, jnp.where(head_of == h, w_att_ref[:, inner : 2 * inner], 0)) for h in range(heads)
+    ]
+    for g in range(residues // tile):
+        rows = [
+            asked[h][i * residues + g * tile : i * residues + (g + 1) * tile]
+            for h in range(heads)
+            for i in range(row_count)
+        ]
+        asked_ref[g] = jnp.concatenate(rows, 0).astype(jnp.bfloat16)
+
+
+def attend_kernel(
+    row_count,
+    own_ref,
+    other_ref,
+    mid_ref,
+    asked_ref,
+    gate_ref,
+    crossing_ref,
+    keep_ref,
+    w_att_ref,
+    w_bias_ref,
+    w_out_ref,
+    out_ref,
+    pair_ref,
+):
+    residues, _, channels = pair_ref.shape
+    heads = w_bias_ref.shape[0]
+    inner = w_out_ref.shape[0]
+    head_dim = inner // heads
+    me = lax.axis_index("row")
+    core = me % 2
+    block_rows = row_count * residues
+    for source, side in ((own_ref, core), (other_ref, 1 - core)):
+        for local in range(residues // 2):
+            spot = (2 * (local // row_count) + side) * row_count + local % row_count
+            pair_ref[pl.ds(spot, 1)] = source[local * residues : (local + 1) * residues].astype(jnp.float32)[None]
+
+    tile = 8
+    wide = residues * tile
+    first = me * row_count
+    pieces = []
+    for i in range(row_count):
+        column = pair_ref[:, pl.ds(first + i, 1), :]
+        spread = jnp.broadcast_to(column, (residues, tile, channels)).reshape(wide, channels)
+        pieces.append(dot_t(w_bias_ref[...], spread.astype(jnp.bfloat16)).astype(jnp.bfloat16).astype(jnp.float32))
+    extra = jnp.concatenate(
+        [
+            jnp.broadcast_to(pieces[i][h : h + 1] + crossing_ref[h * row_count + i : h * row_count + i + 1], (tile, wide))
+            for h in range(heads)
+            for i in range(row_count)
+        ],
+        0,
+    )
+    total_rows = heads * row_count * tile
+    same = (
+        lax.broadcasted_iota(jnp.int32, (total_rows, wide), 0) % tile
+        == lax.broadcasted_iota(jnp.int32, (total_rows, wide), 1) % tile
+    )
+    low = jnp.where(same, -1000000000.0, -1e30)
+    groups = range(residues // tile)
+    keys = [
+        pair_ref[:, g * tile : (g + 1) * tile, :].reshape(wide, channels).astype(jnp.bfloat16) for g in groups
+    ]
+    scores = [dot_t(asked_ref[g], keys[g]) for g in groups]
+    scores = [
+        jnp.where(jnp.logical_and(same, keep_ref[g : g + 1, :] > 0), scores[g] + extra, low) for g in groups
+    ]
+    scores = [jnp.exp(s - jnp.max(s, axis=-1, keepdims=True)) for s in scores]
+    weights = [(s * (1.0 / jnp.sum(s, axis=-1, keepdims=True))).astype(jnp.bfloat16) for s in scores]
+    context = [dot(weights[g], keys[g]) for g in groups]
+
+    head_of = lax.broadcasted_iota(jnp.int32, (1, inner), 1) // head_dim
+    values = jnp.zeros((block_rows, inner), jnp.float32)
+    for h in range(heads):
+        w_value = jnp.where(head_of == h, w_att_ref[:, 2 * inner : 3 * inner], 0)
+        rows = [
+            context[g][(h * row_count + i) * tile : (h * row_count + i + 1) * tile]
+            for i in range(row_count)
+            for g in groups
+        ]
+        values = values + dot(jnp.concatenate(rows, 0).astype(jnp.bfloat16), w_value)
+    gated = (values * gate_ref[...]).astype(jnp.bfloat16)
+    mid = mid_ref[spot_of(block_rows, me // 2)].astype(jnp.float32)
+    out_ref[...] = (mid + dot(gated, w_out_ref[...])).astype(jnp.bfloat16).reshape(out_ref.shape)
+
+
+def call(body, args, outs, cost_us, name, scratch=(), aliases=None, space=pltpu.VMEM):
+    return pl.pallas_call(
+        body,
+        out_shape=[jax.ShapeDtypeStruct(shape, dtype) for shape, dtype in outs],
+        in_specs=[pl.BlockSpec(memory_space=space)] * len(args),
+        out_specs=[pl.BlockSpec(memory_space=pltpu.VMEM)] * len(outs),
+        scratch_shapes=list(scratch),
+        input_output_aliases=aliases or {},
+        compiler_params=pltpu.CompilerParams(vmem_limit_bytes=24 * 2**20),
+        cost_estimate=pl.CostEstimate(flops=int(cost_us * 1e9), bytes_accessed=2**18, transcendentals=0),
+        name=name,
+    )(*args)
+
+
+def gathered(
+    row_devices,
+    pair_acts,
+    res_mask,
+    chain_id,
+    in_gain,
+    w_left,
+    w_right,
+    w_mult_gate,
+    mult_gain,
+    w_mult_out,
+    att_gain,
+    w_att,
+    w_pair_bias,
+    cross_bias,
+    w_att_out,
+):
+    row_count, residues, channels = pair_acts.shape
+    width = w_left.shape[1] // 2
+    heads = w_pair_bias.shape[1]
+    own_count = residues // 2
+    pairs = own_count * residues
+    block_rows = row_count * residues
+    tile = 8
+    wide = residues * tile
+    bf16, f32 = jnp.bfloat16, jnp.float32
+
+    def swap(x, shift):
+        return lax.ppermute(x, "row", [(i, i ^ shift) for i in range(row_devices)])
+
+    base, held = [0], pair_acts
+    far, near, side = 8, 4, 2
+
+    def spread(shifts):
+        return [o ^ s for s in shifts for o in base]
+
+    shift = row_devices // 2
+    while shift > far:
+        held = jnp.concatenate([held, swap(held, shift)], 0)
+        base = base + [o ^ shift for o in base]
+        shift //= 2
+    from_far = swap(held, far)
+    from_side = swap(held, side)
+
+    weights = [
+        in_gain[None],
+        mult_gain[None],
+        att_gain[None],
+        w_right,
+        w_left,
+        w_mult_gate,
+        w_mult_out,
+        w_att,
+        w_pair_bias.T,
+        w_att_out,
+        held,
+    ]
+    live, crossing, keep, in_g, mult_g, att_g, w_r, w_l, w_g, w_m, w_a, w_b, w_o, held = call(
+        functools.partial(stage_kernel, len(weights)),
+        [
+            pltpu.with_memory_space_constraint(x, pltpu.HBM)
+            for x in (cross_bias, chain_id, res_mask[None], chain_id[None], *weights)
+        ],
+        [((residues, channels), f32), ((heads * row_count, wide), f32), ((residues // tile, wide), f32)]
+        + [(w.shape, w.dtype) for w in weights],
+        2.0,
+        "stage",
+        [
+            pltpu.SMEM((heads,), f32),
+            pltpu.SMEM((residues,), jnp.int32),
+            pltpu.VMEM((1, residues), jnp.int32),
+            pltpu.VMEM((1, residues), jnp.int32),
+            pltpu.SemaphoreType.DMA((len(weights) + 4,)),
+        ],
+        space=pltpu.HBM,
+    )
+    pair = jnp.concatenate([held, from_far], 0)
+    from_near = swap(pair, near)
+    from_far_side = swap(from_far, side)
+    from_corner = swap(pair, near ^ side)
+
+    sizes = [((pairs, channels), bf16), ((pairs, width), bf16), ((pairs, width), f32), ((pairs, channels), f32)]
+    acts, right, left, gate = call(
+        functools.partial(early_kernel, spread([0, far, side]), row_count),
+        [live, in_g, w_r, w_l, w_g, pair, from_side],
+        sizes,
+        0.6,
+        "early_edges",
+    )
+    late = spread([near, near ^ far, far ^ side, near ^ side, near ^ far ^ side])
+    acts, right, normed = call(
+        functools.partial(right_kernel, late, row_count),
+        [live, in_g, w_r, from_near, from_far_side, from_corner, acts, right],
+        [*sizes[:2], ((len(late) * block_rows, channels), bf16)],
+        0.5,
+        "right_edges",
+        aliases={6: 0, 7: 1},
+    )
+    other = swap(right, 1)
+    left, gate, near_product = call(
+        functools.partial(left_kernel, late, row_count, residues),
+        [normed, right, w_l, w_g, left, gate],
+        [*sizes[2:], ((own_count * own_count, width), f32)],
+        1.5,
+        "left_edges",
+        scratch=[pltpu.VMEM((pairs, width), f32)],
+        aliases={4: 0, 5: 1},
+    )
+    mid, normed_mid = call(
+        functools.partial(product_kernel, row_count, residues),
+        [left, other, near_product, gate, acts, jnp.concatenate([in_g, mult_g, att_g], 0), w_m],
+        [((pairs, channels), bf16), ((pairs, channels), bf16)],
+        2.4,
+        "product",
+        scratch=[pltpu.VMEM((pairs, width), f32), pltpu.VMEM((pairs, width), f32)],
+    )
+    normed_other = swap(normed_mid, 1)
+    asked, gate_att = call(
+        functools.partial(query_kernel, row_count, residues, heads),
+        [normed_mid, w_a],
+        [((residues // tile, heads * row_count * tile, channels), bf16), ((block_rows, w_o.shape[0]), f32)],
+        0.4,
+        "queries",
+    )
+    (out,) = call(
+        functools.partial(attend_kernel, row_count),
+        [normed_mid, normed_other, mid, asked, gate_att, crossing, keep, w_a, w_b, w_o],
+        [((row_count, residues, channels), bf16)],
+        2.0,
+        "attend",
+        scratch=[pltpu.VMEM((residues, residues, channels), f32)],
+    )
+    return out
+
+
 def solution(mesh):
     placed = (
         P(("groups", "row"), None, None),
@@ -147,8 +609,18 @@
         P(),
         P(),
     )
+    row_devices = mesh.shape["row"]
+
+    def whole(pair_acts, *others):
+        row_count, residues, channels = pair_acts.shape
+        in_vmem = 4 * residues * residues * channels <= vmem_share
+        paired = row_devices % 16 == 0 and row_devices & (row_devices - 1) == 0 and residues % 8 == 0
+        if in_vmem and paired:
+            return gathered(row_devices, pair_acts, *others)
+        return shards(pair_acts, *others)
+
     return jax.shard_map(
-        shards,
+        whole,
         mesh=mesh,
         in_specs=placed,
         out_specs=P(("groups", "row"), None, None),

time: 102 us -> 22.5 us (0.22)
  blocking collectives: 31.1 us -> 0 us
  waiting for transfers between devices: 18.1 us -> 4.03 us
  local copies, waits for them, and re-layouts: 12.5 us -> 0.02 us
  matrix products: 8.73 us -> 0 us
  starting transfers between devices: 18.3 us -> 9.73 us
  Pallas kernels: 0 us -> 8.47 us
  loops' own time: 8.47 us -> 0 us
  other arithmetic: 3.97 us -> 0.01 us
    all_gather x1 -> x0, blocking collectives: 21.8 us -> none  [shards(): bias_table = lax.all_gather(bias_piece, 'row', axis=1, tiled=True)]
    all_to_all x4 -> x0, starting transfers between devices: 18.3 us -> none  [the longest x1 7.52 us: shards(): lax.all_to_all(left_edges, 'row', split_axis=0, concat_axis=1, tiled=True)]
    all_to_all x4 -> x0, waiting for transfers between devices: 18.1 us -> none  [the longest x1 6.58 us: shards(): lax.all_to_all(product, 'row', split_axis=1, concat_axis=0, tiled=True)]
    ppermute x0 -> x7, starting transfers between devices: none -> 9.73 us  [swap(): return lax.ppermute(x, 'row', [(i, i ^ shift) for i in range(row_devices)])]
    all_to_all x1 -> x0, blocking collectives: 9.34 us -> none  [shards(): lax.all_to_all(gated, 'row', split_axis=0, concat_axis=1, tiled=True)]
    another operation x1 -> x0, loops' own time: 8.47 us -> none  [attend(): outputs = lax.map(column, jnp.arange(col_count, dtype=jnp.int32))]
    pallas_call x0 -> x7, Pallas kernels: none -> 8.47 us  [call(): pl.pallas_call(body, out_shape=[jax.ShapeDtypeStruct(shape, dtype) for sh...]
    unnamed x32 -> x1, local copies, waits for them, and re-layouts: 6.83 us -> 0.01 us
  transfers between devices with their start and end apart: 4 -> 7, of which waited for: 3 -> 2; matrix products, arithmetic and copies ran while one was open for 2% -> 0% of each run, Pallas kernels for 0% -> 16%
where the time goes in v2:
time: 22.5 us; the launch traced here: 22.3 us
  starting transfers between devices  9.73 us (43%)
  Pallas kernels  8.47 us (38%)
  waiting for transfers between devices  4.03 us (18%)
    ppermute x7, starting transfers between devices, swap(): return lax.ppermute(x, 'row', [(i, i ^ shift) for i in range(row_devices)])  9.73 us
    pallas_call x7, Pallas kernels, call(): pl.pallas_call(body, out_shape=[jax.ShapeDtypeStruct(shape, dtype) for sh...  8.47 us
    ppermute x7, waiting for transfers between devices, swap(): return lax.ppermute(x, 'row', [(i, i ^ shift) for i in range(row_devices)])  4.03 us
  transfers between devices with their start and end apart: 7, of which 2 were waited for; matrix products, arithmetic and copies ran while one was open for 0% of the time, Pallas kernels for 16%

profile of v2, /device:TPU:0, one launch (start us, length us, event | category | flops | bytes accessed | tf_op | source)
XLA Modules:
  0.0 22.3 jit_solution(5532189649158850491)
XLA Ops:
  0.0 4.0 %collective-permute-start = (bf16[3,48,128]{2,1,0:T(8,128)(2,1)}, bf16[3,48,128]{2,1,0:T(8,128)(2,1)S(1)}, u32[]{:S(2)}, u32[]{:S(2)}) collective-permute-start(bf16[3,48,128]{2,1,0:T(8,128)(2,1)} %refs_14_.1), channel_id=1, source_target_pairs={{0,8},{1,9},{2,10},{3,11},{4,12},{5,13},{6,14},{7,15},{8,0},{9,1},... | collective-permute-start | bytes 110600 | tf_op jit(solution)/shard_map/ppermute | solution.py:488
  4.0 1.5 %collective-permute-start.4 = (bf16[3,48,128]{2,1,0:T(8,128)(2,1)}, bf16[3,48,128]{2,1,0:T(8,128)(2,1)S(1)}, u32[]{:S(2)}, u32[]{:S(2)}) collective-permute-start(bf16[3,48,128]{2,1,0:T(8,128)(2,1)} %refs_14_.1), channel_id=1, source_target_pairs={{0,2},{1,3},{2,0},{3,1},{4,6},{5,7},{6,4},{7,5},{8,10},{9,11},{10,... | collective-permute-start | bytes 110600 | tf_op jit(solution)/shard_map/ppermute | solution.py:488
  5.6 1.2 %stage.1 = (f32[48,128]{1,0:T(8,128)S(1)}, f32[12,384]{1,0:T(8,128)S(1)}, f32[6,384]{1,0:T(8,128)S(1)}, f32[1,128]{1,0:T(1,128)S(1)}, f32[1,128]{1,0:T(1,128)S(1...) custom-call(f32[4]{0:T(128)} %refs_0_.1, ...), custom_call_target="tpu_custom_call" | custom-call | flops 2000000000 | bytes 262144 | tf_op jit(solution)/shard_map/stage/pallas_call | solution.py:447
  6.8 0.0 collective-permute-done
  6.8 1.6 %collective-permute-start.1 = (bf16[6,48,128]{2,1,0:T(8,128)(2,1)S(1)}, bf16[6,48,128]{2,1,0:T(8,128)(2,1)S(1)}, u32[]{:S(2)}, u32[]{:S(2)}) collective-permute-start(bf16[6,48,128]{2,1,0:T(8,128)(2,1)S(1)} %constant_dynamic-update-slice_fusion.refs_0_), channel_id=1, source_target_pairs={{0,4},{1,5},{2,6},{3,7},{4,0},{5,1},{6,2},{7,3},{8,12},{9,13},{10,... | collective-permute-start | bytes 221192 | tf_op jit(solution)/shard_map/ppermute | solution.py:488
  8.5 1.4 %collective-permute-start.3 = (bf16[6,48,128]{2,1,0:T(8,128)(2,1)S(1)}, bf16[6,48,128]{2,1,0:T(8,128)(2,1)S(1)}, u32[]{:S(2)}, u32[]{:S(2)}) collective-permute-start(bf16[6,48,128]{2,1,0:T(8,128)(2,1)S(1)} %constant_dynamic-update-slice_fusion.refs_0_), channel_id=1, source_target_pairs={{0,6},{1,7},{2,4},{3,5},{4,2},{5,3},{6,0},{7,1},{8,14},{9,15},{10,... | collective-permute-start | bytes 221192 | tf_op jit(solution)/shard_map/ppermute | solution.py:488
  9.8 0.5 %collective-permute-start.2 = (bf16[3,48,128]{2,1,0:T(8,128)(2,1)S(1)}, bf16[3,48,128]{2,1,0:T(8,128)(2,1)S(1)}, u32[]{:S(2)}, u32[]{:S(2)}) collective-permute-start(bf16[3,48,128]{2,1,0:T(8,128)(2,1)S(1)} %collective-permute-done), channel_id=1, source_target_pairs={{0,2},{1,3},{2,0},{3,1},{4,6},{5,7},{6,4},{7,5},{8,10},{9,11},{10,... | collective-permute-start | bytes 110600 | tf_op jit(solution)/shard_map/ppermute | solution.py:488
  10.4 0.0 collective-permute-done.4.refs_1_
  10.4 0.6 %early_edges.1 = (bf16[1152,128]{1,0:T(8,128)(2,1)S(1)}, bf16[1152,128]{1,0:T(8,128)(2,1)S(1)}, f32[1152,128]{1,0:T(8,128)S(1)}, f32[1152,128]{1,0:T(8,128)S(1)}) custom-call(f32[48,128]{1,0:T(8,128)S(1)} %get-tuple-element.33.live_ref, f32[1,128]{1,0:T(1,128)S(1)} %get-tuple-element.34.gain_ref, bf16[128,256]{1,0:T(8,128)(2,1)S(1)} %get-tuple-element.35.w_right_ref, ...), custom_call_target="tpu_custom_call" | custom-call | flops 600000000 | bytes 262144 | tf_op jit(solution)/shard_map/early_edges/pallas_call | solution.py:447
  11.0 3.2 %collective-permute-done.2.refs_1_ = bf16[3,48,128]{2,1,0:T(8,128)(2,1)S(1)} collective-permute-done((bf16[3,48,128]{2,1,0:T(8,128)(2,1)S(1)}, bf16[3,48,128]{2,1,0:T(8,128)(2,1)S(1)}, u32[]{:S(2)}, u32[]{:S(2)}) %collective-permute-start.2) | collective-permute-done | bytes 36896 | tf_op jit(solution)/shard_map/ppermute | solution.py:488
  14.1 0.0 collective-permute-done.1.refs_0_
  14.1 0.0 collective-permute-done.3.refs_2_
  14.1 0.5 %right_edges.1 = (bf16[1152,128]{1,0:T(8,128)(2,1)S(1)}, bf16[1152,128]{1,0:T(8,128)(2,1)S(1)}, bf16[720,128]{1,0:T(8,128)(2,1)S(1)}) custom-call(f32[48,128]{1,0:T(8,128)S(1)} %get-tuple-element.33.live_ref, f32[1,128]{1,0:T(1,128)S(1)} %get-tuple-element.34.gain_ref, ...), custom_call_target="tpu_custom_call", output_to_operand_aliasing={{0}: (6, {}), {1}: (7, {})} | custom-call | flops 500000000 | bytes 262144 | tf_op jit(solution)/shard_map/right_edges/pallas_call | solution.py:447
  14.6 0.1 collective-permute-start.5
  14.7 1.5 %left_edges.1 = (f32[1152,128]{1,0:T(8,128)S(1)}, f32[1152,128]{1,0:T(8,128)S(1)}, f32[576,128]{1,0:T(8,128)S(1)}) custom-call(bf16[720,128]{1,0:T(8,128)(2,1)S(1)} %get-tuple-element.41.normed_ref, bf16[1152,128]{1,0:T(8,128)(2,1)S(1)} %get-tuple-element.42.right_ref, ...), custom_call_target="tpu_custom_call", output_to_operand_aliasing={{0}: (4, {}), {1}: (5, {})} | custom-call | flops 1500000000 | bytes 262144 | tf_op jit(solution)/shard_map/left_edges/pallas_call | solution.py:447
  16.2 0.0 collective-permute-done.5.other_ref
  16.3 2.4 %product.1 = (bf16[1152,128]{1,0:T(8,128)(2,1)S(1)}, bf16[1152,128]{1,0:T(8,128)(2,1)S(1)}) custom-call(f32[1152,128]{1,0:T(8,128)S(1)} %get-tuple-element.45.left_ref, bf16[1152,128]{1,0:T(8,128)(2,1)S(1)} %collective-permute-done.5.other_ref, f32[576,128]{1,0:T(8,128)S(1)} %get-tuple-element.46.near_ref, f32[1152,128]{1,0:T(8,128)S(1)} %get-tuple-element.47.gate_ref, ...), custom_call_target="tpu_custom_call" | custom-call | flops 2400000000 | bytes 262144 | tf_op jit(solution)/shard_map/product/pallas_call | solution.py:447
  18.7 0.6 %collective-permute-start.6 = (bf16[1152,128]{1,0:T(8,128)(2,1)S(1)}, bf16[1152,128]{1,0:T(8,128)(2,1)S(1)}, u32[]{:S(2)}, u32[]{:S(2)}) collective-permute-start(bf16[1152,128]{1,0:T(8,128)(2,1)S(1)} %get-tuple-element.52.own_ref), channel_id=1, source_target_pairs={{0,1},{1,0},{2,3},{3,2},{4,5},{5,4},{6,7},{7,6},{8,9},{9,8},{10,11... | collective-permute-start | bytes 884744 | tf_op jit(solution)/shard_map/ppermute | solution.py:488
  19.2 0.3 %queries.1 = (bf16[6,96,128]{2,1,0:T(8,128)(2,1)S(1)}, f32[144,128]{1,0:T(8,128)S(1)}) custom-call(bf16[1152,128]{1,0:T(8,128)(2,1)S(1)} %get-tuple-element.52.own_ref, bf16[128,512]{1,0:T(8,128)(2,1)S(1)} %get-tuple-element.54.w_att_ref), custom_call_target="tpu_custom_call" | custom-call | flops 400000000 | bytes 262144 | tf_op jit(solution)/shard_map/queries/pallas_call | solution.py:447
  19.6 0.9 %collective-permute-done.6.other_ref = bf16[1152,128]{1,0:T(8,128)(2,1)S(1)} collective-permute-done((bf16[1152,128]{1,0:T(8,128)(2,1)S(1)}, bf16[1152,128]{1,0:T(8,128)(2,1)S(1)}, u32[]{:S(2)}, u32[]{:S(2)}) %collective-permute-start.6) | collective-permute-done | bytes 294944 | tf_op jit(solution)/shard_map/ppermute | solution.py:488
  20.4 1.9 %attend.1 = bf16[3,48,128]{2,1,0:T(8,128)(2,1)} custom-call(bf16[1152,128]{1,0:T(8,128)(2,1)S(1)} %get-tuple-element.52.own_ref, bf16[1152,128]{1,0:T(8,128)(2,1)S(1)} %collective-permute-done.6.other_ref, bf16[1152,128]{1,0:T(8,128)(2,1)S(1)} %get-tuple-element.53.mid_ref, bf16[6,96,128]{2,1,0:T(8,128)(2,1)S(1)} %get-tuple-element.55.asked_ref, ...), custom_call_target="tpu_custom_call" | custom-call | flops 2000000000 | bytes 262144 | tf_op jit(solution)/shard_map/attend/pallas_call | solution.py:447
  (3 shorter events, 0.0 us)
Async XLA Ops:
  0.0 6.8 %collective-permute-start = (bf16[3,48,128]{2,1,0:T(8,128)(2,1)}, bf16[3,48,128]{2,1,0:T(8,128)(2,1)S(1)}, u32[]{:S(2)}, u32[]{:S(2)}) collective-permute-start(bf16[3,48,128]{2,1,0:T(8,128)(2,1)} %refs_14_.1), channel_id=1, source_target_pairs={{0,8},{1,9},{2,10},{3,11},{4,12},{5,13},{6,14},{7,15},{8,0},{9,1},... | collective-permute-start | bytes 110600 | tf_op jit(solution)/shard_map/ppermute | solution.py:488
  4.0 6.3 %collective-permute-start.4 = (bf16[3,48,128]{2,1,0:T(8,128)(2,1)}, bf16[3,48,128]{2,1,0:T(8,128)(2,1)S(1)}, u32[]{:S(2)}, u32[]{:S(2)}) collective-permute-start(bf16[3,48,128]{2,1,0:T(8,128)(2,1)} %refs_14_.1), channel_id=1, source_target_pairs={{0,2},{1,3},{2,0},{3,1},{4,6},{5,7},{6,4},{7,5},{8,10},{9,11},{10,... | collective-permute-start | bytes 110600 | tf_op jit(solution)/shard_map/ppermute | solution.py:488
  6.8 7.3 %collective-permute-start.1 = (bf16[6,48,128]{2,1,0:T(8,128)(2,1)S(1)}, bf16[6,48,128]{2,1,0:T(8,128)(2,1)S(1)}, u32[]{:S(2)}, u32[]{:S(2)}) collective-permute-start(bf16[6,48,128]{2,1,0:T(8,128)(2,1)S(1)} %constant_dynamic-update-slice_fusion.refs_0_), channel_id=1, source_target_pairs={{0,4},{1,5},{2,6},{3,7},{4,0},{5,1},{6,2},{7,3},{8,12},{9,13},{10,... | collective-permute-start | bytes 221192 | tf_op jit(solution)/shard_map/ppermute | solution.py:488
  8.5 5.7 %collective-permute-start.3 = (bf16[6,48,128]{2,1,0:T(8,128)(2,1)S(1)}, bf16[6,48,128]{2,1,0:T(8,128)(2,1)S(1)}, u32[]{:S(2)}, u32[]{:S(2)}) collective-permute-start(bf16[6,48,128]{2,1,0:T(8,128)(2,1)S(1)} %constant_dynamic-update-slice_fusion.refs_0_), channel_id=1, source_target_pairs={{0,6},{1,7},{2,4},{3,5},{4,2},{5,3},{6,0},{7,1},{8,14},{9,15},{10,... | collective-permute-start | bytes 221192 | tf_op jit(solution)/shard_map/ppermute | solution.py:488
  9.8 4.3 %collective-permute-start.2 = (bf16[3,48,128]{2,1,0:T(8,128)(2,1)S(1)}, bf16[3,48,128]{2,1,0:T(8,128)(2,1)S(1)}, u32[]{:S(2)}, u32[]{:S(2)}) collective-permute-start(bf16[3,48,128]{2,1,0:T(8,128)(2,1)S(1)} %collective-permute-done), channel_id=1, source_target_pairs={{0,2},{1,3},{2,0},{3,1},{4,6},{5,7},{6,4},{7,5},{8,10},{9,11},{10,... | collective-permute-start | bytes 110600 | tf_op jit(solution)/shard_map/ppermute | solution.py:488
  14.6 1.6 %collective-permute-start.5 = (bf16[1152,128]{1,0:T(8,128)(2,1)S(1)}, bf16[1152,128]{1,0:T(8,128)(2,1)S(1)}, u32[]{:S(2)}, u32[]{:S(2)}) collective-permute-start(bf16[1152,128]{1,0:T(8,128)(2,1)S(1)} %get-tuple-element.42.right_ref), channel_id=1, source_target_pairs={{0,1},{1,0},{2,3},{3,2},{4,5},{5,4},{6,7},{7,6},{8,9},{9,8},{10,11... | collective-permute-start | bytes 884744 | tf_op jit(solution)/shard_map/ppermute | solution.py:488
  18.7 1.8 %collective-permute-start.6 = (bf16[1152,128]{1,0:T(8,128)(2,1)S(1)}, bf16[1152,128]{1,0:T(8,128)(2,1)S(1)}, u32[]{:S(2)}, u32[]{:S(2)}) collective-permute-start(bf16[1152,128]{1,0:T(8,128)(2,1)S(1)} %get-tuple-element.52.own_ref), channel_id=1, source_target_pairs={{0,1},{1,0},{2,3},{3,2},{4,5},{5,4},{6,7},{7,6},{8,9},{9,8},{10,11... | collective-permute-start | bytes 884744 | tf_op jit(solution)/shard_map/ppermute | solution.py:488

commit v3 on v2

--- a/solution.py
+++ b/solution.py
@@ -160,10 +160,23 @@
     return (sigmoid(both[:, :width]) * both[:, width:]).astype(jnp.bfloat16)
 
 
+def odd_bits(number):
+    return bin(number).count("1") % 2
+
+
+def parity(number):
+    bits = lax.axis_size("row").bit_length() - 1
+    return functools.reduce(jnp.bitwise_xor, [number >> b for b in range(bits)]) & 1
+
+
+def own_side():
+    return parity(lax.axis_index("row"))
+
+
 def stage_kernel(copied, *refs):
     sources, refs = refs[: copied + 4], refs[copied + 4 :]
-    (live_ref, crossing_ref, keep_ref), copies = refs[:3], refs[3 : copied + 3]
-    *early, done = refs[copied + 3 :]
+    (live_ref, *half_refs), copies = refs[:5], refs[5 : copied + 5]
+    *early, done = refs[copied + 5 :]
     cross_ref, chain_ref, mask_row_ref, chain_row_ref = early
     moves = [
         pltpu.make_async_copy(source, target, done.at[at])
@@ -174,10 +187,10 @@
     for move in moves[: len(early)]:
         move.wait()
     residues = live_ref.shape[0]
-    blocks, wide = keep_ref.shape
-    tile = wide // residues
+    blocks, wide = half_refs[1].shape
+    tile = 2 * wide // residues
     heads = cross_ref.shape[0]
-    row_count = crossing_ref.shape[0] // heads
+    row_count = half_refs[0].shape[0] // heads
     mask_row = mask_row_ref[...].astype(jnp.float32)
     chain_row = chain_row_ref[...].astype(jnp.float32)
 
@@ -188,19 +201,23 @@
 
     line = lax.broadcasted_iota(jnp.int32, (residues, wide), 0)
     lane = lax.broadcasted_iota(jnp.int32, (residues, wide), 1)
-    by_key = (lane // tile == line).astype(jnp.float32)
     by_column = (lane % tile == line % tile).astype(jnp.float32)
+    local = lane // tile
+    chip = local // row_count
     block = lax.broadcasted_iota(jnp.int32, (blocks, residues), 0)
     spot = lax.broadcasted_iota(jnp.int32, (blocks, residues), 1)
-    column_mask = jnp.where(spot // tile == block, mask_row, 0.0)
-    keep_ref[...] = dot(column_mask, by_column) * dot(mask_row, by_key)
-
-    chain_wide = dot(chain_row, by_key)
+    column_mask = dot(jnp.where(spot // tile == block, mask_row, 0.0), by_column)
     first = lax.axis_index("row") * row_count
-    for i in range(row_count):
-        crossing = (chain_wide != chain_ref[first + i].astype(jnp.float32)).astype(jnp.float32)
-        for h in range(heads):
-            crossing_ref[h * row_count + i : h * row_count + i + 1, :] = cross_ref[h] * crossing
+    for half, side in enumerate((own_side(), 1 - own_side())):
+        key = (2 * chip + jnp.bitwise_xor(parity(chip), side)) * row_count + local % row_count
+        by_key = (key == line).astype(jnp.float32)
+        crossing_ref, keep_ref = half_refs[2 * half : 2 * half + 2]
+        keep_ref[...] = column_mask * dot(mask_row, by_key)
+        chain_wide = dot(chain_row, by_key)
+        for i in range(row_count):
+            crossing = (chain_wide != chain_ref[first + i].astype(jnp.float32)).astype(jnp.float32)
+            for h in range(heads):
+                crossing_ref[h * row_count + i : h * row_count + i + 1, :] = cross_ref[h] * crossing
     for move in moves[len(early) :]:
         move.wait()
 
@@ -275,7 +292,7 @@
             return tuple(out)
 
         zeros = tuple(jnp.zeros((tile, left_ref.shape[1]), jnp.float32) for _ in range(row_block * tiles))
-        totals = lax.fori_loop(0, residues, add, zeros, unroll=8)
+        totals = lax.fori_loop(0, residues, add, zeros, unroll=16)
         for a in range(row_block):
             for t in range(tiles):
                 store(first + a, t, totals[a * tiles + t])
@@ -318,20 +335,22 @@
     turned_ref,
     product_ref,
 ):
-    core = lax.axis_index("row") % 2
+    core = own_side()
     turn(other_ref, turned_ref, row_count, residues)
     count = turned_ref.shape[0] // residues
     chips = count // row_count
     part = chips // 8
 
-    def place(i, t, side):
+    line = lax.broadcasted_iota(jnp.int32, (8, 1), 0)
+    odd_line = (line ^ (line >> 1) ^ (line >> 2)) & 1
+
+    def store(i, t, values):
         r, eighth = t // part, t % part
-        start = i * residues + (eighth * 16 + side) * row_count + r
-        return pl.ds(start, 8, stride=2 * row_count)
-
-    def store(i, t, values):
-        product_ref[place(i, t, 1 - core), :] = values
-        product_ref[place(i, t, core), :] = near_ref[pl.ds(pl.multiple_of(i * count + t * 8, 8), 8), :]
+        near = near_ref[pl.ds(pl.multiple_of(i * count + t * 8, 8), 8), :]
+        near_first = odd_line == (core ^ odd_bits(eighth))
+        for side, rows in ((0, jnp.where(near_first, near, values)), (1, jnp.where(near_first, values, near))):
+            start = i * residues + (eighth * 16 + side) * row_count + r
+            product_ref[pl.ds(start, 8, stride=2 * row_count), :] = rows
 
     multiply(left_ref, turned_ref, residues, store)
 
@@ -346,34 +365,90 @@
         normed_mid_ref[at] = norm_rows(mid.astype(jnp.float32), gain_ref[2:3]).astype(jnp.bfloat16)
 
 
-def query_kernel(row_count, residues, heads, own_ref, w_att_ref, asked_ref, gate_ref):
+def half_attention(rows_ref, pair_ref, asked, w_bias, crossing_ref, keep_ref):
+    count, residues, channels = pair_ref.shape
+    heads = w_bias.shape[0]
+    row_count = crossing_ref.shape[0] // heads
+    tile = 8
+    wide = count * tile
+    for local in range(count):
+        pair_ref[local] = rows_ref[local * residues : (local + 1) * residues].astype(jnp.float32)
+    first = lax.axis_index("row") * row_count
+    pieces = []
+    for i in range(row_count):
+        column = pair_ref[:, pl.ds(first + i, 1), :]
+        spread = jnp.broadcast_to(column, (count, tile, channels)).reshape(wide, channels)
+        pieces.append(dot_t(w_bias, spread.astype(jnp.bfloat16)).astype(jnp.bfloat16).astype(jnp.float32))
+    extra = jnp.concatenate(
+        [
+            jnp.broadcast_to(pieces[i][h : h + 1] + crossing_ref[h * row_count + i : h * row_count + i + 1], (tile, wide))
+            for h in range(heads)
+            for i in range(row_count)
+        ],
+        0,
+    )
+    shape = extra.shape
+    same = lax.broadcasted_iota(jnp.int32, shape, 0) % tile == lax.broadcasted_iota(jnp.int32, shape, 1) % tile
+    low = jnp.where(same, -1000000000.0, -1e30)
+    groups = range(residues // tile)
+    keys = [
+        pair_ref[:, g * tile : (g + 1) * tile, :].reshape(wide, channels).astype(jnp.bfloat16) for g in groups
+    ]
+    scores = [dot_t(asked[g], keys[g]) for g in groups]
+    scores = [
+        jnp.where(jnp.logical_and(same, keep_ref[g : g + 1, :] > 0), scores[g] + extra, low) for g in groups
+    ]
+    return scores, keys
+
+
+def near_attend_kernel(
+    row_count, residues, own_ref, w_att_ref, w_bias_ref, crossing_ref, keep_ref, asked_ref, gate_ref, top_ref, total_ref, context_ref, pair_ref
+):
     block_rows = row_count * residues
+    heads = w_bias_ref.shape[0]
     inner = w_att_ref.shape[1] // 4
     head_dim = inner // heads
     tile = 8
+    groups = range(residues // tile)
     mine = own_ref[spot_of(block_rows, lax.axis_index("row") // 2)]
     query = (dot(mine, w_att_ref[:, :inner]) * head_dim ** (-0.5)).astype(jnp.bfloat16)
     gate_ref[...] = sigmoid(dot(mine, w_att_ref[:, 3 * inner :]))
     head_of = lax.broadcasted_iota(jnp.int32, (1, inner), 1) // head_dim
-    asked = [
+    by_head = [
         dot_t(query, jnp.where(head_of == h, w_att_ref[:, inner : 2 * inner], 0)) for h in range(heads)
     ]
-    for g in range(residues // tile):
-        rows = [
-            asked[h][i * residues + g * tile : i * residues + (g + 1) * tile]
-            for h in range(heads)
-            for i in range(row_count)
-        ]
-        asked_ref[g] = jnp.concatenate(rows, 0).astype(jnp.bfloat16)
+    asked = [
+        jnp.concatenate(
+            [
+                by_head[h][i * residues + g * tile : i * residues + (g + 1) * tile]
+                for h in range(heads)
+                for i in range(row_count)
+            ],
+            0,
+        ).astype(jnp.bfloat16)
+        for g in groups
+    ]
+    for g in groups:
+        asked_ref[g] = asked[g]
+    scores, keys = half_attention(own_ref, pair_ref, asked, w_bias_ref[...], crossing_ref, keep_ref)
+    tops = [jnp.max(s, axis=-1, keepdims=True) for s in scores]
+    scores = [jnp.exp(s - top) for s, top in zip(scores, tops, strict=True)]
+    totals = [jnp.sum(s, axis=-1, keepdims=True) for s in scores]
+    for g in groups:
+        context_ref[g] = dot(scores[g].astype(jnp.bfloat16), keys[g])
+        top_ref[g] = jnp.broadcast_to(tops[g], top_ref.shape[1:])
+        total_ref[g] = jnp.broadcast_to(totals[g], total_ref.shape[1:])
 
 
 def attend_kernel(
     row_count,
-    own_ref,
     other_ref,
     mid_ref,
     asked_ref,
     gate_ref,
+    top_ref,
+    total_ref,
+    context_ref,
     crossing_ref,
     keep_ref,
     w_att_ref,
@@ -382,51 +457,21 @@
     out_ref,
     pair_ref,
 ):
-    residues, _, channels = pair_ref.shape
+    residues = pair_ref.shape[1]
     heads = w_bias_ref.shape[0]
     inner = w_out_ref.shape[0]
     head_dim = inner // heads
-    me = lax.axis_index("row")
-    core = me % 2
     block_rows = row_count * residues
-    for source, side in ((own_ref, core), (other_ref, 1 - core)):
-        for local in range(residues // 2):
-            spot = (2 * (local // row_count) + side) * row_count + local % row_count
-            pair_ref[pl.ds(spot, 1)] = source[local * residues : (local + 1) * residues].astype(jnp.float32)[None]
-
     tile = 8
-    wide = residues * tile
-    first = me * row_count
-    pieces = []
-    for i in range(row_count):
-        column = pair_ref[:, pl.ds(first + i, 1), :]
-        spread = jnp.broadcast_to(column, (residues, tile, channels)).reshape(wide, channels)
-        pieces.append(dot_t(w_bias_ref[...], spread.astype(jnp.bfloat16)).astype(jnp.bfloat16).astype(jnp.float32))
-    extra = jnp.concatenate(
-        [
-            jnp.broadcast_to(pieces[i][h : h + 1] + crossing_ref[h * row_count + i : h * row_count + i + 1], (tile, wide))
-            for h in range(heads)
-            for i in range(row_count)
-        ],
-        0,
-    )
-    total_rows = heads * row_count * tile
-    same = (
-        lax.broadcasted_iota(jnp.int32, (total_rows, wide), 0) % tile
-        == lax.broadcasted_iota(jnp.int32, (total_rows, wide), 1) % tile
-    )
-    low = jnp.where(same, -1000000000.0, -1e30)
     groups = range(residues // tile)
-    keys = [
-        pair_ref[:, g * tile : (g + 1) * tile, :].reshape(wide, channels).astype(jnp.bfloat16) for g in groups
-    ]
-    scores = [dot_t(asked_ref[g], keys[g]) for g in groups]
-    scores = [
-        jnp.where(jnp.logical_and(same, keep_ref[g : g + 1, :] > 0), scores[g] + extra, low) for g in groups
-    ]
-    scores = [jnp.exp(s - jnp.max(s, axis=-1, keepdims=True)) for s in scores]
-    weights = [(s * (1.0 / jnp.sum(s, axis=-1, keepdims=True))).astype(jnp.bfloat16) for s in scores]
-    context = [dot(weights[g], keys[g]) for g in groups]
+    asked = [asked_ref[g] for g in groups]
+    scores, keys = half_attention(other_ref, pair_ref, asked, w_bias_ref[...], crossing_ref, keep_ref)
+    tops = [jnp.maximum(jnp.max(scores[g], axis=-1, keepdims=True), top_ref[g]) for g in groups]
+    scales = [jnp.exp(top_ref[g] - tops[g]) for g in groups]
+    scores = [jnp.exp(scores[g] - tops[g][:, :1]) for g in groups]
+    totals = [jnp.sum(scores[g], axis=-1, keepdims=True) + total_ref[g] * scales[g] for g in groups]
+    context = [dot(scores[g].astype(jnp.bfloat16), keys[g]) + context_ref[g] * scales[g] for g in groups]
+    context = [context[g] * (1.0 / totals[g]) for g in groups]
 
     head_of = lax.broadcasted_iota(jnp.int32, (1, inner), 1) // head_dim
     values = jnp.zeros((block_rows, inner), jnp.float32)
@@ -439,7 +484,7 @@
         ]
         values = values + dot(jnp.concatenate(rows, 0).astype(jnp.bfloat16), w_value)
     gated = (values * gate_ref[...]).astype(jnp.bfloat16)
-    mid = mid_ref[spot_of(block_rows, me // 2)].astype(jnp.float32)
+    mid = mid_ref[spot_of(block_rows, lax.axis_index("row") // 2)].astype(jnp.float32)
     out_ref[...] = (mid + dot(gated, w_out_ref[...])).astype(jnp.bfloat16).reshape(out_ref.shape)
 
 
@@ -481,25 +526,27 @@
     pairs = own_count * residues
     block_rows = row_count * residues
     tile = 8
-    wide = residues * tile
+    wide = own_count * tile
     bf16, f32 = jnp.bfloat16, jnp.float32
 
     def swap(x, shift):
         return lax.ppermute(x, "row", [(i, i ^ shift) for i in range(row_devices)])
 
     base, held = [0], pair_acts
-    far, near, side = 8, 4, 2
+    far, near, side = 9, 5, 3
 
     def spread(shifts):
         return [o ^ s for s in shifts for o in base]
 
     shift = row_devices // 2
     while shift > far:
-        held = jnp.concatenate([held, swap(held, shift)], 0)
-        base = base + [o ^ shift for o in base]
+        held = jnp.concatenate([held, swap(held, shift + 1)], 0)
+        base = base + [o ^ (shift + 1) for o in base]
         shift //= 2
     from_far = swap(held, far)
     from_side = swap(held, side)
+    from_near = swap(held, near)
+    from_corner = swap(held, near ^ side)
 
     weights = [
         in_gain[None],
@@ -514,15 +561,15 @@
         w_att_out,
         held,
     ]
-    live, crossing, keep, in_g, mult_g, att_g, w_r, w_l, w_g, w_m, w_a, w_b, w_o, held = call(
+    live, crossing, keep, far_crossing, far_keep, in_g, mult_g, att_g, w_r, w_l, w_g, w_m, w_a, w_b, w_o, held = call(
         functools.partial(stage_kernel, len(weights)),
         [
             pltpu.with_memory_space_constraint(x, pltpu.HBM)
             for x in (cross_bias, chain_id, res_mask[None], chain_id[None], *weights)
         ],
-        [((residues, channels), f32), ((heads * row_count, wide), f32), ((residues // tile, wide), f32)]
+        [((residues, channels), f32)] + 2 * [((heads * row_count, wide), f32), ((residues // tile, wide), f32)]
         + [(w.shape, w.dtype) for w in weights],
-        2.0,
+        0.05,
         "stage",
         [
             pltpu.SMEM((heads,), f32),
@@ -533,23 +580,22 @@
         ],
         space=pltpu.HBM,
     )
-    pair = jnp.concatenate([held, from_far], 0)
-    from_near = swap(pair, near)
+    from_far_near = swap(from_far, near)
+    from_far_corner = swap(from_far, near ^ side)
     from_far_side = swap(from_far, side)
-    from_corner = swap(pair, near ^ side)
 
     sizes = [((pairs, channels), bf16), ((pairs, width), bf16), ((pairs, width), f32), ((pairs, channels), f32)]
     acts, right, left, gate = call(
-        functools.partial(early_kernel, spread([0, far, side]), row_count),
-        [live, in_g, w_r, w_l, w_g, pair, from_side],
+        functools.partial(early_kernel, spread([0, far, side, near, near ^ side]), row_count),
+        [live, in_g, w_r, w_l, w_g, held, from_far, from_side, from_near, from_corner],
         sizes,
-        0.6,
+        0.05,
         "early_edges",
     )
-    late = spread([near, near ^ far, far ^ side, near ^ side, near ^ far ^ side])
+    late = spread([far ^ near ^ side, far ^ near, far ^ side])
     acts, right, normed = call(
         functools.partial(right_kernel, late, row_count),
-        [live, in_g, w_r, from_near, from_far_side, from_corner, acts, right],
+        [live, in_g, w_r, from_far_corner, from_far_near, from_far_side, acts, right],
         [*sizes[:2], ((len(late) * block_rows, channels), bf16)],
         0.5,
         "right_edges",
@@ -574,20 +620,23 @@
         scratch=[pltpu.VMEM((pairs, width), f32), pltpu.VMEM((pairs, width), f32)],
     )
     normed_other = swap(normed_mid, 1)
-    asked, gate_att = call(
-        functools.partial(query_kernel, row_count, residues, heads),
-        [normed_mid, w_a],
-        [((residues // tile, heads * row_count * tile, channels), bf16), ((block_rows, w_o.shape[0]), f32)],
-        0.4,
-        "queries",
+    groups, asked_rows = residues // tile, heads * row_count * tile
+    asked, gate_att, top, total, context = call(
+        functools.partial(near_attend_kernel, row_count, residues),
+        [normed_mid, w_a, w_b, crossing, keep],
+        [((groups, asked_rows, channels), bf16), ((block_rows, w_o.shape[0]), f32)]
+        + 3 * [((groups, asked_rows, channels), f32)],
+        1.2,
+        "near_attend",
+        scratch=[pltpu.VMEM((own_count, residues, channels), f32)],
     )
     (out,) = call(
         functools.partial(attend_kernel, row_count),
-        [normed_mid, normed_other, mid, asked, gate_att, crossing, keep, w_a, w_b, w_o],
+        [normed_other, mid, asked, gate_att, top, total, context, far_crossing, far_keep, w_a, w_b, w_o],
         [((row_count, residues, channels), bf16)],
-        2.0,
+        1.5,
         "attend",
-        scratch=[pltpu.VMEM((residues, residues, channels), f32)],
+        scratch=[pltpu.VMEM((own_count, residues, channels), f32)],
     )
     return out
 

time: 22.5 us -> 21.1 us (0.938)
  waiting for transfers between devices: 4.03 us -> 1.3 us
  starting transfers between devices: 9.73 us -> 10.8 us
  Pallas kernels: 8.47 us -> 8.77 us
    ppermute x7 -> x9, waiting for transfers between devices: 4.03 us -> 1.3 us  [swap(): return lax.ppermute(x, 'row', [(i, i ^ shift) for i in range(row_devices)])]
    ppermute x7 -> x9, starting transfers between devices: 9.73 us -> 10.8 us  [swap(): return lax.ppermute(x, 'row', [(i, i ^ shift) for i in range(row_devices)])]
    pallas_call x7, Pallas kernels: 8.47 us -> 8.77 us  [call(): pl.pallas_call(body, out_shape=[jax.ShapeDtypeStruct(shape, dtype) for sh...]
  transfers between devices with their start and end apart: 7 -> 9, of which waited for: 2 -> 4; matrix products, arithmetic and copies ran while one was open for 0% -> 0% of each run, Pallas kernels for 16% -> 20%
where the time goes in v3:
time: 21.1 us; the launch traced here: 20.9 us
  starting transfers between devices  10.8 us (51%)
  Pallas kernels  8.77 us (42%)
  waiting for transfers between devices  1.3 us (6%)
    ppermute x9, starting transfers between devices, swap(): return lax.ppermute(x, 'row', [(i, i ^ shift) for i in range(row_devices)])  10.8 us
    pallas_call x7, Pallas kernels, call(): pl.pallas_call(body, out_shape=[jax.ShapeDtypeStruct(shape, dtype) for sh...  8.77 us
    ppermute x9, waiting for transfers between devices, swap(): return lax.ppermute(x, 'row', [(i, i ^ shift) for i in range(row_devices)])  1.3 us
  transfers between devices with their start and end apart: 9, of which 4 were waited for; matrix products, arithmetic and copies ran while one was open for 0% of the time, Pallas kernels for 20%

profile of v3, /device:TPU:0, one launch (start us, length us, event | category | flops | bytes accessed | tf_op | source)
XLA Modules:
  0.0 20.9 jit_solution(12165966973333344502)
XLA Ops:
  0.0 3.5 %collective-permute-start = (bf16[3,48,128]{2,1,0:T(8,128)(2,1)}, bf16[3,48,128]{2,1,0:T(8,128)(2,1)S(1)}, u32[]{:S(2)}, u32[]{:S(2)}) collective-permute-start(bf16[3,48,128]{2,1,0:T(8,128)(2,1)} %refs_14_.1), channel_id=1, source_target_pairs={{0,9},{1,8},{2,11},{3,10},{4,13},{5,12},{6,15},{7,14},{8,1},{9,0},... | collective-permute-start | bytes 110600 | tf_op jit(solution)/shard_map/ppermute | solution.py:533
  3.5 1.8 %collective-permute-start.4 = (bf16[3,48,128]{2,1,0:T(8,128)(2,1)}, bf16[3,48,128]{2,1,0:T(8,128)(2,1)S(1)}, u32[]{:S(2)}, u32[]{:S(2)}) collective-permute-start(bf16[3,48,128]{2,1,0:T(8,128)(2,1)} %refs_14_.1), channel_id=1, source_target_pairs={{0,3},{1,2},{2,1},{3,0},{4,7},{5,6},{6,5},{7,4},{8,11},{9,10},{10,... | collective-permute-start | bytes 110600 | tf_op jit(solution)/shard_map/ppermute | solution.py:533
  5.3 1.0 %collective-permute-start.5 = (bf16[3,48,128]{2,1,0:T(8,128)(2,1)}, bf16[3,48,128]{2,1,0:T(8,128)(2,1)S(1)}, u32[]{:S(2)}, u32[]{:S(2)}) collective-permute-start(bf16[3,48,128]{2,1,0:T(8,128)(2,1)} %refs_14_.1), channel_id=1, source_target_pairs={{0,5},{1,4},{2,7},{3,6},{4,1},{5,0},{6,3},{7,2},{8,13},{9,12},{10,... | collective-permute-start | bytes 110600 | tf_op jit(solution)/shard_map/ppermute | solution.py:533
  6.3 0.5 %collective-permute-start.6 = (bf16[3,48,128]{2,1,0:T(8,128)(2,1)}, bf16[3,48,128]{2,1,0:T(8,128)(2,1)S(1)}, u32[]{:S(2)}, u32[]{:S(2)}) collective-permute-start(bf16[3,48,128]{2,1,0:T(8,128)(2,1)} %refs_14_.1), channel_id=1, source_target_pairs={{0,6},{1,7},{2,4},{3,5},{4,2},{5,3},{6,0},{7,1},{8,14},{9,15},{10,... | collective-permute-start | bytes 110600 | tf_op jit(solution)/shard_map/ppermute | solution.py:533
  6.8 0.0 collective-permute-done.refs_1_
  6.8 2.4 %collective-permute-start.1 = (bf16[3,48,128]{2,1,0:T(8,128)(2,1)S(1)}, bf16[3,48,128]{2,1,0:T(8,128)(2,1)S(1)}, u32[]{:S(2)}, u32[]{:S(2)}) collective-permute-start(bf16[3,48,128]{2,1,0:T(8,128)(2,1)S(1)} %collective-permute-done.refs_1_), channel_id=1, source_target_pairs={{0,6},{1,7},{2,4},{3,5},{4,2},{5,3},{6,0},{7,1},{8,14},{9,15},{10,... | collective-permute-start | bytes 110600 | tf_op jit(solution)/shard_map/ppermute | solution.py:533
  9.2 0.2 collective-permute-start.2
  9.4 0.0 collective-permute-done.4.refs_2_
  9.4 0.6 %collective-permute-start.3 = (bf16[3,48,128]{2,1,0:T(8,128)(2,1)S(1)}, bf16[3,48,128]{2,1,0:T(8,128)(2,1)S(1)}, u32[]{:S(2)}, u32[]{:S(2)}) collective-permute-start(bf16[3,48,128]{2,1,0:T(8,128)(2,1)S(1)} %collective-permute-done.refs_1_), channel_id=1, source_target_pairs={{0,3},{1,2},{2,1},{3,0},{4,7},{5,6},{6,5},{7,4},{8,11},{9,10},{10,... | collective-permute-start | bytes 110600 | tf_op jit(solution)/shard_map/ppermute | solution.py:533
  10.0 1.2 %stage.1 = (f32[48,128]{1,0:T(8,128)S(1)}, f32[12,192]{1,0:T(8,128)S(1)}, f32[6,192]{1,0:T(8,128)S(1)}, f32[12,192]{1,0:T(8,128)S(1)}, f32[6,192]{1,0:T(8,128)S(...) custom-call(f32[4]{0:T(128)} %refs_0_.1, ...), custom_call_target="tpu_custom_call" | custom-call | flops 50000000 | bytes 262144 | tf_op jit(solution)/shard_map/stage/pallas_call | solution.py:492
  11.2 0.0 collective-permute-done.5.refs_3_
  11.3 0.5 %collective-permute-done.6.refs_4_ = bf16[3,48,128]{2,1,0:T(8,128)(2,1)S(1)} collective-permute-done((bf16[3,48,128]{2,1,0:T(8,128)(2,1)}, bf16[3,48,128]{2,1,0:T(8,128)(2,1)S(1)}, u32[]{:S(2)}, u32[]{:S(2)}) %collective-permute-start.6) | collective-permute-done | bytes 36896 | tf_op jit(solution)/shard_map/ppermute | solution.py:533
  11.8 0.8 %early_edges.1 = (bf16[1152,128]{1,0:T(8,128)(2,1)S(1)}, bf16[1152,128]{1,0:T(8,128)(2,1)S(1)}, f32[1152,128]{1,0:T(8,128)S(1)}, f32[1152,128]{1,0:T(8,128)S(1)}) custom-call(f32[48,128]{1,0:T(8,128)S(1)} %get-tuple-element.38.live_ref, f32[1,128]{1,0:T(1,128)S(1)} %get-tuple-element.39.gain_ref, bf16[128,256]{1,0:T(8,128)(2,1)S(1)} %get-tuple-element.40.w_right_ref, ...), custom_call_target="tpu_custom_call" | custom-call | flops 50000000 | bytes 262144 | tf_op jit(solution)/shard_map/early_edges/pallas_call | solution.py:492
  12.6 0.0 collective-permute-done.1.refs_0_
  12.6 0.1 collective-permute-done.2.refs_1_
  12.7 0.1 collective-permute-done.3.refs_2_
  12.8 0.4 %right_edges.1 = (bf16[1152,128]{1,0:T(8,128)(2,1)S(1)}, bf16[1152,128]{1,0:T(8,128)(2,1)S(1)}, bf16[432,128]{1,0:T(8,128)(2,1)S(1)}) custom-call(f32[48,128]{1,0:T(8,128)S(1)} %get-tuple-element.38.live_ref, f32[1,128]{1,0:T(1,128)S(1)} %get-tuple-element.39.gain_ref, ...), custom_call_target="tpu_custom_call", output_to_operand_aliasing={{0}: (6, {}), {1}: (7, {})} | custom-call | flops 500000000 | bytes 262144 | tf_op jit(solution)/shard_map/right_edges/pallas_call | solution.py:492
  13.2 0.6 %collective-permute-start.7 = (bf16[1152,128]{1,0:T(8,128)(2,1)S(1)}, bf16[1152,128]{1,0:T(8,128)(2,1)S(1)}, u32[]{:S(2)}, u32[]{:S(2)}) collective-permute-start(bf16[1152,128]{1,0:T(8,128)(2,1)S(1)} %get-tuple-element.47.right_ref), channel_id=1, source_target_pairs={{0,1},{1,0},{2,3},{3,2},{4,5},{5,4},{6,7},{7,6},{8,9},{9,8},{10,11... | collective-permute-start | bytes 884744 | tf_op jit(solution)/shard_map/ppermute | solution.py:533
  13.7 1.4 %left_edges.1 = (f32[1152,128]{1,0:T(8,128)S(1)}, f32[1152,128]{1,0:T(8,128)S(1)}, f32[576,128]{1,0:T(8,128)S(1)}) custom-call(bf16[432,128]{1,0:T(8,128)(2,1)S(1)} %get-tuple-element.46.normed_ref, bf16[1152,128]{1,0:T(8,128)(2,1)S(1)} %get-tuple-element.47.right_ref, ...), custom_call_target="tpu_custom_call", output_to_operand_aliasing={{0}: (4, {}), {1}: (5, {})} | custom-call | flops 1500000000 | bytes 262144 | tf_op jit(solution)/shard_map/left_edges/pallas_call | solution.py:492
  15.1 0.0 collective-permute-done.7.other_ref
  15.2 2.3 %product.1 = (bf16[1152,128]{1,0:T(8,128)(2,1)S(1)}, bf16[1152,128]{1,0:T(8,128)(2,1)S(1)}) custom-call(f32[1152,128]{1,0:T(8,128)S(1)} %get-tuple-element.50.left_ref, bf16[1152,128]{1,0:T(8,128)(2,1)S(1)} %collective-permute-done.7.other_ref, f32[576,128]{1,0:T(8,128)S(1)} %get-tuple-element.51.near_ref, f32[1152,128]{1,0:T(8,128)S(1)} %get-tuple-element.52.gate_ref, ...), custom_call_target="tpu_custom_call" | custom-call | flops 2400000000 | bytes 262144 | tf_op jit(solution)/shard_map/product/pallas_call | solution.py:492
  17.5 0.2 %collective-permute-start.8 = (bf16[1152,128]{1,0:T(8,128)(2,1)S(1)}, bf16[1152,128]{1,0:T(8,128)(2,1)S(1)}, u32[]{:S(2)}, u32[]{:S(2)}) collective-permute-start(bf16[1152,128]{1,0:T(8,128)(2,1)S(1)} %get-tuple-element.57.own_ref), channel_id=1, source_target_pairs={{0,1},{1,0},{2,3},{3,2},{4,5},{5,4},{6,7},{7,6},{8,9},{9,8},{10,11... | collective-permute-start | bytes 884744 | tf_op jit(solution)/shard_map/ppermute | solution.py:533
  17.7 0.8 %near_attend.1 = (bf16[6,96,128]{2,1,0:T(8,128)(2,1)S(1)}, f32[144,128]{1,0:T(8,128)S(1)}, f32[6,96,128]{2,1,0:T(8,128)S(1)}, f32[6,96,128]{2,1,0:T(8,128)S(1)}, f32[6,96,128]{2,1,0:T(8,128)S(1)}) custom-call(bf16[1152,128]{1,0:T(8,128)(2,1)S(1)} %get-tuple-element.57.own_ref, bf16[128,512]{1,0:T(8,128)(2,1)S(1)} %get-tuple-element.59.w_att_ref, ...), custom_call_target="tpu_custom_call" | custom-call | flops 1200000000 | bytes 262144 | tf_op jit(solution)/shard_map/near_attend/pallas_call | solution.py:492
  18.5 0.6 %collective-permute-done.8.other_ref = bf16[1152,128]{1,0:T(8,128)(2,1)S(1)} collective-permute-done((bf16[1152,128]{1,0:T(8,128)(2,1)S(1)}, bf16[1152,128]{1,0:T(8,128)(2,1)S(1)}, u32[]{:S(2)}, u32[]{:S(2)}) %collective-permute-start.8) | collective-permute-done | bytes 294944 | tf_op jit(solution)/shard_map/ppermute | solution.py:533
  19.1 1.8 %attend.1 = bf16[3,48,128]{2,1,0:T(8,128)(2,1)} custom-call(bf16[1152,128]{1,0:T(8,128)(2,1)S(1)} %collective-permute-done.8.other_ref, bf16[1152,128]{1,0:T(8,128)(2,1)S(1)} %get-tuple-element.58.mid_ref, bf16[6,96,128]{2,1,0:T(8,128)(2,1)S(1)} %get-tuple-element.63.asked_ref, f32[144,128]{1,0:T(8,128)S(1)} %get-tuple-element.64.gate_ref, ...), custom_call_target="tpu_custom_call" | custom-call | flops 1500000000 | bytes 262144 | tf_op jit(solution)/shard_map/attend/pallas_call | solution.py:492
  (1 shorter events, 0.0 us)
Async XLA Ops:
  0.0 6.8 %collective-permute-start = (bf16[3,48,128]{2,1,0:T(8,128)(2,1)}, bf16[3,48,128]{2,1,0:T(8,128)(2,1)S(1)}, u32[]{:S(2)}, u32[]{:S(2)}) collective-permute-start(bf16[3,48,128]{2,1,0:T(8,128)(2,1)} %refs_14_.1), channel_id=1, source_target_pairs={{0,9},{1,8},{2,11},{3,10},{4,13},{5,12},{6,15},{7,14},{8,1},{9,0},... | collective-permute-start | bytes 110600 | tf_op jit(solution)/shard_map/ppermute | solution.py:533
  3.5 5.9 %collective-permute-start.4 = (bf16[3,48,128]{2,1,0:T(8,128)(2,1)}, bf16[3,48,128]{2,1,0:T(8,128)(2,1)S(1)}, u32[]{:S(2)}, u32[]{:S(2)}) collective-permute-start(bf16[3,48,128]{2,1,0:T(8,128)(2,1)} %refs_14_.1), channel_id=1, source_target_pairs={{0,3},{1,2},{2,1},{3,0},{4,7},{5,6},{6,5},{7,4},{8,11},{9,10},{10,... | collective-permute-start | bytes 110600 | tf_op jit(solution)/shard_map/ppermute | solution.py:533
  5.3 6.0 %collective-permute-start.5 = (bf16[3,48,128]{2,1,0:T(8,128)(2,1)}, bf16[3,48,128]{2,1,0:T(8,128)(2,1)S(1)}, u32[]{:S(2)}, u32[]{:S(2)}) collective-permute-start(bf16[3,48,128]{2,1,0:T(8,128)(2,1)} %refs_14_.1), channel_id=1, source_target_pairs={{0,5},{1,4},{2,7},{3,6},{4,1},{5,0},{6,3},{7,2},{8,13},{9,12},{10,... | collective-permute-start | bytes 110600 | tf_op jit(solution)/shard_map/ppermute | solution.py:533
  6.3 5.5 %collective-permute-start.6 = (bf16[3,48,128]{2,1,0:T(8,128)(2,1)}, bf16[3,48,128]{2,1,0:T(8,128)(2,1)S(1)}, u32[]{:S(2)}, u32[]{:S(2)}) collective-permute-start(bf16[3,48,128]{2,1,0:T(8,128)(2,1)} %refs_14_.1), channel_id=1, source_target_pairs={{0,6},{1,7},{2,4},{3,5},{4,2},{5,3},{6,0},{7,1},{8,14},{9,15},{10,... | collective-permute-start | bytes 110600 | tf_op jit(solution)/shard_map/ppermute | solution.py:533
  6.8 5.8 %collective-permute-start.1 = (bf16[3,48,128]{2,1,0:T(8,128)(2,1)S(1)}, bf16[3,48,128]{2,1,0:T(8,128)(2,1)S(1)}, u32[]{:S(2)}, u32[]{:S(2)}) collective-permute-start(bf16[3,48,128]{2,1,0:T(8,128)(2,1)S(1)} %collective-permute-done.refs_1_), channel_id=1, source_target_pairs={{0,6},{1,7},{2,4},{3,5},{4,2},{5,3},{6,0},{7,1},{8,14},{9,15},{10,... | collective-permute-start | bytes 110600 | tf_op jit(solution)/shard_map/ppermute | solution.py:533
  9.2 3.4 %collective-permute-start.2 = (bf16[3,48,128]{2,1,0:T(8,128)(2,1)S(1)}, bf16[3,48,128]{2,1,0:T(8,128)(2,1)S(1)}, u32[]{:S(2)}, u32[]{:S(2)}) collective-permute-start(bf16[3,48,128]{2,1,0:T(8,128)(2,1)S(1)} %collective-permute-done.refs_1_), channel_id=1, source_target_pairs={{0,5},{1,4},{2,7},{3,6},{4,1},{5,0},{6,3},{7,2},{8,13},{9,12},{10,... | collective-permute-start | bytes 110600 | tf_op jit(solution)/shard_map/ppermute | solution.py:533
  9.4 3.4 %collective-permute-start.3 = (bf16[3,48,128]{2,1,0:T(8,128)(2,1)S(1)}, bf16[3,48,128]{2,1,0:T(8,128)(2,1)S(1)}, u32[]{:S(2)}, u32[]{:S(2)}) collective-permute-start(bf16[3,48,128]{2,1,0:T(8,128)(2,1)S(1)} %collective-permute-done.refs_1_), channel_id=1, source_target_pairs={{0,3},{1,2},{2,1},{3,0},{4,7},{5,6},{6,5},{7,4},{8,11},{9,10},{10,... | collective-permute-start | bytes 110600 | tf_op jit(solution)/shard_map/ppermute | solution.py:533
  13.2 2.0 %collective-permute-start.7 = (bf16[1152,128]{1,0:T(8,128)(2,1)S(1)}, bf16[1152,128]{1,0:T(8,128)(2,1)S(1)}, u32[]{:S(2)}, u32[]{:S(2)}) collective-permute-start(bf16[1152,128]{1,0:T(8,128)(2,1)S(1)} %get-tuple-element.47.right_ref), channel_id=1, source_target_pairs={{0,1},{1,0},{2,3},{3,2},{4,5},{5,4},{6,7},{7,6},{8,9},{9,8},{10,11... | collective-permute-start | bytes 884744 | tf_op jit(solution)/shard_map/ppermute | solution.py:533
  17.5 1.6 %collective-permute-start.8 = (bf16[1152,128]{1,0:T(8,128)(2,1)S(1)}, bf16[1152,128]{1,0:T(8,128)(2,1)S(1)}, u32[]{:S(2)}, u32[]{:S(2)}) collective-permute-start(bf16[1152,128]{1,0:T(8,128)(2,1)S(1)} %get-tuple-element.57.own_ref), channel_id=1, source_target_pairs={{0,1},{1,0},{2,3},{3,2},{4,5},{5,4},{6,7},{7,6},{8,9},{9,8},{10,11... | collective-permute-start | bytes 884744 | tf_op jit(solution)/shard_map/ppermute | solution.py:533

commit v4 on v3

--- a/solution.py
+++ b/solution.py
@@ -154,6 +154,17 @@
     return centred * lax.rsqrt(spread + norm_eps) * gain
 
 
+def norm_all(pieces, gain):
+    width = pieces[0].shape[-1]
+    ones = jnp.ones((width, width), jnp.bfloat16)
+    sums = [dot(x, ones) for x in pieces]
+    centred = [x.astype(jnp.float32) - s * (1.0 / width) for x, s in zip(pieces, sums, strict=True)]
+    spreads = [jnp.mean(c * c, axis=-1, keepdims=True) for c in centred]
+    return [
+        (c * lax.rsqrt(s + norm_eps) * gain).astype(jnp.bfloat16) for c, s in zip(centred, spreads, strict=True)
+    ]
+
+
 def gated_edges(normed, weight):
     both = dot(normed, weight)
     width = both.shape[1] // 2
@@ -354,15 +365,18 @@
 
     multiply(left_ref, turned_ref, residues, store)
 
-    block_rows = row_count * residues
-    for lower in range(0, acts_ref.shape[0], block_rows):
-        at = slice(lower, lower + block_rows)
-        product = product_ref[at].astype(jnp.bfloat16).astype(jnp.float32)
-        product = norm_rows(product, gain_ref[1:2]).astype(jnp.bfloat16)
-        update = gate_ref[at] * dot(product, w_out_ref[...])
-        mid = (acts_ref[at].astype(jnp.float32) + update).astype(jnp.bfloat16)
+    step = 2 * row_count * residues
+    spots = [slice(lower, lower + step) for lower in range(0, acts_ref.shape[0], step)]
+    normed = norm_all([product_ref[at].astype(jnp.bfloat16) for at in spots], gain_ref[1:2])
+    updates = [gate_ref[at] * dot(rows, w_out_ref[...]) for at, rows in zip(spots, normed, strict=True)]
+    mids = [
+        (acts_ref[at].astype(jnp.float32) + update).astype(jnp.bfloat16)
+        for at, update in zip(spots, updates, strict=True)
+    ]
+    for at, mid in zip(spots, mids, strict=True):
         mid_ref[at] = mid
-        normed_mid_ref[at] = norm_rows(mid.astype(jnp.float32), gain_ref[2:3]).astype(jnp.bfloat16)
+    for at, rows in zip(spots, norm_all(mids, gain_ref[2:3]), strict=True):
+        normed_mid_ref[at] = rows
 
 
 def half_attention(rows_ref, pair_ref, asked, w_bias, crossing_ref, keep_ref):
@@ -414,9 +428,9 @@
     query = (dot(mine, w_att_ref[:, :inner]) * head_dim ** (-0.5)).astype(jnp.bfloat16)
     gate_ref[...] = sigmoid(dot(mine, w_att_ref[:, 3 * inner :]))
     head_of = lax.broadcasted_iota(jnp.int32, (1, inner), 1) // head_dim
-    by_head = [
-        dot_t(query, jnp.where(head_of == h, w_att_ref[:, inner : 2 * inner], 0)) for h in range(heads)
-    ]
+    w_key = w_att_ref[:, inner : 2 * inner]
+    w_key = jnp.concatenate([jnp.where(head_of == h, w_key, 0) for h in range(heads)], 0)
+    by_head = jnp.split(dot_t(query, w_key), heads, 1)
     asked = [
         jnp.concatenate(
             [
@@ -468,21 +482,27 @@
     scores, keys = half_attention(other_ref, pair_ref, asked, w_bias_ref[...], crossing_ref, keep_ref)
     tops = [jnp.maximum(jnp.max(scores[g], axis=-1, keepdims=True), top_ref[g]) for g in groups]
     scales = [jnp.exp(top_ref[g] - tops[g]) for g in groups]
-    scores = [jnp.exp(scores[g] - tops[g][:, :1]) for g in groups]
+    copies = pl.cdiv(scores[0].shape[1], tops[0].shape[1])
+    scores = [jnp.exp(s - jnp.concatenate([top] * copies, 1)[:, : s.shape[1]]) for s, top in zip(scores, tops, strict=True)]
     totals = [jnp.sum(scores[g], axis=-1, keepdims=True) + total_ref[g] * scales[g] for g in groups]
     context = [dot(scores[g].astype(jnp.bfloat16), keys[g]) + context_ref[g] * scales[g] for g in groups]
     context = [context[g] * (1.0 / totals[g]) for g in groups]
 
     head_of = lax.broadcasted_iota(jnp.int32, (1, inner), 1) // head_dim
-    values = jnp.zeros((block_rows, inner), jnp.float32)
-    for h in range(heads):
-        w_value = jnp.where(head_of == h, w_att_ref[:, 2 * inner : 3 * inner], 0)
-        rows = [
-            context[g][(h * row_count + i) * tile : (h * row_count + i + 1) * tile]
-            for i in range(row_count)
-            for g in groups
-        ]
-        values = values + dot(jnp.concatenate(rows, 0).astype(jnp.bfloat16), w_value)
+    by_head = [
+        jnp.concatenate(
+            [
+                context[g][(h * row_count + i) * tile : (h * row_count + i + 1) * tile]
+                for i in range(row_count)
+                for g in groups
+            ],
+            0,
+        ).astype(jnp.bfloat16)
+        for h in range(heads)
+    ]
+    w_value = w_att_ref[:, 2 * inner : 3 * inner]
+    w_value = jnp.concatenate([jnp.where(head_of == h, w_value, 0) for h in range(heads)], 0)
+    values = dot(jnp.concatenate(by_head, 1), w_value)
     gated = (values * gate_ref[...]).astype(jnp.bfloat16)
     mid = mid_ref[spot_of(block_rows, lax.axis_index("row") // 2)].astype(jnp.float32)
     out_ref[...] = (mid + dot(gated, w_out_ref[...])).astype(jnp.bfloat16).reshape(out_ref.shape)

time: 21.1 us -> 20.6 us (0.976)
  Pallas kernels: 8.77 us -> 8.18 us
    pallas_call x7, Pallas kernels: 8.77 us -> 8.18 us  [call(): pl.pallas_call(body, out_shape=[jax.ShapeDtypeStruct(shape, dtype) for sh...]
  transfers between devices with their start and end apart: 9 -> 9, of which waited for: 4 -> 4; matrix products, arithmetic and copies ran while one was open for 0% -> 0% of each run, Pallas kernels for 20% -> 21%
where the time goes in v4:
time: 20.6 us; the launch traced here: 20.4 us
  starting transfers between devices  10.8 us (52%)
  Pallas kernels  8.18 us (40%)
  waiting for transfers between devices  1.36 us (7%)
    ppermute x9, starting transfers between devices, swap(): return lax.ppermute(x, 'row', [(i, i ^ shift) for i in range(row_devices)])  10.8 us
    pallas_call x7, Pallas kernels, call(): pl.pallas_call(body, out_shape=[jax.ShapeDtypeStruct(shape, dtype) for sh...  8.18 us
    ppermute x9, waiting for transfers between devices, swap(): return lax.ppermute(x, 'row', [(i, i ^ shift) for i in range(row_devices)])  1.36 us
  transfers between devices with their start and end apart: 9, of which 4 were waited for; matrix products, arithmetic and copies ran while one was open for 0% of the time, Pallas kernels for 21%

profile of v4, /device:TPU:0, one launch (start us, length us, event | category | flops | bytes accessed | tf_op | source)
XLA Modules:
  0.0 20.4 jit_solution(8347872880051424992)
XLA Ops:
  0.0 3.5 %collective-permute-start = (bf16[3,48,128]{2,1,0:T(8,128)(2,1)}, bf16[3,48,128]{2,1,0:T(8,128)(2,1)S(1)}, u32[]{:S(2)}, u32[]{:S(2)}) collective-permute-start(bf16[3,48,128]{2,1,0:T(8,128)(2,1)} %refs_14_.1), channel_id=1, source_target_pairs={{0,9},{1,8},{2,11},{3,10},{4,13},{5,12},{6,15},{7,14},{8,1},{9,0},... | collective-permute-start | bytes 110600 | tf_op jit(solution)/shard_map/ppermute | solution.py:553
  3.5 1.8 %collective-permute-start.4 = (bf16[3,48,128]{2,1,0:T(8,128)(2,1)}, bf16[3,48,128]{2,1,0:T(8,128)(2,1)S(1)}, u32[]{:S(2)}, u32[]{:S(2)}) collective-permute-start(bf16[3,48,128]{2,1,0:T(8,128)(2,1)} %refs_14_.1), channel_id=1, source_target_pairs={{0,3},{1,2},{2,1},{3,0},{4,7},{5,6},{6,5},{7,4},{8,11},{9,10},{10,... | collective-permute-start | bytes 110600 | tf_op jit(solution)/shard_map/ppermute | solution.py:553
  5.3 1.0 %collective-permute-start.5 = (bf16[3,48,128]{2,1,0:T(8,128)(2,1)}, bf16[3,48,128]{2,1,0:T(8,128)(2,1)S(1)}, u32[]{:S(2)}, u32[]{:S(2)}) collective-permute-start(bf16[3,48,128]{2,1,0:T(8,128)(2,1)} %refs_14_.1), channel_id=1, source_target_pairs={{0,5},{1,4},{2,7},{3,6},{4,1},{5,0},{6,3},{7,2},{8,13},{9,12},{10,... | collective-permute-start | bytes 110600 | tf_op jit(solution)/shard_map/ppermute | solution.py:553
  6.3 0.5 %collective-permute-start.6 = (bf16[3,48,128]{2,1,0:T(8,128)(2,1)}, bf16[3,48,128]{2,1,0:T(8,128)(2,1)S(1)}, u32[]{:S(2)}, u32[]{:S(2)}) collective-permute-start(bf16[3,48,128]{2,1,0:T(8,128)(2,1)} %refs_14_.1), channel_id=1, source_target_pairs={{0,6},{1,7},{2,4},{3,5},{4,2},{5,3},{6,0},{7,1},{8,14},{9,15},{10,... | collective-permute-start | bytes 110600 | tf_op jit(solution)/shard_map/ppermute | solution.py:553
  6.8 0.0 collective-permute-done.refs_1_
  6.8 2.4 %collective-permute-start.1 = (bf16[3,48,128]{2,1,0:T(8,128)(2,1)S(1)}, bf16[3,48,128]{2,1,0:T(8,128)(2,1)S(1)}, u32[]{:S(2)}, u32[]{:S(2)}) collective-permute-start(bf16[3,48,128]{2,1,0:T(8,128)(2,1)S(1)} %collective-permute-done.refs_1_), channel_id=1, source_target_pairs={{0,6},{1,7},{2,4},{3,5},{4,2},{5,3},{6,0},{7,1},{8,14},{9,15},{10,... | collective-permute-start | bytes 110600 | tf_op jit(solution)/shard_map/ppermute | solution.py:553
  9.2 0.2 collective-permute-start.2
  9.4 0.0 collective-permute-done.4.refs_2_
  9.4 0.6 %collective-permute-start.3 = (bf16[3,48,128]{2,1,0:T(8,128)(2,1)S(1)}, bf16[3,48,128]{2,1,0:T(8,128)(2,1)S(1)}, u32[]{:S(2)}, u32[]{:S(2)}) collective-permute-start(bf16[3,48,128]{2,1,0:T(8,128)(2,1)S(1)} %collective-permute-done.refs_1_), channel_id=1, source_target_pairs={{0,3},{1,2},{2,1},{3,0},{4,7},{5,6},{6,5},{7,4},{8,11},{9,10},{10,... | collective-permute-start | bytes 110600 | tf_op jit(solution)/shard_map/ppermute | solution.py:553
  10.0 1.2 %stage.1 = (f32[48,128]{1,0:T(8,128)S(1)}, f32[12,192]{1,0:T(8,128)S(1)}, f32[6,192]{1,0:T(8,128)S(1)}, f32[12,192]{1,0:T(8,128)S(1)}, f32[6,192]{1,0:T(8,128)S(...) custom-call(f32[4]{0:T(128)} %refs_0_.1, ...), custom_call_target="tpu_custom_call" | custom-call | flops 50000000 | bytes 262144 | tf_op jit(solution)/shard_map/stage/pallas_call | solution.py:512
  11.2 0.0 collective-permute-done.5.refs_3_
  11.3 0.5 %collective-permute-done.6.refs_4_ = bf16[3,48,128]{2,1,0:T(8,128)(2,1)S(1)} collective-permute-done((bf16[3,48,128]{2,1,0:T(8,128)(2,1)}, bf16[3,48,128]{2,1,0:T(8,128)(2,1)S(1)}, u32[]{:S(2)}, u32[]{:S(2)}) %collective-permute-start.6) | collective-permute-done | bytes 36896 | tf_op jit(solution)/shard_map/ppermute | solution.py:553
  11.8 0.8 %early_edges.1 = (bf16[1152,128]{1,0:T(8,128)(2,1)S(1)}, bf16[1152,128]{1,0:T(8,128)(2,1)S(1)}, f32[1152,128]{1,0:T(8,128)S(1)}, f32[1152,128]{1,0:T(8,128)S(1)}) custom-call(f32[48,128]{1,0:T(8,128)S(1)} %get-tuple-element.38.live_ref, f32[1,128]{1,0:T(1,128)S(1)} %get-tuple-element.39.gain_ref, bf16[128,256]{1,0:T(8,128)(2,1)S(1)} %get-tuple-element.40.w_right_ref, ...), custom_call_target="tpu_custom_call" | custom-call | flops 50000000 | bytes 262144 | tf_op jit(solution)/shard_map/early_edges/pallas_call | solution.py:512
  12.6 0.0 collective-permute-done.1.refs_0_
  12.6 0.1 collective-permute-done.2.refs_1_
  12.7 0.1 collective-permute-done.3.refs_2_
  12.8 0.4 %right_edges.1 = (bf16[1152,128]{1,0:T(8,128)(2,1)S(1)}, bf16[1152,128]{1,0:T(8,128)(2,1)S(1)}, bf16[432,128]{1,0:T(8,128)(2,1)S(1)}) custom-call(f32[48,128]{1,0:T(8,128)S(1)} %get-tuple-element.38.live_ref, f32[1,128]{1,0:T(1,128)S(1)} %get-tuple-element.39.gain_ref, ...), custom_call_target="tpu_custom_call", output_to_operand_aliasing={{0}: (6, {}), {1}: (7, {})} | custom-call | flops 500000000 | bytes 262144 | tf_op jit(solution)/shard_map/right_edges/pallas_call | solution.py:512
  13.2 0.6 %collective-permute-start.7 = (bf16[1152,128]{1,0:T(8,128)(2,1)S(1)}, bf16[1152,128]{1,0:T(8,128)(2,1)S(1)}, u32[]{:S(2)}, u32[]{:S(2)}) collective-permute-start(bf16[1152,128]{1,0:T(8,128)(2,1)S(1)} %get-tuple-element.47.right_ref), channel_id=1, source_target_pairs={{0,1},{1,0},{2,3},{3,2},{4,5},{5,4},{6,7},{7,6},{8,9},{9,8},{10,11... | collective-permute-start | bytes 884744 | tf_op jit(solution)/shard_map/ppermute | solution.py:553
  13.7 1.4 %left_edges.1 = (f32[1152,128]{1,0:T(8,128)S(1)}, f32[1152,128]{1,0:T(8,128)S(1)}, f32[576,128]{1,0:T(8,128)S(1)}) custom-call(bf16[432,128]{1,0:T(8,128)(2,1)S(1)} %get-tuple-element.46.normed_ref, bf16[1152,128]{1,0:T(8,128)(2,1)S(1)} %get-tuple-element.47.right_ref, ...), custom_call_target="tpu_custom_call", output_to_operand_aliasing={{0}: (4, {}), {1}: (5, {})} | custom-call | flops 1500000000 | bytes 262144 | tf_op jit(solution)/shard_map/left_edges/pallas_call | solution.py:512
  15.1 0.0 collective-permute-done.7.other_ref
  15.2 2.0 %product.1 = (bf16[1152,128]{1,0:T(8,128)(2,1)S(1)}, bf16[1152,128]{1,0:T(8,128)(2,1)S(1)}) custom-call(f32[1152,128]{1,0:T(8,128)S(1)} %get-tuple-element.50.left_ref, bf16[1152,128]{1,0:T(8,128)(2,1)S(1)} %collective-permute-done.7.other_ref, f32[576,128]{1,0:T(8,128)S(1)} %get-tuple-element.51.near_ref, f32[1152,128]{1,0:T(8,128)S(1)} %get-tuple-element.52.gate_ref, ...), custom_call_target="tpu_custom_call" | custom-call | flops 2400000000 | bytes 262144 | tf_op jit(solution)/shard_map/product/pallas_call | solution.py:512
  17.1 0.2 %collective-permute-start.8 = (bf16[1152,128]{1,0:T(8,128)(2,1)S(1)}, bf16[1152,128]{1,0:T(8,128)(2,1)S(1)}, u32[]{:S(2)}, u32[]{:S(2)}) collective-permute-start(bf16[1152,128]{1,0:T(8,128)(2,1)S(1)} %get-tuple-element.57.own_ref), channel_id=1, source_target_pairs={{0,1},{1,0},{2,3},{3,2},{4,5},{5,4},{6,7},{7,6},{8,9},{9,8},{10,11... | collective-permute-start | bytes 884744 | tf_op jit(solution)/shard_map/ppermute | solution.py:553
  17.4 0.8 %near_attend.1 = (bf16[6,96,128]{2,1,0:T(8,128)(2,1)S(1)}, f32[144,128]{1,0:T(8,128)S(1)}, f32[6,96,128]{2,1,0:T(8,128)S(1)}, f32[6,96,128]{2,1,0:T(8,128)S(1)}, f32[6,96,128]{2,1,0:T(8,128)S(1)}) custom-call(bf16[1152,128]{1,0:T(8,128)(2,1)S(1)} %get-tuple-element.57.own_ref, bf16[128,512]{1,0:T(8,128)(2,1)S(1)} %get-tuple-element.59.w_att_ref, ...), custom_call_target="tpu_custom_call" | custom-call | flops 1200000000 | bytes 262144 | tf_op jit(solution)/shard_map/near_attend/pallas_call | solution.py:512
  18.1 0.6 %collective-permute-done.8.other_ref = bf16[1152,128]{1,0:T(8,128)(2,1)S(1)} collective-permute-done((bf16[1152,128]{1,0:T(8,128)(2,1)S(1)}, bf16[1152,128]{1,0:T(8,128)(2,1)S(1)}, u32[]{:S(2)}, u32[]{:S(2)}) %collective-permute-start.8) | collective-permute-done | bytes 294944 | tf_op jit(solution)/shard_map/ppermute | solution.py:553
  18.8 1.6 %attend.1 = bf16[3,48,128]{2,1,0:T(8,128)(2,1)} custom-call(bf16[1152,128]{1,0:T(8,128)(2,1)S(1)} %collective-permute-done.8.other_ref, bf16[1152,128]{1,0:T(8,128)(2,1)S(1)} %get-tuple-element.58.mid_ref, bf16[6,96,128]{2,1,0:T(8,128)(2,1)S(1)} %get-tuple-element.63.asked_ref, f32[144,128]{1,0:T(8,128)S(1)} %get-tuple-element.64.gate_ref, ...), custom_call_target="tpu_custom_call" | custom-call | flops 1500000000 | bytes 262144 | tf_op jit(solution)/shard_map/attend/pallas_call | solution.py:512
  (1 shorter events, 0.0 us)
Async XLA Ops:
  0.0 6.8 %collective-permute-start = (bf16[3,48,128]{2,1,0:T(8,128)(2,1)}, bf16[3,48,128]{2,1,0:T(8,128)(2,1)S(1)}, u32[]{:S(2)}, u32[]{:S(2)}) collective-permute-start(bf16[3,48,128]{2,1,0:T(8,128)(2,1)} %refs_14_.1), channel_id=1, source_target_pairs={{0,9},{1,8},{2,11},{3,10},{4,13},{5,12},{6,15},{7,14},{8,1},{9,0},... | collective-permute-start | bytes 110600 | tf_op jit(solution)/shard_map/ppermute | solution.py:553
  3.5 5.9 %collective-permute-start.4 = (bf16[3,48,128]{2,1,0:T(8,128)(2,1)}, bf16[3,48,128]{2,1,0:T(8,128)(2,1)S(1)}, u32[]{:S(2)}, u32[]{:S(2)}) collective-permute-start(bf16[3,48,128]{2,1,0:T(8,128)(2,1)} %refs_14_.1), channel_id=1, source_target_pairs={{0,3},{1,2},{2,1},{3,0},{4,7},{5,6},{6,5},{7,4},{8,11},{9,10},{10,... | collective-permute-start | bytes 110600 | tf_op jit(solution)/shard_map/ppermute | solution.py:553
  5.3 6.0 %collective-permute-start.5 = (bf16[3,48,128]{2,1,0:T(8,128)(2,1)}, bf16[3,48,128]{2,1,0:T(8,128)(2,1)S(1)}, u32[]{:S(2)}, u32[]{:S(2)}) collective-permute-start(bf16[3,48,128]{2,1,0:T(8,128)(2,1)} %refs_14_.1), channel_id=1, source_target_pairs={{0,5},{1,4},{2,7},{3,6},{4,1},{5,0},{6,3},{7,2},{8,13},{9,12},{10,... | collective-permute-start | bytes 110600 | tf_op jit(solution)/shard_map/ppermute | solution.py:553
  6.3 5.5 %collective-permute-start.6 = (bf16[3,48,128]{2,1,0:T(8,128)(2,1)}, bf16[3,48,128]{2,1,0:T(8,128)(2,1)S(1)}, u32[]{:S(2)}, u32[]{:S(2)}) collective-permute-start(bf16[3,48,128]{2,1,0:T(8,128)(2,1)} %refs_14_.1), channel_id=1, source_target_pairs={{0,6},{1,7},{2,4},{3,5},{4,2},{5,3},{6,0},{7,1},{8,14},{9,15},{10,... | collective-permute-start | bytes 110600 | tf_op jit(solution)/shard_map/ppermute | solution.py:553
  6.8 5.8 %collective-permute-start.1 = (bf16[3,48,128]{2,1,0:T(8,128)(2,1)S(1)}, bf16[3,48,128]{2,1,0:T(8,128)(2,1)S(1)}, u32[]{:S(2)}, u32[]{:S(2)}) collective-permute-start(bf16[3,48,128]{2,1,0:T(8,128)(2,1)S(1)} %collective-permute-done.refs_1_), channel_id=1, source_target_pairs={{0,6},{1,7},{2,4},{3,5},{4,2},{5,3},{6,0},{7,1},{8,14},{9,15},{10,... | collective-permute-start | bytes 110600 | tf_op jit(solution)/shard_map/ppermute | solution.py:553
  9.2 3.4 %collective-permute-start.2 = (bf16[3,48,128]{2,1,0:T(8,128)(2,1)S(1)}, bf16[3,48,128]{2,1,0:T(8,128)(2,1)S(1)}, u32[]{:S(2)}, u32[]{:S(2)}) collective-permute-start(bf16[3,48,128]{2,1,0:T(8,128)(2,1)S(1)} %collective-permute-done.refs_1_), channel_id=1, source_target_pairs={{0,5},{1,4},{2,7},{3,6},{4,1},{5,0},{6,3},{7,2},{8,13},{9,12},{10,... | collective-permute-start | bytes 110600 | tf_op jit(solution)/shard_map/ppermute | solution.py:553
  9.4 3.4 %collective-permute-start.3 = (bf16[3,48,128]{2,1,0:T(8,128)(2,1)S(1)}, bf16[3,48,128]{2,1,0:T(8,128)(2,1)S(1)}, u32[]{:S(2)}, u32[]{:S(2)}) collective-permute-start(bf16[3,48,128]{2,1,0:T(8,128)(2,1)S(1)} %collective-permute-done.refs_1_), channel_id=1, source_target_pairs={{0,3},{1,2},{2,1},{3,0},{4,7},{5,6},{6,5},{7,4},{8,11},{9,10},{10,... | collective-permute-start | bytes 110600 | tf_op jit(solution)/shard_map/ppermute | solution.py:553
  13.2 2.0 %collective-permute-start.7 = (bf16[1152,128]{1,0:T(8,128)(2,1)S(1)}, bf16[1152,128]{1,0:T(8,128)(2,1)S(1)}, u32[]{:S(2)}, u32[]{:S(2)}) collective-permute-start(bf16[1152,128]{1,0:T(8,128)(2,1)S(1)} %get-tuple-element.47.right_ref), channel_id=1, source_target_pairs={{0,1},{1,0},{2,3},{3,2},{4,5},{5,4},{6,7},{7,6},{8,9},{9,8},{10,11... | collective-permute-start | bytes 884744 | tf_op jit(solution)/shard_map/ppermute | solution.py:553
  17.1 1.6 %collective-permute-start.8 = (bf16[1152,128]{1,0:T(8,128)(2,1)S(1)}, bf16[1152,128]{1,0:T(8,128)(2,1)S(1)}, u32[]{:S(2)}, u32[]{:S(2)}) collective-permute-start(bf16[1152,128]{1,0:T(8,128)(2,1)S(1)} %get-tuple-element.57.own_ref), channel_id=1, source_target_pairs={{0,1},{1,0},{2,3},{3,2},{4,5},{5,4},{6,7},{7,6},{8,9},{9,8},{10,11... | collective-permute-start | bytes 884744 | tf_op jit(solution)/shard_map/ppermute | solution.py:553

commit v5 on v4

--- a/solution.py
+++ b/solution.py
@@ -312,16 +312,16 @@
     lax.fori_loop(0, own_count // row_block, rows_of, 0)
 
 
-def left_kernel(
-    offsets, row_count, residues, normed_ref, right_ref, w_left_ref, w_gate_ref, _, __, left_ref, gate_ref, near_ref, turned_ref
-):
+def left_kernel(late, row_count, residues, *refs):
+    *normed_refs, right_ref, w_left_ref, w_gate_ref, _, _, left_ref, gate_ref, near_ref, turned_ref = refs
     me = lax.axis_index("row")
     block_rows = row_count * residues
-    for t, offset in enumerate(offsets):
-        spot = spot_of(block_rows, jnp.bitwise_xor(me, offset) // 2)
-        normed = normed_ref[t * block_rows : (t + 1) * block_rows]
-        left_ref[spot] = gated_edges(normed, w_left_ref[...]).astype(jnp.float32)
-        gate_ref[spot] = sigmoid(dot(normed, w_gate_ref[...]))
+    for offsets, normed_ref in zip(late, normed_refs, strict=True):
+        for t, offset in enumerate(offsets):
+            spot = spot_of(block_rows, jnp.bitwise_xor(me, offset) // 2)
+            normed = normed_ref[t * block_rows : (t + 1) * block_rows]
+            left_ref[spot] = gated_edges(normed, w_left_ref[...]).astype(jnp.float32)
+            gate_ref[spot] = sigmoid(dot(normed, w_gate_ref[...]))
     turn(right_ref, turned_ref, row_count, residues)
     count = turned_ref.shape[0] // residues
 
@@ -612,24 +612,27 @@
         0.05,
         "early_edges",
     )
-    late = spread([far ^ near ^ side, far ^ near, far ^ side])
-    acts, right, normed = call(
-        functools.partial(right_kernel, late, row_count),
-        [live, in_g, w_r, from_far_corner, from_far_near, from_far_side, acts, right],
-        [*sizes[:2], ((len(late) * block_rows, channels), bf16)],
-        0.5,
-        "right_edges",
-        aliases={6: 0, 7: 1},
-    )
+    late = [spread([far ^ near ^ side, far ^ near]), spread([far ^ side])]
+    normed = []
+    for offsets, pieces in zip(late, ([from_far_corner, from_far_near], [from_far_side]), strict=True):
+        acts, right, rows = call(
+            functools.partial(right_kernel, offsets, row_count),
+            [live, in_g, w_r, *pieces, acts, right],
+            [*sizes[:2], ((len(offsets) * block_rows, channels), bf16)],
+            0.05,
+            "right_edges",
+            aliases={3 + len(pieces): 0, 4 + len(pieces): 1},
+        )
+        normed.append(rows)
     other = swap(right, 1)
     left, gate, near_product = call(
         functools.partial(left_kernel, late, row_count, residues),
-        [normed, right, w_l, w_g, left, gate],
+        [*normed, right, w_l, w_g, left, gate],
         [*sizes[2:], ((own_count * own_count, width), f32)],
         1.5,
         "left_edges",
         scratch=[pltpu.VMEM((pairs, width), f32)],
-        aliases={4: 0, 5: 1},
+        aliases={3 + len(normed): 0, 4 + len(normed): 1},
     )
     mid, normed_mid = call(
         functools.partial(product_kernel, row_count, residues),

time: 20.6 us -> 20.5 us (level)
  Pallas kernels: 8.18 us -> 8.45 us
  waiting for transfers between devices: 1.36 us -> 1.15 us
    pallas_call x7 -> x8, Pallas kernels: 8.18 us -> 8.45 us  [call(): pl.pallas_call(body, out_shape=[jax.ShapeDtypeStruct(shape, dtype) for sh...]
    ppermute x9, waiting for transfers between devices: 1.36 us -> 1.15 us  [swap(): return lax.ppermute(x, 'row', [(i, i ^ shift) for i in range(row_devices)])]
  transfers between devices with their start and end apart: 9 -> 9, of which waited for: 4 -> 3; matrix products, arithmetic and copies ran while one was open for 0% -> 0% of each run, Pallas kernels for 21% -> 22%
where the time goes in v5:
time: 20.5 us; the launch traced here: 20.3 us
  starting transfers between devices  10.6 us (52%)
  Pallas kernels  8.45 us (41%)
  waiting for transfers between devices  1.15 us (6%)
    ppermute x9, starting transfers between devices, swap(): return lax.ppermute(x, 'row', [(i, i ^ shift) for i in range(row_devices)])  10.6 us
    pallas_call x8, Pallas kernels, call(): pl.pallas_call(body, out_shape=[jax.ShapeDtypeStruct(shape, dtype) for sh...  8.45 us
    ppermute x9, waiting for transfers between devices, swap(): return lax.ppermute(x, 'row', [(i, i ^ shift) for i in range(row_devices)])  1.15 us
  transfers between devices with their start and end apart: 9, of which 3 were waited for; matrix products, arithmetic and copies ran while one was open for 0% of the time, Pallas kernels for 22%

profile of v5, /device:TPU:0, one launch (start us, length us, event | category | flops | bytes accessed | tf_op | source)
XLA Modules:
  0.0 20.3 jit_solution(6144394017885015566)
XLA Ops:
  0.0 3.5 %collective-permute-start = (bf16[3,48,128]{2,1,0:T(8,128)(2,1)}, bf16[3,48,128]{2,1,0:T(8,128)(2,1)S(1)}, u32[]{:S(2)}, u32[]{:S(2)}) collective-permute-start(bf16[3,48,128]{2,1,0:T(8,128)(2,1)} %refs_14_.1), channel_id=1, source_target_pairs={{0,9},{1,8},{2,11},{3,10},{4,13},{5,12},{6,15},{7,14},{8,1},{9,0},... | collective-permute-start | bytes 110600 | tf_op jit(solution)/shard_map/ppermute | solution.py:553
  3.5 1.8 %collective-permute-start.3 = (bf16[3,48,128]{2,1,0:T(8,128)(2,1)}, bf16[3,48,128]{2,1,0:T(8,128)(2,1)S(1)}, u32[]{:S(2)}, u32[]{:S(2)}) collective-permute-start(bf16[3,48,128]{2,1,0:T(8,128)(2,1)} %refs_14_.1), channel_id=1, source_target_pairs={{0,3},{1,2},{2,1},{3,0},{4,7},{5,6},{6,5},{7,4},{8,11},{9,10},{10,... | collective-permute-start | bytes 110600 | tf_op jit(solution)/shard_map/ppermute | solution.py:553
  5.3 1.0 %collective-permute-start.4 = (bf16[3,48,128]{2,1,0:T(8,128)(2,1)}, bf16[3,48,128]{2,1,0:T(8,128)(2,1)S(1)}, u32[]{:S(2)}, u32[]{:S(2)}) collective-permute-start(bf16[3,48,128]{2,1,0:T(8,128)(2,1)} %refs_14_.1), channel_id=1, source_target_pairs={{0,5},{1,4},{2,7},{3,6},{4,1},{5,0},{6,3},{7,2},{8,13},{9,12},{10,... | collective-permute-start | bytes 110600 | tf_op jit(solution)/shard_map/ppermute | solution.py:553
  6.3 0.5 %collective-permute-start.5 = (bf16[3,48,128]{2,1,0:T(8,128)(2,1)}, bf16[3,48,128]{2,1,0:T(8,128)(2,1)S(1)}, u32[]{:S(2)}, u32[]{:S(2)}) collective-permute-start(bf16[3,48,128]{2,1,0:T(8,128)(2,1)} %refs_14_.1), channel_id=1, source_target_pairs={{0,6},{1,7},{2,4},{3,5},{4,2},{5,3},{6,0},{7,1},{8,14},{9,15},{10,... | collective-permute-start | bytes 110600 | tf_op jit(solution)/shard_map/ppermute | solution.py:553
  6.8 0.0 collective-permute-done.refs_1_
  6.8 2.4 %collective-permute-start.1 = (bf16[3,48,128]{2,1,0:T(8,128)(2,1)S(1)}, bf16[3,48,128]{2,1,0:T(8,128)(2,1)S(1)}, u32[]{:S(2)}, u32[]{:S(2)}) collective-permute-start(bf16[3,48,128]{2,1,0:T(8,128)(2,1)S(1)} %collective-permute-done.refs_1_), channel_id=1, source_target_pairs={{0,6},{1,7},{2,4},{3,5},{4,2},{5,3},{6,0},{7,1},{8,14},{9,15},{10,... | collective-permute-start | bytes 110600 | tf_op jit(solution)/shard_map/ppermute | solution.py:553
  9.2 0.2 collective-permute-start.2
  9.4 0.0 collective-permute-done.3.refs_2_
  9.4 0.6 %collective-permute-start.6 = (bf16[3,48,128]{2,1,0:T(8,128)(2,1)S(1)}, bf16[3,48,128]{2,1,0:T(8,128)(2,1)S(1)}, u32[]{:S(2)}, u32[]{:S(2)}) collective-permute-start(bf16[3,48,128]{2,1,0:T(8,128)(2,1)S(1)} %collective-permute-done.refs_1_), channel_id=1, source_target_pairs={{0,3},{1,2},{2,1},{3,0},{4,7},{5,6},{6,5},{7,4},{8,11},{9,10},{10,... | collective-permute-start | bytes 110600 | tf_op jit(solution)/shard_map/ppermute | solution.py:553
  10.0 1.2 %stage.1 = (f32[48,128]{1,0:T(8,128)S(1)}, f32[12,192]{1,0:T(8,128)S(1)}, f32[6,192]{1,0:T(8,128)S(1)}, f32[12,192]{1,0:T(8,128)S(1)}, f32[6,192]{1,0:T(8,128)S(...) custom-call(f32[4]{0:T(128)} %refs_0_.1, ...), custom_call_target="tpu_custom_call" | custom-call | flops 50000000 | bytes 262144 | tf_op jit(solution)/shard_map/stage/pallas_call | solution.py:512
  11.2 0.0 collective-permute-done.4.refs_3_
  11.3 0.5 %collective-permute-done.5.refs_4_ = bf16[3,48,128]{2,1,0:T(8,128)(2,1)S(1)} collective-permute-done((bf16[3,48,128]{2,1,0:T(8,128)(2,1)}, bf16[3,48,128]{2,1,0:T(8,128)(2,1)S(1)}, u32[]{:S(2)}, u32[]{:S(2)}) %collective-permute-start.5) | collective-permute-done | bytes 36896 | tf_op jit(solution)/shard_map/ppermute | solution.py:553
  11.8 0.8 %early_edges.1 = (bf16[1152,128]{1,0:T(8,128)(2,1)S(1)}, bf16[1152,128]{1,0:T(8,128)(2,1)S(1)}, f32[1152,128]{1,0:T(8,128)S(1)}, f32[1152,128]{1,0:T(8,128)S(1)}) custom-call(f32[48,128]{1,0:T(8,128)S(1)} %get-tuple-element.41.live_ref, f32[1,128]{1,0:T(1,128)S(1)} %get-tuple-element.42.gain_ref, bf16[128,256]{1,0:T(8,128)(2,1)S(1)} %get-tuple-element.43.w_right_ref, ...), custom_call_target="tpu_custom_call" | custom-call | flops 50000000 | bytes 262144 | tf_op jit(solution)/shard_map/early_edges/pallas_call | solution.py:512
  12.6 0.0 collective-permute-done.1.refs_0_
  12.6 0.1 collective-permute-done.2.refs_1_
  12.7 0.3 %right_edges.2 = (bf16[1152,128]{1,0:T(8,128)(2,1)S(1)}, bf16[1152,128]{1,0:T(8,128)(2,1)S(1)}, bf16[288,128]{1,0:T(8,128)(2,1)S(1)}) custom-call(f32[48,128]{1,0:T(8,128)S(1)} %get-tuple-element.41.live_ref, f32[1,128]{1,0:T(1,128)S(1)} %get-tuple-element.42.gain_ref, ...), custom_call_target="tpu_custom_call", output_to_operand_aliasing={{0}: (5, {}), {1}: (6, {})} | custom-call | flops 50000000 | bytes 262144 | tf_op jit(solution)/shard_map/right_edges/pallas_call | solution.py:512
  13.0 0.0 collective-permute-done.6.refs_0_
  13.0 0.3 %right_edges.3 = (bf16[1152,128]{1,0:T(8,128)(2,1)S(1)}, bf16[1152,128]{1,0:T(8,128)(2,1)S(1)}, bf16[144,128]{1,0:T(8,128)(2,1)S(1)}) custom-call(f32[48,128]{1,0:T(8,128)S(1)} %get-tuple-element.41.live_ref, f32[1,128]{1,0:T(1,128)S(1)} %get-tuple-element.42.gain_ref, ...), custom_call_target="tpu_custom_call", output_to_operand_aliasing={{0}: (4, {}), {1}: (5, {})} | custom-call | flops 50000000 | bytes 262144 | tf_op jit(solution)/shard_map/right_edges/pallas_call | solution.py:512
  13.4 0.3 %collective-permute-start.7 = (bf16[1152,128]{1,0:T(8,128)(2,1)S(1)}, bf16[1152,128]{1,0:T(8,128)(2,1)S(1)}, u32[]{:S(2)}, u32[]{:S(2)}) collective-permute-start(bf16[1152,128]{1,0:T(8,128)(2,1)S(1)} %get-tuple-element.53.refs_2_), channel_id=1, source_target_pairs={{0,1},{1,0},{2,3},{3,2},{4,5},{5,4},{6,7},{7,6},{8,9},{9,8},{10,11... | collective-permute-start | bytes 884744 | tf_op jit(solution)/shard_map/ppermute | solution.py:553
  13.7 1.4 %left_edges.1 = (f32[1152,128]{1,0:T(8,128)S(1)}, f32[1152,128]{1,0:T(8,128)S(1)}, f32[576,128]{1,0:T(8,128)S(1)}) custom-call(bf16[288,128]{1,0:T(8,128)(2,1)S(1)} %get-tuple-element.49.refs_0_, bf16[144,128]{1,0:T(8,128)(2,1)S(1)} %get-tuple-element.52.refs_1_, ...), custom_call_target="tpu_custom_call", output_to_operand_aliasing={{0}: (5, {}), {1}: (6, {})} | custom-call | flops 1500000000 | bytes 262144 | tf_op jit(solution)/shard_map/left_edges/pallas_call | solution.py:512
  15.1 0.0 collective-permute-done.7.other_ref
  15.1 2.0 %product.1 = (bf16[1152,128]{1,0:T(8,128)(2,1)S(1)}, bf16[1152,128]{1,0:T(8,128)(2,1)S(1)}) custom-call(f32[1152,128]{1,0:T(8,128)S(1)} %get-tuple-element.56.left_ref, bf16[1152,128]{1,0:T(8,128)(2,1)S(1)} %collective-permute-done.7.other_ref, f32[576,128]{1,0:T(8,128)S(1)} %get-tuple-element.57.near_ref, f32[1152,128]{1,0:T(8,128)S(1)} %get-tuple-element.58.gate_ref, ...), custom_call_target="tpu_custom_call" | custom-call | flops 2400000000 | bytes 262144 | tf_op jit(solution)/shard_map/product/pallas_call | solution.py:512
  17.1 0.3 %collective-permute-start.8 = (bf16[1152,128]{1,0:T(8,128)(2,1)S(1)}, bf16[1152,128]{1,0:T(8,128)(2,1)S(1)}, u32[]{:S(2)}, u32[]{:S(2)}) collective-permute-start(bf16[1152,128]{1,0:T(8,128)(2,1)S(1)} %get-tuple-element.63.own_ref), channel_id=1, source_target_pairs={{0,1},{1,0},{2,3},{3,2},{4,5},{5,4},{6,7},{7,6},{8,9},{9,8},{10,11... | collective-permute-start | bytes 884744 | tf_op jit(solution)/shard_map/ppermute | solution.py:553
  17.4 0.8 %near_attend.1 = (bf16[6,96,128]{2,1,0:T(8,128)(2,1)S(1)}, f32[144,128]{1,0:T(8,128)S(1)}, f32[6,96,128]{2,1,0:T(8,128)S(1)}, f32[6,96,128]{2,1,0:T(8,128)S(1)}, f32[6,96,128]{2,1,0:T(8,128)S(1)}) custom-call(bf16[1152,128]{1,0:T(8,128)(2,1)S(1)} %get-tuple-element.63.own_ref, bf16[128,512]{1,0:T(8,128)(2,1)S(1)} %get-tuple-element.65.w_att_ref, ...), custom_call_target="tpu_custom_call" | custom-call | flops 1200000000 | bytes 262144 | tf_op jit(solution)/shard_map/near_attend/pallas_call | solution.py:512
  18.2 0.5 %collective-permute-done.8.other_ref = bf16[1152,128]{1,0:T(8,128)(2,1)S(1)} collective-permute-done((bf16[1152,128]{1,0:T(8,128)(2,1)S(1)}, bf16[1152,128]{1,0:T(8,128)(2,1)S(1)}, u32[]{:S(2)}, u32[]{:S(2)}) %collective-permute-start.8) | collective-permute-done | bytes 294944 | tf_op jit(solution)/shard_map/ppermute | solution.py:553
  18.7 1.6 %attend.1 = bf16[3,48,128]{2,1,0:T(8,128)(2,1)} custom-call(bf16[1152,128]{1,0:T(8,128)(2,1)S(1)} %collective-permute-done.8.other_ref, bf16[1152,128]{1,0:T(8,128)(2,1)S(1)} %get-tuple-element.64.mid_ref, bf16[6,96,128]{2,1,0:T(8,128)(2,1)S(1)} %get-tuple-element.69.asked_ref, f32[144,128]{1,0:T(8,128)S(1)} %get-tuple-element.70.gate_ref, ...), custom_call_target="tpu_custom_call" | custom-call | flops 1500000000 | bytes 262144 | tf_op jit(solution)/shard_map/attend/pallas_call | solution.py:512
  (1 shorter events, 0.0 us)
Async XLA Ops:
  0.0 6.8 %collective-permute-start = (bf16[3,48,128]{2,1,0:T(8,128)(2,1)}, bf16[3,48,128]{2,1,0:T(8,128)(2,1)S(1)}, u32[]{:S(2)}, u32[]{:S(2)}) collective-permute-start(bf16[3,48,128]{2,1,0:T(8,128)(2,1)} %refs_14_.1), channel_id=1, source_target_pairs={{0,9},{1,8},{2,11},{3,10},{4,13},{5,12},{6,15},{7,14},{8,1},{9,0},... | collective-permute-start | bytes 110600 | tf_op jit(solution)/shard_map/ppermute | solution.py:553
  3.5 5.9 %collective-permute-start.3 = (bf16[3,48,128]{2,1,0:T(8,128)(2,1)}, bf16[3,48,128]{2,1,0:T(8,128)(2,1)S(1)}, u32[]{:S(2)}, u32[]{:S(2)}) collective-permute-start(bf16[3,48,128]{2,1,0:T(8,128)(2,1)} %refs_14_.1), channel_id=1, source_target_pairs={{0,3},{1,2},{2,1},{3,0},{4,7},{5,6},{6,5},{7,4},{8,11},{9,10},{10,... | collective-permute-start | bytes 110600 | tf_op jit(solution)/shard_map/ppermute | solution.py:553
  5.3 6.0 %collective-permute-start.4 = (bf16[3,48,128]{2,1,0:T(8,128)(2,1)}, bf16[3,48,128]{2,1,0:T(8,128)(2,1)S(1)}, u32[]{:S(2)}, u32[]{:S(2)}) collective-permute-start(bf16[3,48,128]{2,1,0:T(8,128)(2,1)} %refs_14_.1), channel_id=1, source_target_pairs={{0,5},{1,4},{2,7},{3,6},{4,1},{5,0},{6,3},{7,2},{8,13},{9,12},{10,... | collective-permute-start | bytes 110600 | tf_op jit(solution)/shard_map/ppermute | solution.py:553
  6.3 5.5 %collective-permute-start.5 = (bf16[3,48,128]{2,1,0:T(8,128)(2,1)}, bf16[3,48,128]{2,1,0:T(8,128)(2,1)S(1)}, u32[]{:S(2)}, u32[]{:S(2)}) collective-permute-start(bf16[3,48,128]{2,1,0:T(8,128)(2,1)} %refs_14_.1), channel_id=1, source_target_pairs={{0,6},{1,7},{2,4},{3,5},{4,2},{5,3},{6,0},{7,1},{8,14},{9,15},{10,... | collective-permute-start | bytes 110600 | tf_op jit(solution)/shard_map/ppermute | solution.py:553
  6.8 5.8 %collective-permute-start.1 = (bf16[3,48,128]{2,1,0:T(8,128)(2,1)S(1)}, bf16[3,48,128]{2,1,0:T(8,128)(2,1)S(1)}, u32[]{:S(2)}, u32[]{:S(2)}) collective-permute-start(bf16[3,48,128]{2,1,0:T(8,128)(2,1)S(1)} %collective-permute-done.refs_1_), channel_id=1, source_target_pairs={{0,6},{1,7},{2,4},{3,5},{4,2},{5,3},{6,0},{7,1},{8,14},{9,15},{10,... | collective-permute-start | bytes 110600 | tf_op jit(solution)/shard_map/ppermute | solution.py:553
  9.2 3.4 %collective-permute-start.2 = (bf16[3,48,128]{2,1,0:T(8,128)(2,1)S(1)}, bf16[3,48,128]{2,1,0:T(8,128)(2,1)S(1)}, u32[]{:S(2)}, u32[]{:S(2)}) collective-permute-start(bf16[3,48,128]{2,1,0:T(8,128)(2,1)S(1)} %collective-permute-done.refs_1_), channel_id=1, source_target_pairs={{0,5},{1,4},{2,7},{3,6},{4,1},{5,0},{6,3},{7,2},{8,13},{9,12},{10,... | collective-permute-start | bytes 110600 | tf_op jit(solution)/shard_map/ppermute | solution.py:553
  9.4 3.6 %collective-permute-start.6 = (bf16[3,48,128]{2,1,0:T(8,128)(2,1)S(1)}, bf16[3,48,128]{2,1,0:T(8,128)(2,1)S(1)}, u32[]{:S(2)}, u32[]{:S(2)}) collective-permute-start(bf16[3,48,128]{2,1,0:T(8,128)(2,1)S(1)} %collective-permute-done.refs_1_), channel_id=1, source_target_pairs={{0,3},{1,2},{2,1},{3,0},{4,7},{5,6},{6,5},{7,4},{8,11},{9,10},{10,... | collective-permute-start | bytes 110600 | tf_op jit(solution)/shard_map/ppermute | solution.py:553
  13.4 1.7 %collective-permute-start.7 = (bf16[1152,128]{1,0:T(8,128)(2,1)S(1)}, bf16[1152,128]{1,0:T(8,128)(2,1)S(1)}, u32[]{:S(2)}, u32[]{:S(2)}) collective-permute-start(bf16[1152,128]{1,0:T(8,128)(2,1)S(1)} %get-tuple-element.53.refs_2_), channel_id=1, source_target_pairs={{0,1},{1,0},{2,3},{3,2},{4,5},{5,4},{6,7},{7,6},{8,9},{9,8},{10,11... | collective-permute-start | bytes 884744 | tf_op jit(solution)/shard_map/ppermute | solution.py:553
  17.1 1.6 %collective-permute-start.8 = (bf16[1152,128]{1,0:T(8,128)(2,1)S(1)}, bf16[1152,128]{1,0:T(8,128)(2,1)S(1)}, u32[]{:S(2)}, u32[]{:S(2)}) collective-permute-start(bf16[1152,128]{1,0:T(8,128)(2,1)S(1)} %get-tuple-element.63.own_ref), channel_id=1, source_target_pairs={{0,1},{1,0},{2,3},{3,2},{4,5},{5,4},{6,7},{7,6},{8,9},{9,8},{10,11... | collective-permute-start | bytes 884744 | tf_op jit(solution)/shard_map/ppermute | solution.py:553

commit v6 on v4

--- a/solution.py
+++ b/solution.py
@@ -237,37 +237,58 @@
     return pl.ds(pl.multiple_of(place * block_rows, block_rows), block_rows)
 
 
-def take_blocks(pieces, offsets, row_count, residues, live_ref, gain_ref):
+def blocks_of(pieces, row_count):
+    return [ref[at : at + row_count] for ref in pieces for at in range(0, ref.shape[0], row_count)]
+
+
+def masked_norms(pieces, offsets, row_count, live_ref, gain_ref):
     me = lax.axis_index("row")
-    block_rows = row_count * residues
-    blocks = [(ref, at) for ref in pieces for at in range(ref.shape[0] // row_count)]
-    for (ref, at), offset in zip(blocks, offsets, strict=True):
+    for acts, offset in zip(blocks_of(pieces, row_count), offsets, strict=True):
         device = jnp.bitwise_xor(me, offset)
-        acts = ref[at * row_count : (at + 1) * row_count]
         normed = norm_rows(acts.astype(jnp.float32), gain_ref[0:1])
         live_all = live_ref[...]
         rows = [normed[r] * (live_all * live_ref[pl.ds(device * row_count + r, 1), :]) for r in range(row_count)]
-        normed = jnp.concatenate(rows, 0).astype(jnp.bfloat16)
-        yield spot_of(block_rows, device // 2), acts.reshape(block_rows, acts.shape[-1]), normed
+        yield jnp.concatenate(rows, 0).astype(jnp.bfloat16)
+
+
+def parts_of(ref, count):
+    step = ref.shape[0] // count
+    return [ref[at : at + step] for at in range(0, ref.shape[0], step)]
+
+
+def spots_of(offsets, block_rows):
+    me = lax.axis_index("row")
+    return [spot_of(block_rows, jnp.bitwise_xor(me, offset) // 2) for offset in offsets]
 
 
 def early_kernel(offsets, row_count, live_ref, gain_ref, w_right_ref, w_left_ref, w_gate_ref, *refs):
-    pieces, (acts_ref, right_ref, left_ref, gate_ref) = refs[:-4], refs[-4:]
-    residues = live_ref.shape[0]
-    for spot, acts, normed in take_blocks(pieces, offsets, row_count, residues, live_ref, gain_ref):
-        acts_ref[spot] = acts
-        right_ref[spot] = gated_edges(normed, w_right_ref[...])
-        left_ref[spot] = gated_edges(normed, w_left_ref[...]).astype(jnp.float32)
-        gate_ref[spot] = sigmoid(dot(normed, w_gate_ref[...]))
-
-
-def right_kernel(offsets, row_count, live_ref, gain_ref, w_right_ref, *refs):
-    pieces, (_, _, acts_ref, right_ref, normed_ref) = refs[:-5], refs[-5:]
-    residues = live_ref.shape[0]
-    block_rows = row_count * residues
-    blocks = take_blocks(pieces, offsets, row_count, residues, live_ref, gain_ref)
-    for t, (spot, acts, normed) in enumerate(blocks):
-        acts_ref[spot] = acts
+    pieces, (right_ref, left_ref, gate_ref) = refs[:-3], refs[-3:]
+    block_rows = row_count * live_ref.shape[0]
+    for t, normed in enumerate(masked_norms(pieces, offsets, row_count, live_ref, gain_ref)):
+        at = slice(t * block_rows, (t + 1) * block_rows)
+        right_ref[at] = gated_edges(normed, w_right_ref[...])
+        left_ref[at] = gated_edges(normed, w_left_ref[...]).astype(jnp.float32)
+        gate_ref[at] = sigmoid(dot(normed, w_gate_ref[...]))
+
+
+def middle_kernel(offsets, row_count, live_ref, gain_ref, w_right_ref, *refs):
+    pieces, (right_ref, normed_ref) = refs[:-2], refs[-2:]
+    block_rows = row_count * live_ref.shape[0]
+    for t, normed in enumerate(masked_norms(pieces, offsets, row_count, live_ref, gain_ref)):
+        at = slice(t * block_rows, (t + 1) * block_rows)
+        right_ref[at] = gated_edges(normed, w_right_ref[...])
+        normed_ref[at] = normed
+
+
+def right_kernel(done_offsets, offsets, row_count, live_ref, gain_ref, w_right_ref, *refs):
+    done_refs, pieces = refs[: len(done_offsets)], refs[len(done_offsets) : -2]
+    right_ref, normed_ref = refs[-2:]
+    block_rows = row_count * live_ref.shape[0]
+    for ref, held in zip(done_refs, done_offsets, strict=True):
+        for spot, edges in zip(spots_of(held, block_rows), parts_of(ref, len(held)), strict=True):
+            right_ref[spot] = edges
+    normed_blocks = masked_norms(pieces, offsets, row_count, live_ref, gain_ref)
+    for t, (spot, normed) in enumerate(zip(spots_of(offsets, block_rows), normed_blocks, strict=True)):
         right_ref[spot] = gated_edges(normed, w_right_ref[...])
         normed_ref[t * block_rows : (t + 1) * block_rows] = normed
 
@@ -312,16 +333,26 @@
     lax.fori_loop(0, own_count // row_block, rows_of, 0)
 
 
-def left_kernel(
-    offsets, row_count, residues, normed_ref, right_ref, w_left_ref, w_gate_ref, _, __, left_ref, gate_ref, near_ref, turned_ref
-):
-    me = lax.axis_index("row")
+def left_kernel(early, late, row_count, residues, right_ref, w_left_ref, w_gate_ref, early_left_ref, early_gate_ref, *refs):
+    normed_refs, pieces = refs[: len(late)], refs[len(late) : -5]
+    left_ref, gate_ref, acts_ref, near_ref, turned_ref = refs[-5:]
     block_rows = row_count * residues
-    for t, offset in enumerate(offsets):
-        spot = spot_of(block_rows, jnp.bitwise_xor(me, offset) // 2)
-        normed = normed_ref[t * block_rows : (t + 1) * block_rows]
-        left_ref[spot] = gated_edges(normed, w_left_ref[...]).astype(jnp.float32)
-        gate_ref[spot] = sigmoid(dot(normed, w_gate_ref[...]))
+    blocks = zip(
+        spots_of(early, block_rows),
+        parts_of(early_left_ref, len(early)),
+        parts_of(early_gate_ref, len(early)),
+        strict=True,
+    )
+    for spot, edges, gate in blocks:
+        left_ref[spot] = edges
+        gate_ref[spot] = gate
+    for offsets, normed_ref in zip(late, normed_refs, strict=True):
+        for spot, normed in zip(spots_of(offsets, block_rows), parts_of(normed_ref, len(offsets)), strict=True):
+            left_ref[spot] = gated_edges(normed, w_left_ref[...]).astype(jnp.float32)
+            gate_ref[spot] = sigmoid(dot(normed, w_gate_ref[...]))
+    order = early + [offset for offsets in late for offset in offsets]
+    for spot, acts in zip(spots_of(order, block_rows), blocks_of(pieces, row_count), strict=True):
+        acts_ref[spot] = acts.reshape(block_rows, acts.shape[-1])
     turn(right_ref, turned_ref, row_count, residues)
     count = turned_ref.shape[0] // residues
 
@@ -508,14 +539,13 @@
     out_ref[...] = (mid + dot(gated, w_out_ref[...])).astype(jnp.bfloat16).reshape(out_ref.shape)
 
 
-def call(body, args, outs, cost_us, name, scratch=(), aliases=None, space=pltpu.VMEM):
+def call(body, args, outs, cost_us, name, scratch=(), space=pltpu.VMEM):
     return pl.pallas_call(
         body,
         out_shape=[jax.ShapeDtypeStruct(shape, dtype) for shape, dtype in outs],
         in_specs=[pl.BlockSpec(memory_space=space)] * len(args),
         out_specs=[pl.BlockSpec(memory_space=pltpu.VMEM)] * len(outs),
         scratch_shapes=list(scratch),
-        input_output_aliases=aliases or {},
         compiler_params=pltpu.CompilerParams(vmem_limit_bytes=24 * 2**20),
         cost_estimate=pl.CostEstimate(flops=int(cost_us * 1e9), bytes_accessed=2**18, transcendentals=0),
         name=name,
@@ -604,32 +634,47 @@
     from_far_corner = swap(from_far, near ^ side)
     from_far_side = swap(from_far, side)
 
-    sizes = [((pairs, channels), bf16), ((pairs, width), bf16), ((pairs, width), f32), ((pairs, channels), f32)]
-    acts, right, left, gate = call(
-        functools.partial(early_kernel, spread([0, far, side, near, near ^ side]), row_count),
-        [live, in_g, w_r, w_l, w_g, held, from_far, from_side, from_near, from_corner],
-        sizes,
+    early = spread([0, far, side, near, near ^ side])
+    early_pieces = [held, from_far, from_side, from_near, from_corner]
+
+    def rows_like(count, dtype, blocks=None):
+        return (((blocks or own_count // row_count) * block_rows, count), dtype)
+
+    early_right, early_left, early_gate = call(
+        functools.partial(early_kernel, early, row_count),
+        [live, in_g, w_r, w_l, w_g, *early_pieces],
+        [rows_like(width, bf16, len(early)), rows_like(width, f32, len(early)), rows_like(channels, f32, len(early))],
         0.05,
         "early_edges",
     )
-    late = spread([far ^ near ^ side, far ^ near, far ^ side])
-    acts, right, normed = call(
-        functools.partial(right_kernel, late, row_count),
-        [live, in_g, w_r, from_far_corner, from_far_near, from_far_side, acts, right],
-        [*sizes[:2], ((len(late) * block_rows, channels), bf16)],
-        0.5,
+    middle, last = spread([far ^ near ^ side, far ^ near]), spread([far ^ side])
+    middle_pieces, last_pieces = [from_far_corner, from_far_near], [from_far_side]
+    middle_right, middle_normed = call(
+        functools.partial(middle_kernel, middle, row_count),
+        [live, in_g, w_r, *middle_pieces],
+        [rows_like(width, bf16, len(middle)), rows_like(channels, bf16, len(middle))],
+        0.05,
+        "middle_edges",
+    )
+    right, last_normed = call(
+        functools.partial(right_kernel, [early, middle], last, row_count),
+        [live, in_g, w_r, early_right, middle_right, *last_pieces],
+        [rows_like(width, bf16), rows_like(channels, bf16, len(last))],
+        0.05,
         "right_edges",
-        aliases={6: 0, 7: 1},
     )
     other = swap(right, 1)
-    left, gate, near_product = call(
-        functools.partial(left_kernel, late, row_count, residues),
-        [normed, right, w_l, w_g, left, gate],
-        [*sizes[2:], ((own_count * own_count, width), f32)],
+    left, gate, acts, near_product = call(
+        functools.partial(left_kernel, early, [middle, last], row_count, residues),
+        [right, w_l, w_g, early_left, early_gate, middle_normed, last_normed]
+        + early_pieces
+        + middle_pieces
+        + last_pieces,
+        [rows_like(width, f32), rows_like(channels, f32), rows_like(channels, bf16)]
+        + [((own_count * own_count, width), f32)],
         1.5,
         "left_edges",
-        scratch=[pltpu.VMEM((pairs, width), f32)],
-        aliases={4: 0, 5: 1},
+        scratch=[pltpu.VMEM((pairs + own_count, width), f32)],
     )
     mid, normed_mid = call(
         functools.partial(product_kernel, row_count, residues),
@@ -637,7 +682,7 @@
         [((pairs, channels), bf16), ((pairs, channels), bf16)],
         2.4,
         "product",
-        scratch=[pltpu.VMEM((pairs, width), f32), pltpu.VMEM((pairs, width), f32)],
+        scratch=[pltpu.VMEM((pairs + own_count, width), f32), pltpu.VMEM((pairs + 2 * row_count, width), f32)],
     )
     normed_other = swap(normed_mid, 1)
     groups, asked_rows = residues // tile, heads * row_count * tile

time: 20.6 us -> 20.5 us (level)
  Pallas kernels: 8.18 us -> 8.47 us
    pallas_call x7 -> x8, Pallas kernels: 8.18 us -> 8.47 us  [call(): pl.pallas_call(body, out_shape=[jax.ShapeDtypeStruct(shape, dtype) for sh...]
  transfers between devices with their start and end apart: 9 -> 9, of which waited for: 4 -> 3; matrix products, arithmetic and copies ran while one was open for 0% -> 0% of each run, Pallas kernels for 21% -> 22%
where the time goes in v6:
time: 20.5 us; the launch traced here: 20.4 us
  starting transfers between devices  10.6 us (52%)
  Pallas kernels  8.47 us (41%)
  waiting for transfers between devices  1.16 us (6%)
    ppermute x9, starting transfers between devices, swap(): return lax.ppermute(x, 'row', [(i, i ^ shift) for i in range(row_devices)])  10.6 us
    pallas_call x8, Pallas kernels, call(): pl.pallas_call(body, out_shape=[jax.ShapeDtypeStruct(shape, dtype) for sh...  8.47 us
    ppermute x9, waiting for transfers between devices, swap(): return lax.ppermute(x, 'row', [(i, i ^ shift) for i in range(row_devices)])  1.16 us
  transfers between devices with their start and end apart: 9, of which 3 were waited for; matrix products, arithmetic and copies ran while one was open for 0% of the time, Pallas kernels for 22%

profile of v6, /device:TPU:0, one launch (start us, length us, event | category | flops | bytes accessed | tf_op | source)
XLA Modules:
  0.0 20.4 jit_solution(5500891830193314422)
XLA Ops:
  0.0 3.5 %collective-permute-start = (bf16[3,48,128]{2,1,0:T(8,128)(2,1)}, bf16[3,48,128]{2,1,0:T(8,128)(2,1)S(1)}, u32[]{:S(2)}, u32[]{:S(2)}) collective-permute-start(bf16[3,48,128]{2,1,0:T(8,128)(2,1)} %refs_14_.1), channel_id=1, source_target_pairs={{0,9},{1,8},{2,11},{3,10},{4,13},{5,12},{6,15},{7,14},{8,1},{9,0},... | collective-permute-start | bytes 110600 | tf_op jit(solution)/shard_map/ppermute | solution.py:583
  3.5 1.8 %collective-permute-start.1 = (bf16[3,48,128]{2,1,0:T(8,128)(2,1)}, bf16[3,48,128]{2,1,0:T(8,128)(2,1)S(1)}, u32[]{:S(2)}, u32[]{:S(2)}) collective-permute-start(bf16[3,48,128]{2,1,0:T(8,128)(2,1)} %refs_14_.1), channel_id=1, source_target_pairs={{0,3},{1,2},{2,1},{3,0},{4,7},{5,6},{6,5},{7,4},{8,11},{9,10},{10,... | collective-permute-start | bytes 110600 | tf_op jit(solution)/shard_map/ppermute | solution.py:583
  5.3 1.0 %collective-permute-start.2 = (bf16[3,48,128]{2,1,0:T(8,128)(2,1)}, bf16[3,48,128]{2,1,0:T(8,128)(2,1)S(1)}, u32[]{:S(2)}, u32[]{:S(2)}) collective-permute-start(bf16[3,48,128]{2,1,0:T(8,128)(2,1)} %refs_14_.1), channel_id=1, source_target_pairs={{0,5},{1,4},{2,7},{3,6},{4,1},{5,0},{6,3},{7,2},{8,13},{9,12},{10,... | collective-permute-start | bytes 110600 | tf_op jit(solution)/shard_map/ppermute | solution.py:583
  6.3 0.5 %collective-permute-start.3 = (bf16[3,48,128]{2,1,0:T(8,128)(2,1)}, bf16[3,48,128]{2,1,0:T(8,128)(2,1)S(1)}, u32[]{:S(2)}, u32[]{:S(2)}) collective-permute-start(bf16[3,48,128]{2,1,0:T(8,128)(2,1)} %refs_14_.1), channel_id=1, source_target_pairs={{0,6},{1,7},{2,4},{3,5},{4,2},{5,3},{6,0},{7,1},{8,14},{9,15},{10,... | collective-permute-start | bytes 110600 | tf_op jit(solution)/shard_map/ppermute | solution.py:583
  6.8 0.0 collective-permute-done.refs_1_.refs_3_
  6.8 2.4 %collective-permute-start.4 = (bf16[3,48,128]{2,1,0:T(8,128)(2,1)S(1)}, bf16[3,48,128]{2,1,0:T(8,128)(2,1)S(1)}, u32[]{:S(2)}, u32[]{:S(2)}) collective-permute-start(bf16[3,48,128]{2,1,0:T(8,128)(2,1)S(1)} %collective-permute-done.refs_1_.refs_3_), channel_id=1, source_target_pairs={{0,6},{1,7},{2,4},{3,5},{4,2},{5,3},{6,0},{7,1},{8,14},{9,15},{10,... | collective-permute-start | bytes 110600 | tf_op jit(solution)/shard_map/ppermute | solution.py:583
  9.2 0.2 collective-permute-start.5
  9.4 0.0 collective-permute-done.1.refs_2_.refs_4_
  9.4 0.6 %collective-permute-start.6 = (bf16[3,48,128]{2,1,0:T(8,128)(2,1)S(1)}, bf16[3,48,128]{2,1,0:T(8,128)(2,1)S(1)}, u32[]{:S(2)}, u32[]{:S(2)}) collective-permute-start(bf16[3,48,128]{2,1,0:T(8,128)(2,1)S(1)} %collective-permute-done.refs_1_.refs_3_), channel_id=1, source_target_pairs={{0,3},{1,2},{2,1},{3,0},{4,7},{5,6},{6,5},{7,4},{8,11},{9,10},{10,... | collective-permute-start | bytes 110600 | tf_op jit(solution)/shard_map/ppermute | solution.py:583
  10.0 1.2 %stage.1 = (f32[48,128]{1,0:T(8,128)S(1)}, f32[12,192]{1,0:T(8,128)S(1)}, f32[6,192]{1,0:T(8,128)S(1)}, f32[12,192]{1,0:T(8,128)S(1)}, f32[6,192]{1,0:T(8,128)S(...) custom-call(f32[4]{0:T(128)} %refs_0_.1, ...), custom_call_target="tpu_custom_call" | custom-call | flops 50000000 | bytes 262144 | tf_op jit(solution)/shard_map/stage/pallas_call | solution.py:543
  11.2 0.0 collective-permute-done.2.refs_3_.refs_5_
  11.3 0.5 %collective-permute-done.3.refs_4_.refs_6_ = bf16[3,48,128]{2,1,0:T(8,128)(2,1)S(1)} collective-permute-done((bf16[3,48,128]{2,1,0:T(8,128)(2,1)}, bf16[3,48,128]{2,1,0:T(8,128)(2,1)S(1)}, u32[]{:S(2)}, u32[]{:S(2)}) %collective-permute-start.3) | collective-permute-done | bytes 36896 | tf_op jit(solution)/shard_map/ppermute | solution.py:583
  11.8 0.8 %early_edges.1 = (bf16[720,128]{1,0:T(8,128)(2,1)S(1)}, f32[720,128]{1,0:T(8,128)S(1)}, f32[720,128]{1,0:T(8,128)S(1)}) custom-call(f32[48,128]{1,0:T(8,128)S(1)} %get-tuple-element.39.live_ref, f32[1,128]{1,0:T(1,128)S(1)} %get-tuple-element.40.gain_ref, bf16[128,256]{1,0:T(8,128)(2,1)S(1)} %get-tuple-element.41.w_right_ref, ...), custom_call_target="tpu_custom_call" | custom-call | flops 50000000 | bytes 262144 | tf_op jit(solution)/shard_map/early_edges/pallas_call | solution.py:543
  12.6 0.0 collective-permute-done.4.refs_0_.refs_7_
  12.6 0.1 collective-permute-done.5.refs_1_.refs_8_
  12.7 0.3 %middle_edges.1 = (bf16[288,128]{1,0:T(8,128)(2,1)S(1)}, bf16[288,128]{1,0:T(8,128)(2,1)S(1)}) custom-call(f32[48,128]{1,0:T(8,128)S(1)} %get-tuple-element.39.live_ref, f32[1,128]{1,0:T(1,128)S(1)} %get-tuple-element.40.gain_ref, bf16[128,256]{1,0:T(8,128)(2,1)S(1)} %get-tuple-element.41.w_right_ref, ...), custom_call_target="tpu_custom_call" | custom-call | flops 50000000 | bytes 262144 | tf_op jit(solution)/shard_map/middle_edges/pallas_call | solution.py:543
  13.0 0.0 collective-permute-done.6.refs_2_.refs_9_
  13.0 0.3 %right_edges.1 = (bf16[1152,128]{1,0:T(8,128)(2,1)S(1)}, bf16[144,128]{1,0:T(8,128)(2,1)S(1)}) custom-call(f32[48,128]{1,0:T(8,128)S(1)} %get-tuple-element.39.live_ref, f32[1,128]{1,0:T(1,128)S(1)} %get-tuple-element.40.gain_ref, bf16[128,256]{1,0:T(8,128)(2,1)S(1)} %get-tuple-element.41.w_right_ref, bf16[720,128]{1,0:T(8,128)(2,1)S(1)} %get-tuple-element.45.refs_0_, ...), custom_call_target="tpu_custom_call" | custom-call | flops 50000000 | bytes 262144 | tf_op jit(solution)/shard_map/right_edges/pallas_call | solution.py:543
  13.4 0.3 %collective-permute-start.7 = (bf16[1152,128]{1,0:T(8,128)(2,1)S(1)}, bf16[1152,128]{1,0:T(8,128)(2,1)S(1)}, u32[]{:S(2)}, u32[]{:S(2)}) collective-permute-start(bf16[1152,128]{1,0:T(8,128)(2,1)S(1)} %get-tuple-element.47.right_ref), channel_id=1, source_target_pairs={{0,1},{1,0},{2,3},{3,2},{4,5},{5,4},{6,7},{7,6},{8,9},{9,8},{10,11... | collective-permute-start | bytes 884744 | tf_op jit(solution)/shard_map/ppermute | solution.py:583
  13.7 1.4 %left_edges.1 = (f32[1152,128]{1,0:T(8,128)S(1)}, f32[1152,128]{1,0:T(8,128)S(1)}, bf16[1152,128]{1,0:T(8,128)(2,1)S(1)}, f32[576,128]{1,0:T(8,128)S(1)}) custom-call(bf16[1152,128]{1,0:T(8,128)(2,1)S(1)} %get-tuple-element.47.right_ref, bf16[128,256]{1,0:T(8,128)(2,1)S(1)} %get-tuple-element.42.w_left_ref, ...), custom_call_target="tpu_custom_call" | custom-call | flops 1500000000 | bytes 262144 | tf_op jit(solution)/shard_map/left_edges/pallas_call | solution.py:543
  15.1 0.0 collective-permute-done.7.other_ref
  15.1 2.0 %product.1 = (bf16[1152,128]{1,0:T(8,128)(2,1)S(1)}, bf16[1152,128]{1,0:T(8,128)(2,1)S(1)}) custom-call(f32[1152,128]{1,0:T(8,128)S(1)} %get-tuple-element.52.left_ref, bf16[1152,128]{1,0:T(8,128)(2,1)S(1)} %collective-permute-done.7.other_ref, f32[576,128]{1,0:T(8,128)S(1)} %get-tuple-element.53.near_ref, f32[1152,128]{1,0:T(8,128)S(1)} %get-tuple-element.54.gate_ref, ...), custom_call_target="tpu_custom_call" | custom-call | flops 2400000000 | bytes 262144 | tf_op jit(solution)/shard_map/product/pallas_call | solution.py:543
  17.1 0.3 %collective-permute-start.8 = (bf16[1152,128]{1,0:T(8,128)(2,1)S(1)}, bf16[1152,128]{1,0:T(8,128)(2,1)S(1)}, u32[]{:S(2)}, u32[]{:S(2)}) collective-permute-start(bf16[1152,128]{1,0:T(8,128)(2,1)S(1)} %get-tuple-element.59.own_ref), channel_id=1, source_target_pairs={{0,1},{1,0},{2,3},{3,2},{4,5},{5,4},{6,7},{7,6},{8,9},{9,8},{10,11... | collective-permute-start | bytes 884744 | tf_op jit(solution)/shard_map/ppermute | solution.py:583
  17.4 0.8 %near_attend.1 = (bf16[6,96,128]{2,1,0:T(8,128)(2,1)S(1)}, f32[144,128]{1,0:T(8,128)S(1)}, f32[6,96,128]{2,1,0:T(8,128)S(1)}, f32[6,96,128]{2,1,0:T(8,128)S(1)}, f32[6,96,128]{2,1,0:T(8,128)S(1)}) custom-call(bf16[1152,128]{1,0:T(8,128)(2,1)S(1)} %get-tuple-element.59.own_ref, bf16[128,512]{1,0:T(8,128)(2,1)S(1)} %get-tuple-element.61.w_att_ref, ...), custom_call_target="tpu_custom_call" | custom-call | flops 1200000000 | bytes 262144 | tf_op jit(solution)/shard_map/near_attend/pallas_call | solution.py:543
  18.2 0.5 %collective-permute-done.8.other_ref = bf16[1152,128]{1,0:T(8,128)(2,1)S(1)} collective-permute-done((bf16[1152,128]{1,0:T(8,128)(2,1)S(1)}, bf16[1152,128]{1,0:T(8,128)(2,1)S(1)}, u32[]{:S(2)}, u32[]{:S(2)}) %collective-permute-start.8) | collective-permute-done | bytes 294944 | tf_op jit(solution)/shard_map/ppermute | solution.py:583
  18.7 1.6 %attend.1 = bf16[3,48,128]{2,1,0:T(8,128)(2,1)} custom-call(bf16[1152,128]{1,0:T(8,128)(2,1)S(1)} %collective-permute-done.8.other_ref, bf16[1152,128]{1,0:T(8,128)(2,1)S(1)} %get-tuple-element.60.mid_ref, bf16[6,96,128]{2,1,0:T(8,128)(2,1)S(1)} %get-tuple-element.65.asked_ref, f32[144,128]{1,0:T(8,128)S(1)} %get-tuple-element.66.gate_ref, ...), custom_call_target="tpu_custom_call" | custom-call | flops 1500000000 | bytes 262144 | tf_op jit(solution)/shard_map/attend/pallas_call | solution.py:543
  (1 shorter events, 0.0 us)
Async XLA Ops:
  0.0 6.8 %collective-permute-start = (bf16[3,48,128]{2,1,0:T(8,128)(2,1)}, bf16[3,48,128]{2,1,0:T(8,128)(2,1)S(1)}, u32[]{:S(2)}, u32[]{:S(2)}) collective-permute-start(bf16[3,48,128]{2,1,0:T(8,128)(2,1)} %refs_14_.1), channel_id=1, source_target_pairs={{0,9},{1,8},{2,11},{3,10},{4,13},{5,12},{6,15},{7,14},{8,1},{9,0},... | collective-permute-start | bytes 110600 | tf_op jit(solution)/shard_map/ppermute | solution.py:583
  3.5 5.9 %collective-permute-start.1 = (bf16[3,48,128]{2,1,0:T(8,128)(2,1)}, bf16[3,48,128]{2,1,0:T(8,128)(2,1)S(1)}, u32[]{:S(2)}, u32[]{:S(2)}) collective-permute-start(bf16[3,48,128]{2,1,0:T(8,128)(2,1)} %refs_14_.1), channel_id=1, source_target_pairs={{0,3},{1,2},{2,1},{3,0},{4,7},{5,6},{6,5},{7,4},{8,11},{9,10},{10,... | collective-permute-start | bytes 110600 | tf_op jit(solution)/shard_map/ppermute | solution.py:583
  5.3 6.0 %collective-permute-start.2 = (bf16[3,48,128]{2,1,0:T(8,128)(2,1)}, bf16[3,48,128]{2,1,0:T(8,128)(2,1)S(1)}, u32[]{:S(2)}, u32[]{:S(2)}) collective-permute-start(bf16[3,48,128]{2,1,0:T(8,128)(2,1)} %refs_14_.1), channel_id=1, source_target_pairs={{0,5},{1,4},{2,7},{3,6},{4,1},{5,0},{6,3},{7,2},{8,13},{9,12},{10,... | collective-permute-start | bytes 110600 | tf_op jit(solution)/shard_map/ppermute | solution.py:583
  6.3 5.5 %collective-permute-start.3 = (bf16[3,48,128]{2,1,0:T(8,128)(2,1)}, bf16[3,48,128]{2,1,0:T(8,128)(2,1)S(1)}, u32[]{:S(2)}, u32[]{:S(2)}) collective-permute-start(bf16[3,48,128]{2,1,0:T(8,128)(2,1)} %refs_14_.1), channel_id=1, source_target_pairs={{0,6},{1,7},{2,4},{3,5},{4,2},{5,3},{6,0},{7,1},{8,14},{9,15},{10,... | collective-permute-start | bytes 110600 | tf_op jit(solution)/shard_map/ppermute | solution.py:583
  6.8 5.8 %collective-permute-start.4 = (bf16[3,48,128]{2,1,0:T(8,128)(2,1)S(1)}, bf16[3,48,128]{2,1,0:T(8,128)(2,1)S(1)}, u32[]{:S(2)}, u32[]{:S(2)}) collective-permute-start(bf16[3,48,128]{2,1,0:T(8,128)(2,1)S(1)} %collective-permute-done.refs_1_.refs_3_), channel_id=1, source_target_pairs={{0,6},{1,7},{2,4},{3,5},{4,2},{5,3},{6,0},{7,1},{8,14},{9,15},{10,... | collective-permute-start | bytes 110600 | tf_op jit(solution)/shard_map/ppermute | solution.py:583
  9.2 3.4 %collective-permute-start.5 = (bf16[3,48,128]{2,1,0:T(8,128)(2,1)S(1)}, bf16[3,48,128]{2,1,0:T(8,128)(2,1)S(1)}, u32[]{:S(2)}, u32[]{:S(2)}) collective-permute-start(bf16[3,48,128]{2,1,0:T(8,128)(2,1)S(1)} %collective-permute-done.refs_1_.refs_3_), channel_id=1, source_target_pairs={{0,5},{1,4},{2,7},{3,6},{4,1},{5,0},{6,3},{7,2},{8,13},{9,12},{10,... | collective-permute-start | bytes 110600 | tf_op jit(solution)/shard_map/ppermute | solution.py:583
  9.4 3.6 %collective-permute-start.6 = (bf16[3,48,128]{2,1,0:T(8,128)(2,1)S(1)}, bf16[3,48,128]{2,1,0:T(8,128)(2,1)S(1)}, u32[]{:S(2)}, u32[]{:S(2)}) collective-permute-start(bf16[3,48,128]{2,1,0:T(8,128)(2,1)S(1)} %collective-permute-done.refs_1_.refs_3_), channel_id=1, source_target_pairs={{0,3},{1,2},{2,1},{3,0},{4,7},{5,6},{6,5},{7,4},{8,11},{9,10},{10,... | collective-permute-start | bytes 110600 | tf_op jit(solution)/shard_map/ppermute | solution.py:583
  13.4 1.7 %collective-permute-start.7 = (bf16[1152,128]{1,0:T(8,128)(2,1)S(1)}, bf16[1152,128]{1,0:T(8,128)(2,1)S(1)}, u32[]{:S(2)}, u32[]{:S(2)}) collective-permute-start(bf16[1152,128]{1,0:T(8,128)(2,1)S(1)} %get-tuple-element.47.right_ref), channel_id=1, source_target_pairs={{0,1},{1,0},{2,3},{3,2},{4,5},{5,4},{6,7},{7,6},{8,9},{9,8},{10,11... | collective-permute-start | bytes 884744 | tf_op jit(solution)/shard_map/ppermute | solution.py:583
  17.1 1.6 %collective-permute-start.8 = (bf16[1152,128]{1,0:T(8,128)(2,1)S(1)}, bf16[1152,128]{1,0:T(8,128)(2,1)S(1)}, u32[]{:S(2)}, u32[]{:S(2)}) collective-permute-start(bf16[1152,128]{1,0:T(8,128)(2,1)S(1)} %get-tuple-element.59.own_ref), channel_id=1, source_target_pairs={{0,1},{1,0},{2,3},{3,2},{4,5},{5,4},{6,7},{7,6},{8,9},{9,8},{10,11... | collective-permute-start | bytes 884744 | tf_op jit(solution)/shard_map/ppermute | solution.py:583

commit v7 on v6

--- a/solution.py
+++ b/solution.py
@@ -594,9 +594,9 @@
         base = base + [o ^ (shift + 1) for o in base]
         shift //= 2
     from_far = swap(held, far)
+    from_corner = swap(held, near ^ side)
+    from_near = swap(held, near)
     from_side = swap(held, side)
-    from_near = swap(held, near)
-    from_corner = swap(held, near ^ side)
 
     weights = [
         in_gain[None],
@@ -634,8 +634,8 @@
     from_far_corner = swap(from_far, near ^ side)
     from_far_side = swap(from_far, side)
 
-    early = spread([0, far, side, near, near ^ side])
-    early_pieces = [held, from_far, from_side, from_near, from_corner]
+    early = spread([0, far, near ^ side, near, side])
+    early_pieces = [held, from_far, from_corner, from_near, from_side]
 
     def rows_like(count, dtype, blocks=None):
         return (((blocks or own_count // row_count) * block_rows, count), dtype)
@@ -647,8 +647,8 @@
         0.05,
         "early_edges",
     )
-    middle, last = spread([far ^ near ^ side, far ^ near]), spread([far ^ side])
-    middle_pieces, last_pieces = [from_far_corner, from_far_near], [from_far_side]
+    middle, last = spread([far ^ near ^ side]), spread([far ^ near, far ^ side])
+    middle_pieces, last_pieces = [from_far_corner], [from_far_near, from_far_side]
     middle_right, middle_normed = call(
         functools.partial(middle_kernel, middle, row_count),
         [live, in_g, w_r, *middle_pieces],

time: 20.5 us -> 20.4 us (level)
  no operation moved by 1% of the time
where the time goes in v7:
time: 20.4 us; the launch traced here: 20.3 us
  starting transfers between devices  10.5 us (51%)
  Pallas kernels  8.45 us (41%)
  waiting for transfers between devices  1.18 us (6%)
    ppermute x9, starting transfers between devices, swap(): return lax.ppermute(x, 'row', [(i, i ^ shift) for i in range(row_devices)])  10.5 us
    pallas_call x8, Pallas kernels, call(): pl.pallas_call(body, out_shape=[jax.ShapeDtypeStruct(shape, dtype) for sh...  8.45 us
    ppermute x9, waiting for transfers between devices, swap(): return lax.ppermute(x, 'row', [(i, i ^ shift) for i in range(row_devices)])  1.18 us
  transfers between devices with their start and end apart: 9, of which 3 were waited for; matrix products, arithmetic and copies ran while one was open for 0% of the time, Pallas kernels for 22%

profile of v7, /device:TPU:0, one launch (start us, length us, event | category | flops | bytes accessed | tf_op | source)
XLA Modules:
  0.0 20.3 jit_solution(16930530321465520521)
XLA Ops:
  0.0 3.5 %collective-permute-start = (bf16[3,48,128]{2,1,0:T(8,128)(2,1)}, bf16[3,48,128]{2,1,0:T(8,128)(2,1)S(1)}, u32[]{:S(2)}, u32[]{:S(2)}) collective-permute-start(bf16[3,48,128]{2,1,0:T(8,128)(2,1)} %refs_14_.1), channel_id=1, source_target_pairs={{0,9},{1,8},{2,11},{3,10},{4,13},{5,12},{6,15},{7,14},{8,1},{9,0},... | collective-permute-start | bytes 110600 | tf_op jit(solution)/shard_map/ppermute | solution.py:583
  3.5 2.5 %collective-permute-start.1 = (bf16[3,48,128]{2,1,0:T(8,128)(2,1)}, bf16[3,48,128]{2,1,0:T(8,128)(2,1)S(1)}, u32[]{:S(2)}, u32[]{:S(2)}) collective-permute-start(bf16[3,48,128]{2,1,0:T(8,128)(2,1)} %refs_14_.1), channel_id=1, source_target_pairs={{0,6},{1,7},{2,4},{3,5},{4,2},{5,3},{6,0},{7,1},{8,14},{9,15},{10,... | collective-permute-start | bytes 110600 | tf_op jit(solution)/shard_map/ppermute | solution.py:583
  6.0 0.5 %collective-permute-start.2 = (bf16[3,48,128]{2,1,0:T(8,128)(2,1)}, bf16[3,48,128]{2,1,0:T(8,128)(2,1)S(1)}, u32[]{:S(2)}, u32[]{:S(2)}) collective-permute-start(bf16[3,48,128]{2,1,0:T(8,128)(2,1)} %refs_14_.1), channel_id=1, source_target_pairs={{0,5},{1,4},{2,7},{3,6},{4,1},{5,0},{6,3},{7,2},{8,13},{9,12},{10,... | collective-permute-start | bytes 110600 | tf_op jit(solution)/shard_map/ppermute | solution.py:583
  6.5 0.2 collective-permute-start.3
  6.7 0.0 collective-permute-done.refs_1_.refs_3_
  6.7 2.5 %collective-permute-start.4 = (bf16[3,48,128]{2,1,0:T(8,128)(2,1)S(1)}, bf16[3,48,128]{2,1,0:T(8,128)(2,1)S(1)}, u32[]{:S(2)}, u32[]{:S(2)}) collective-permute-start(bf16[3,48,128]{2,1,0:T(8,128)(2,1)S(1)} %collective-permute-done.refs_1_.refs_3_), channel_id=1, source_target_pairs={{0,6},{1,7},{2,4},{3,5},{4,2},{5,3},{6,0},{7,1},{8,14},{9,15},{10,... | collective-permute-start | bytes 110600 | tf_op jit(solution)/shard_map/ppermute | solution.py:583
  9.2 0.2 %collective-permute-start.5 = (bf16[3,48,128]{2,1,0:T(8,128)(2,1)S(1)}, bf16[3,48,128]{2,1,0:T(8,128)(2,1)S(1)}, u32[]{:S(2)}, u32[]{:S(2)}) collective-permute-start(bf16[3,48,128]{2,1,0:T(8,128)(2,1)S(1)} %collective-permute-done.refs_1_.refs_3_), channel_id=1, source_target_pairs={{0,5},{1,4},{2,7},{3,6},{4,1},{5,0},{6,3},{7,2},{8,13},{9,12},{10,... | collective-permute-start | bytes 110600 | tf_op jit(solution)/shard_map/ppermute | solution.py:583
  9.4 0.0 collective-permute-done.1.refs_2_.refs_4_
  9.4 0.5 %collective-permute-start.6 = (bf16[3,48,128]{2,1,0:T(8,128)(2,1)S(1)}, bf16[3,48,128]{2,1,0:T(8,128)(2,1)S(1)}, u32[]{:S(2)}, u32[]{:S(2)}) collective-permute-start(bf16[3,48,128]{2,1,0:T(8,128)(2,1)S(1)} %collective-permute-done.refs_1_.refs_3_), channel_id=1, source_target_pairs={{0,3},{1,2},{2,1},{3,0},{4,7},{5,6},{6,5},{7,4},{8,11},{9,10},{10,... | collective-permute-start | bytes 110600 | tf_op jit(solution)/shard_map/ppermute | solution.py:583
  9.9 1.2 %stage.1 = (f32[48,128]{1,0:T(8,128)S(1)}, f32[12,192]{1,0:T(8,128)S(1)}, f32[6,192]{1,0:T(8,128)S(1)}, f32[12,192]{1,0:T(8,128)S(1)}, f32[6,192]{1,0:T(8,128)S(...) custom-call(f32[4]{0:T(128)} %refs_0_.1, ...), custom_call_target="tpu_custom_call" | custom-call | flops 50000000 | bytes 262144 | tf_op jit(solution)/shard_map/stage/pallas_call | solution.py:543
  11.1 0.0 collective-permute-done.2.refs_3_.refs_5_
  11.1 0.0 collective-permute-done.3.refs_4_.refs_6_
  11.1 0.8 %early_edges.1 = (bf16[720,128]{1,0:T(8,128)(2,1)S(1)}, f32[720,128]{1,0:T(8,128)S(1)}, f32[720,128]{1,0:T(8,128)S(1)}) custom-call(f32[48,128]{1,0:T(8,128)S(1)} %get-tuple-element.39.live_ref, f32[1,128]{1,0:T(1,128)S(1)} %get-tuple-element.40.gain_ref, bf16[128,256]{1,0:T(8,128)(2,1)S(1)} %get-tuple-element.41.w_right_ref, ...), custom_call_target="tpu_custom_call" | custom-call | flops 50000000 | bytes 262144 | tf_op jit(solution)/shard_map/early_edges/pallas_call | solution.py:543
  12.0 0.0 collective-permute-done.4.refs_0_.refs_7_
  12.0 0.3 %middle_edges.1 = (bf16[144,128]{1,0:T(8,128)(2,1)S(1)}, bf16[144,128]{1,0:T(8,128)(2,1)S(1)}) custom-call(f32[48,128]{1,0:T(8,128)S(1)} %get-tuple-element.39.live_ref, f32[1,128]{1,0:T(1,128)S(1)} %get-tuple-element.40.gain_ref, bf16[128,256]{1,0:T(8,128)(2,1)S(1)} %get-tuple-element.41.w_right_ref, ...), custom_call_target="tpu_custom_call" | custom-call | flops 50000000 | bytes 262144 | tf_op jit(solution)/shard_map/middle_edges/pallas_call | solution.py:543
  12.3 0.4 %collective-permute-done.5.refs_2_.refs_8_ = bf16[3,48,128]{2,1,0:T(8,128)(2,1)S(1)} collective-permute-done((bf16[3,48,128]{2,1,0:T(8,128)(2,1)S(1)}, bf16[3,48,128]{2,1,0:T(8,128)(2,1)S(1)}, u32[]{:S(2)}, u32[]{:S(2)}) %collective-permute-start.5) | collective-permute-done | bytes 36896 | tf_op jit(solution)/shard_map/ppermute | solution.py:583
  12.7 0.2 collective-permute-done.6.refs_3_.refs_9_
  12.8 0.3 %right_edges.1 = (bf16[1152,128]{1,0:T(8,128)(2,1)S(1)}, bf16[288,128]{1,0:T(8,128)(2,1)S(1)}) custom-call(f32[48,128]{1,0:T(8,128)S(1)} %get-tuple-element.39.live_ref, f32[1,128]{1,0:T(1,128)S(1)} %get-tuple-element.40.gain_ref, bf16[128,256]{1,0:T(8,128)(2,1)S(1)} %get-tuple-element.41.w_right_ref, bf16[720,128]{1,0:T(8,128)(2,1)S(1)} %get-tuple-element.45.refs_0_, ...), custom_call_target="tpu_custom_call" | custom-call | flops 50000000 | bytes 262144 | tf_op jit(solution)/shard_map/right_edges/pallas_call | solution.py:543
  13.2 0.4 %collective-permute-start.7 = (bf16[1152,128]{1,0:T(8,128)(2,1)S(1)}, bf16[1152,128]{1,0:T(8,128)(2,1)S(1)}, u32[]{:S(2)}, u32[]{:S(2)}) collective-permute-start(bf16[1152,128]{1,0:T(8,128)(2,1)S(1)} %get-tuple-element.47.right_ref), channel_id=1, source_target_pairs={{0,1},{1,0},{2,3},{3,2},{4,5},{5,4},{6,7},{7,6},{8,9},{9,8},{10,11... | collective-permute-start | bytes 884744 | tf_op jit(solution)/shard_map/ppermute | solution.py:583
  13.6 1.4 %left_edges.1 = (f32[1152,128]{1,0:T(8,128)S(1)}, f32[1152,128]{1,0:T(8,128)S(1)}, bf16[1152,128]{1,0:T(8,128)(2,1)S(1)}, f32[576,128]{1,0:T(8,128)S(1)}) custom-call(bf16[1152,128]{1,0:T(8,128)(2,1)S(1)} %get-tuple-element.47.right_ref, bf16[128,256]{1,0:T(8,128)(2,1)S(1)} %get-tuple-element.42.w_left_ref, ...), custom_call_target="tpu_custom_call" | custom-call | flops 1500000000 | bytes 262144 | tf_op jit(solution)/shard_map/left_edges/pallas_call | solution.py:543
  15.0 0.0 collective-permute-done.7.other_ref
  15.0 2.0 %product.1 = (bf16[1152,128]{1,0:T(8,128)(2,1)S(1)}, bf16[1152,128]{1,0:T(8,128)(2,1)S(1)}) custom-call(f32[1152,128]{1,0:T(8,128)S(1)} %get-tuple-element.52.left_ref, bf16[1152,128]{1,0:T(8,128)(2,1)S(1)} %collective-permute-done.7.other_ref, f32[576,128]{1,0:T(8,128)S(1)} %get-tuple-element.53.near_ref, f32[1152,128]{1,0:T(8,128)S(1)} %get-tuple-element.54.gate_ref, ...), custom_call_target="tpu_custom_call" | custom-call | flops 2400000000 | bytes 262144 | tf_op jit(solution)/shard_map/product/pallas_call | solution.py:543
  17.0 0.2 %collective-permute-start.8 = (bf16[1152,128]{1,0:T(8,128)(2,1)S(1)}, bf16[1152,128]{1,0:T(8,128)(2,1)S(1)}, u32[]{:S(2)}, u32[]{:S(2)}) collective-permute-start(bf16[1152,128]{1,0:T(8,128)(2,1)S(1)} %get-tuple-element.59.own_ref), channel_id=1, source_target_pairs={{0,1},{1,0},{2,3},{3,2},{4,5},{5,4},{6,7},{7,6},{8,9},{9,8},{10,11... | collective-permute-start | bytes 884744 | tf_op jit(solution)/shard_map/ppermute | solution.py:583
  17.2 0.8 %near_attend.1 = (bf16[6,96,128]{2,1,0:T(8,128)(2,1)S(1)}, f32[144,128]{1,0:T(8,128)S(1)}, f32[6,96,128]{2,1,0:T(8,128)S(1)}, f32[6,96,128]{2,1,0:T(8,128)S(1)}, f32[6,96,128]{2,1,0:T(8,128)S(1)}) custom-call(bf16[1152,128]{1,0:T(8,128)(2,1)S(1)} %get-tuple-element.59.own_ref, bf16[128,512]{1,0:T(8,128)(2,1)S(1)} %get-tuple-element.61.w_att_ref, ...), custom_call_target="tpu_custom_call" | custom-call | flops 1200000000 | bytes 262144 | tf_op jit(solution)/shard_map/near_attend/pallas_call | solution.py:543
  18.0 0.6 %collective-permute-done.8.other_ref = bf16[1152,128]{1,0:T(8,128)(2,1)S(1)} collective-permute-done((bf16[1152,128]{1,0:T(8,128)(2,1)S(1)}, bf16[1152,128]{1,0:T(8,128)(2,1)S(1)}, u32[]{:S(2)}, u32[]{:S(2)}) %collective-permute-start.8) | collective-permute-done | bytes 294944 | tf_op jit(solution)/shard_map/ppermute | solution.py:583
  18.6 1.6 %attend.1 = bf16[3,48,128]{2,1,0:T(8,128)(2,1)} custom-call(bf16[1152,128]{1,0:T(8,128)(2,1)S(1)} %collective-permute-done.8.other_ref, bf16[1152,128]{1,0:T(8,128)(2,1)S(1)} %get-tuple-element.60.mid_ref, bf16[6,96,128]{2,1,0:T(8,128)(2,1)S(1)} %get-tuple-element.65.asked_ref, f32[144,128]{1,0:T(8,128)S(1)} %get-tuple-element.66.gate_ref, ...), custom_call_target="tpu_custom_call" | custom-call | flops 1500000000 | bytes 262144 | tf_op jit(solution)/shard_map/attend/pallas_call | solution.py:543
  (1 shorter events, 0.0 us)
Async XLA Ops:
  0.0 6.7 %collective-permute-start = (bf16[3,48,128]{2,1,0:T(8,128)(2,1)}, bf16[3,48,128]{2,1,0:T(8,128)(2,1)S(1)}, u32[]{:S(2)}, u32[]{:S(2)}) collective-permute-start(bf16[3,48,128]{2,1,0:T(8,128)(2,1)} %refs_14_.1), channel_id=1, source_target_pairs={{0,9},{1,8},{2,11},{3,10},{4,13},{5,12},{6,15},{7,14},{8,1},{9,0},... | collective-permute-start | bytes 110600 | tf_op jit(solution)/shard_map/ppermute | solution.py:583
  3.5 6.0 %collective-permute-start.1 = (bf16[3,48,128]{2,1,0:T(8,128)(2,1)}, bf16[3,48,128]{2,1,0:T(8,128)(2,1)S(1)}, u32[]{:S(2)}, u32[]{:S(2)}) collective-permute-start(bf16[3,48,128]{2,1,0:T(8,128)(2,1)} %refs_14_.1), channel_id=1, source_target_pairs={{0,6},{1,7},{2,4},{3,5},{4,2},{5,3},{6,0},{7,1},{8,14},{9,15},{10,... | collective-permute-start | bytes 110600 | tf_op jit(solution)/shard_map/ppermute | solution.py:583
  6.0 5.1 %collective-permute-start.2 = (bf16[3,48,128]{2,1,0:T(8,128)(2,1)}, bf16[3,48,128]{2,1,0:T(8,128)(2,1)S(1)}, u32[]{:S(2)}, u32[]{:S(2)}) collective-permute-start(bf16[3,48,128]{2,1,0:T(8,128)(2,1)} %refs_14_.1), channel_id=1, source_target_pairs={{0,5},{1,4},{2,7},{3,6},{4,1},{5,0},{6,3},{7,2},{8,13},{9,12},{10,... | collective-permute-start | bytes 110600 | tf_op jit(solution)/shard_map/ppermute | solution.py:583
  6.5 4.6 %collective-permute-start.3 = (bf16[3,48,128]{2,1,0:T(8,128)(2,1)}, bf16[3,48,128]{2,1,0:T(8,128)(2,1)S(1)}, u32[]{:S(2)}, u32[]{:S(2)}) collective-permute-start(bf16[3,48,128]{2,1,0:T(8,128)(2,1)} %refs_14_.1), channel_id=1, source_target_pairs={{0,3},{1,2},{2,1},{3,0},{4,7},{5,6},{6,5},{7,4},{8,11},{9,10},{10,... | collective-permute-start | bytes 110600 | tf_op jit(solution)/shard_map/ppermute | solution.py:583
  6.7 5.3 %collective-permute-start.4 = (bf16[3,48,128]{2,1,0:T(8,128)(2,1)S(1)}, bf16[3,48,128]{2,1,0:T(8,128)(2,1)S(1)}, u32[]{:S(2)}, u32[]{:S(2)}) collective-permute-start(bf16[3,48,128]{2,1,0:T(8,128)(2,1)S(1)} %collective-permute-done.refs_1_.refs_3_), channel_id=1, source_target_pairs={{0,6},{1,7},{2,4},{3,5},{4,2},{5,3},{6,0},{7,1},{8,14},{9,15},{10,... | collective-permute-start | bytes 110600 | tf_op jit(solution)/shard_map/ppermute | solution.py:583
  9.2 3.4 %collective-permute-start.5 = (bf16[3,48,128]{2,1,0:T(8,128)(2,1)S(1)}, bf16[3,48,128]{2,1,0:T(8,128)(2,1)S(1)}, u32[]{:S(2)}, u32[]{:S(2)}) collective-permute-start(bf16[3,48,128]{2,1,0:T(8,128)(2,1)S(1)} %collective-permute-done.refs_1_.refs_3_), channel_id=1, source_target_pairs={{0,5},{1,4},{2,7},{3,6},{4,1},{5,0},{6,3},{7,2},{8,13},{9,12},{10,... | collective-permute-start | bytes 110600 | tf_op jit(solution)/shard_map/ppermute | solution.py:583
  9.4 3.4 %collective-permute-start.6 = (bf16[3,48,128]{2,1,0:T(8,128)(2,1)S(1)}, bf16[3,48,128]{2,1,0:T(8,128)(2,1)S(1)}, u32[]{:S(2)}, u32[]{:S(2)}) collective-permute-start(bf16[3,48,128]{2,1,0:T(8,128)(2,1)S(1)} %collective-permute-done.refs_1_.refs_3_), channel_id=1, source_target_pairs={{0,3},{1,2},{2,1},{3,0},{4,7},{5,6},{6,5},{7,4},{8,11},{9,10},{10,... | collective-permute-start | bytes 110600 | tf_op jit(solution)/shard_map/ppermute | solution.py:583
  13.2 1.8 %collective-permute-start.7 = (bf16[1152,128]{1,0:T(8,128)(2,1)S(1)}, bf16[1152,128]{1,0:T(8,128)(2,1)S(1)}, u32[]{:S(2)}, u32[]{:S(2)}) collective-permute-start(bf16[1152,128]{1,0:T(8,128)(2,1)S(1)} %get-tuple-element.47.right_ref), channel_id=1, source_target_pairs={{0,1},{1,0},{2,3},{3,2},{4,5},{5,4},{6,7},{7,6},{8,9},{9,8},{10,11... | collective-permute-start | bytes 884744 | tf_op jit(solution)/shard_map/ppermute | solution.py:583
  17.0 1.6 %collective-permute-start.8 = (bf16[1152,128]{1,0:T(8,128)(2,1)S(1)}, bf16[1152,128]{1,0:T(8,128)(2,1)S(1)}, u32[]{:S(2)}, u32[]{:S(2)}) collective-permute-start(bf16[1152,128]{1,0:T(8,128)(2,1)S(1)} %get-tuple-element.59.own_ref), channel_id=1, source_target_pairs={{0,1},{1,0},{2,3},{3,2},{4,5},{5,4},{6,7},{7,6},{8,9},{9,8},{10,11... | collective-permute-start | bytes 884744 | tf_op jit(solution)/shard_map/ppermute | solution.py:583

commit v8 on v7

--- a/solution.py
+++ b/solution.py
@@ -324,7 +324,7 @@
             return tuple(out)
 
         zeros = tuple(jnp.zeros((tile, left_ref.shape[1]), jnp.float32) for _ in range(row_block * tiles))
-        totals = lax.fori_loop(0, residues, add, zeros, unroll=16)
+        totals = lax.fori_loop(0, residues, add, zeros, unroll=24)
         for a in range(row_block):
             for t in range(tiles):
                 store(first + a, t, totals[a * tiles + t])

time: 20.4 us -> 20.4 us (level)
  no operation moved by 1% of the time
where the time goes in v8:
time: 20.4 us; the launch traced here: 20.2 us
  starting transfers between devices  10.6 us (52%)
  Pallas kernels  8.41 us (41%)
  waiting for transfers between devices  1.17 us (6%)
    ppermute x9, starting transfers between devices, swap(): return lax.ppermute(x, 'row', [(i, i ^ shift) for i in range(row_devices)])  10.6 us
    pallas_call x8, Pallas kernels, call(): pl.pallas_call(body, out_shape=[jax.ShapeDtypeStruct(shape, dtype) for sh...  8.41 us
    ppermute x9, waiting for transfers between devices, swap(): return lax.ppermute(x, 'row', [(i, i ^ shift) for i in range(row_devices)])  1.17 us
  transfers between devices with their start and end apart: 9, of which 3 were waited for; matrix products, arithmetic and copies ran while one was open for 0% of the time, Pallas kernels for 22%

profile of v8, /device:TPU:0, one launch (start us, length us, event | category | flops | bytes accessed | tf_op | source)
XLA Modules:
  0.0 20.2 jit_solution(14280667036347915161)
XLA Ops:
  0.0 3.5 %collective-permute-start = (bf16[3,48,128]{2,1,0:T(8,128)(2,1)}, bf16[3,48,128]{2,1,0:T(8,128)(2,1)S(1)}, u32[]{:S(2)}, u32[]{:S(2)}) collective-permute-start(bf16[3,48,128]{2,1,0:T(8,128)(2,1)} %refs_14_.1), channel_id=1, source_target_pairs={{0,9},{1,8},{2,11},{3,10},{4,13},{5,12},{6,15},{7,14},{8,1},{9,0},... | collective-permute-start | bytes 110600 | tf_op jit(solution)/shard_map/ppermute | solution.py:583
  3.5 2.5 %collective-permute-start.1 = (bf16[3,48,128]{2,1,0:T(8,128)(2,1)}, bf16[3,48,128]{2,1,0:T(8,128)(2,1)S(1)}, u32[]{:S(2)}, u32[]{:S(2)}) collective-permute-start(bf16[3,48,128]{2,1,0:T(8,128)(2,1)} %refs_14_.1), channel_id=1, source_target_pairs={{0,6},{1,7},{2,4},{3,5},{4,2},{5,3},{6,0},{7,1},{8,14},{9,15},{10,... | collective-permute-start | bytes 110600 | tf_op jit(solution)/shard_map/ppermute | solution.py:583
  6.0 0.5 %collective-permute-start.2 = (bf16[3,48,128]{2,1,0:T(8,128)(2,1)}, bf16[3,48,128]{2,1,0:T(8,128)(2,1)S(1)}, u32[]{:S(2)}, u32[]{:S(2)}) collective-permute-start(bf16[3,48,128]{2,1,0:T(8,128)(2,1)} %refs_14_.1), channel_id=1, source_target_pairs={{0,5},{1,4},{2,7},{3,6},{4,1},{5,0},{6,3},{7,2},{8,13},{9,12},{10,... | collective-permute-start | bytes 110600 | tf_op jit(solution)/shard_map/ppermute | solution.py:583
  6.5 0.2 collective-permute-start.3
  6.7 0.0 collective-permute-done.refs_1_.refs_3_
  6.7 2.5 %collective-permute-start.4 = (bf16[3,48,128]{2,1,0:T(8,128)(2,1)S(1)}, bf16[3,48,128]{2,1,0:T(8,128)(2,1)S(1)}, u32[]{:S(2)}, u32[]{:S(2)}) collective-permute-start(bf16[3,48,128]{2,1,0:T(8,128)(2,1)S(1)} %collective-permute-done.refs_1_.refs_3_), channel_id=1, source_target_pairs={{0,6},{1,7},{2,4},{3,5},{4,2},{5,3},{6,0},{7,1},{8,14},{9,15},{10,... | collective-permute-start | bytes 110600 | tf_op jit(solution)/shard_map/ppermute | solution.py:583
  9.2 0.2 %collective-permute-start.5 = (bf16[3,48,128]{2,1,0:T(8,128)(2,1)S(1)}, bf16[3,48,128]{2,1,0:T(8,128)(2,1)S(1)}, u32[]{:S(2)}, u32[]{:S(2)}) collective-permute-start(bf16[3,48,128]{2,1,0:T(8,128)(2,1)S(1)} %collective-permute-done.refs_1_.refs_3_), channel_id=1, source_target_pairs={{0,5},{1,4},{2,7},{3,6},{4,1},{5,0},{6,3},{7,2},{8,13},{9,12},{10,... | collective-permute-start | bytes 110600 | tf_op jit(solution)/shard_map/ppermute | solution.py:583
  9.4 0.0 collective-permute-done.1.refs_2_.refs_4_
  9.4 0.5 %collective-permute-start.6 = (bf16[3,48,128]{2,1,0:T(8,128)(2,1)S(1)}, bf16[3,48,128]{2,1,0:T(8,128)(2,1)S(1)}, u32[]{:S(2)}, u32[]{:S(2)}) collective-permute-start(bf16[3,48,128]{2,1,0:T(8,128)(2,1)S(1)} %collective-permute-done.refs_1_.refs_3_), channel_id=1, source_target_pairs={{0,3},{1,2},{2,1},{3,0},{4,7},{5,6},{6,5},{7,4},{8,11},{9,10},{10,... | collective-permute-start | bytes 110600 | tf_op jit(solution)/shard_map/ppermute | solution.py:583
  9.9 1.2 %stage.1 = (f32[48,128]{1,0:T(8,128)S(1)}, f32[12,192]{1,0:T(8,128)S(1)}, f32[6,192]{1,0:T(8,128)S(1)}, f32[12,192]{1,0:T(8,128)S(1)}, f32[6,192]{1,0:T(8,128)S(...) custom-call(f32[4]{0:T(128)} %refs_0_.1, ...), custom_call_target="tpu_custom_call" | custom-call | flops 50000000 | bytes 262144 | tf_op jit(solution)/shard_map/stage/pallas_call | solution.py:543
  11.1 0.0 collective-permute-done.2.refs_3_.refs_5_
  11.1 0.0 collective-permute-done.3.refs_4_.refs_6_
  11.1 0.8 %early_edges.1 = (bf16[720,128]{1,0:T(8,128)(2,1)S(1)}, f32[720,128]{1,0:T(8,128)S(1)}, f32[720,128]{1,0:T(8,128)S(1)}) custom-call(f32[48,128]{1,0:T(8,128)S(1)} %get-tuple-element.39.live_ref, f32[1,128]{1,0:T(1,128)S(1)} %get-tuple-element.40.gain_ref, bf16[128,256]{1,0:T(8,128)(2,1)S(1)} %get-tuple-element.41.w_right_ref, ...), custom_call_target="tpu_custom_call" | custom-call | flops 50000000 | bytes 262144 | tf_op jit(solution)/shard_map/early_edges/pallas_call | solution.py:543
  12.0 0.0 collective-permute-done.4.refs_0_.refs_7_
  12.0 0.3 %middle_edges.1 = (bf16[144,128]{1,0:T(8,128)(2,1)S(1)}, bf16[144,128]{1,0:T(8,128)(2,1)S(1)}) custom-call(f32[48,128]{1,0:T(8,128)S(1)} %get-tuple-element.39.live_ref, f32[1,128]{1,0:T(1,128)S(1)} %get-tuple-element.40.gain_ref, bf16[128,256]{1,0:T(8,128)(2,1)S(1)} %get-tuple-element.41.w_right_ref, ...), custom_call_target="tpu_custom_call" | custom-call | flops 50000000 | bytes 262144 | tf_op jit(solution)/shard_map/middle_edges/pallas_call | solution.py:543
  12.3 0.4 %collective-permute-done.5.refs_2_.refs_8_ = bf16[3,48,128]{2,1,0:T(8,128)(2,1)S(1)} collective-permute-done((bf16[3,48,128]{2,1,0:T(8,128)(2,1)S(1)}, bf16[3,48,128]{2,1,0:T(8,128)(2,1)S(1)}, u32[]{:S(2)}, u32[]{:S(2)}) %collective-permute-start.5) | collective-permute-done | bytes 36896 | tf_op jit(solution)/shard_map/ppermute | solution.py:583
  12.7 0.2 collective-permute-done.6.refs_3_.refs_9_
  12.8 0.3 %right_edges.1 = (bf16[1152,128]{1,0:T(8,128)(2,1)S(1)}, bf16[288,128]{1,0:T(8,128)(2,1)S(1)}) custom-call(f32[48,128]{1,0:T(8,128)S(1)} %get-tuple-element.39.live_ref, f32[1,128]{1,0:T(1,128)S(1)} %get-tuple-element.40.gain_ref, bf16[128,256]{1,0:T(8,128)(2,1)S(1)} %get-tuple-element.41.w_right_ref, bf16[720,128]{1,0:T(8,128)(2,1)S(1)} %get-tuple-element.45.refs_0_, ...), custom_call_target="tpu_custom_call" | custom-call | flops 50000000 | bytes 262144 | tf_op jit(solution)/shard_map/right_edges/pallas_call | solution.py:543
  13.2 0.4 %collective-permute-start.7 = (bf16[1152,128]{1,0:T(8,128)(2,1)S(1)}, bf16[1152,128]{1,0:T(8,128)(2,1)S(1)}, u32[]{:S(2)}, u32[]{:S(2)}) collective-permute-start(bf16[1152,128]{1,0:T(8,128)(2,1)S(1)} %get-tuple-element.47.right_ref), channel_id=1, source_target_pairs={{0,1},{1,0},{2,3},{3,2},{4,5},{5,4},{6,7},{7,6},{8,9},{9,8},{10,11... | collective-permute-start | bytes 884744 | tf_op jit(solution)/shard_map/ppermute | solution.py:583
  13.6 1.4 %left_edges.1 = (f32[1152,128]{1,0:T(8,128)S(1)}, f32[1152,128]{1,0:T(8,128)S(1)}, bf16[1152,128]{1,0:T(8,128)(2,1)S(1)}, f32[576,128]{1,0:T(8,128)S(1)}) custom-call(bf16[1152,128]{1,0:T(8,128)(2,1)S(1)} %get-tuple-element.47.right_ref, bf16[128,256]{1,0:T(8,128)(2,1)S(1)} %get-tuple-element.42.w_left_ref, ...), custom_call_target="tpu_custom_call" | custom-call | flops 1500000000 | bytes 262144 | tf_op jit(solution)/shard_map/left_edges/pallas_call | solution.py:543
  15.0 0.0 collective-permute-done.7.other_ref
  15.0 1.9 %product.1 = (bf16[1152,128]{1,0:T(8,128)(2,1)S(1)}, bf16[1152,128]{1,0:T(8,128)(2,1)S(1)}) custom-call(f32[1152,128]{1,0:T(8,128)S(1)} %get-tuple-element.52.left_ref, bf16[1152,128]{1,0:T(8,128)(2,1)S(1)} %collective-permute-done.7.other_ref, f32[576,128]{1,0:T(8,128)S(1)} %get-tuple-element.53.near_ref, f32[1152,128]{1,0:T(8,128)S(1)} %get-tuple-element.54.gate_ref, ...), custom_call_target="tpu_custom_call" | custom-call | flops 2400000000 | bytes 262144 | tf_op jit(solution)/shard_map/product/pallas_call | solution.py:543
  16.9 0.2 %collective-permute-start.8 = (bf16[1152,128]{1,0:T(8,128)(2,1)S(1)}, bf16[1152,128]{1,0:T(8,128)(2,1)S(1)}, u32[]{:S(2)}, u32[]{:S(2)}) collective-permute-start(bf16[1152,128]{1,0:T(8,128)(2,1)S(1)} %get-tuple-element.59.own_ref), channel_id=1, source_target_pairs={{0,1},{1,0},{2,3},{3,2},{4,5},{5,4},{6,7},{7,6},{8,9},{9,8},{10,11... | collective-permute-start | bytes 884744 | tf_op jit(solution)/shard_map/ppermute | solution.py:583
  17.2 0.8 %near_attend.1 = (bf16[6,96,128]{2,1,0:T(8,128)(2,1)S(1)}, f32[144,128]{1,0:T(8,128)S(1)}, f32[6,96,128]{2,1,0:T(8,128)S(1)}, f32[6,96,128]{2,1,0:T(8,128)S(1)}, f32[6,96,128]{2,1,0:T(8,128)S(1)}) custom-call(bf16[1152,128]{1,0:T(8,128)(2,1)S(1)} %get-tuple-element.59.own_ref, bf16[128,512]{1,0:T(8,128)(2,1)S(1)} %get-tuple-element.61.w_att_ref, ...), custom_call_target="tpu_custom_call" | custom-call | flops 1200000000 | bytes 262144 | tf_op jit(solution)/shard_map/near_attend/pallas_call | solution.py:543
  18.0 0.6 %collective-permute-done.8.other_ref = bf16[1152,128]{1,0:T(8,128)(2,1)S(1)} collective-permute-done((bf16[1152,128]{1,0:T(8,128)(2,1)S(1)}, bf16[1152,128]{1,0:T(8,128)(2,1)S(1)}, u32[]{:S(2)}, u32[]{:S(2)}) %collective-permute-start.8) | collective-permute-done | bytes 294944 | tf_op jit(solution)/shard_map/ppermute | solution.py:583
  18.6 1.6 %attend.1 = bf16[3,48,128]{2,1,0:T(8,128)(2,1)} custom-call(bf16[1152,128]{1,0:T(8,128)(2,1)S(1)} %collective-permute-done.8.other_ref, bf16[1152,128]{1,0:T(8,128)(2,1)S(1)} %get-tuple-element.60.mid_ref, bf16[6,96,128]{2,1,0:T(8,128)(2,1)S(1)} %get-tuple-element.65.asked_ref, f32[144,128]{1,0:T(8,128)S(1)} %get-tuple-element.66.gate_ref, ...), custom_call_target="tpu_custom_call" | custom-call | flops 1500000000 | bytes 262144 | tf_op jit(solution)/shard_map/attend/pallas_call | solution.py:543
  (1 shorter events, 0.0 us)
Async XLA Ops:
  0.0 6.7 %collective-permute-start = (bf16[3,48,128]{2,1,0:T(8,128)(2,1)}, bf16[3,48,128]{2,1,0:T(8,128)(2,1)S(1)}, u32[]{:S(2)}, u32[]{:S(2)}) collective-permute-start(bf16[3,48,128]{2,1,0:T(8,128)(2,1)} %refs_14_.1), channel_id=1, source_target_pairs={{0,9},{1,8},{2,11},{3,10},{4,13},{5,12},{6,15},{7,14},{8,1},{9,0},... | collective-permute-start | bytes 110600 | tf_op jit(solution)/shard_map/ppermute | solution.py:583
  3.5 6.0 %collective-permute-start.1 = (bf16[3,48,128]{2,1,0:T(8,128)(2,1)}, bf16[3,48,128]{2,1,0:T(8,128)(2,1)S(1)}, u32[]{:S(2)}, u32[]{:S(2)}) collective-permute-start(bf16[3,48,128]{2,1,0:T(8,128)(2,1)} %refs_14_.1), channel_id=1, source_target_pairs={{0,6},{1,7},{2,4},{3,5},{4,2},{5,3},{6,0},{7,1},{8,14},{9,15},{10,... | collective-permute-start | bytes 110600 | tf_op jit(solution)/shard_map/ppermute | solution.py:583
  6.0 5.1 %collective-permute-start.2 = (bf16[3,48,128]{2,1,0:T(8,128)(2,1)}, bf16[3,48,128]{2,1,0:T(8,128)(2,1)S(1)}, u32[]{:S(2)}, u32[]{:S(2)}) collective-permute-start(bf16[3,48,128]{2,1,0:T(8,128)(2,1)} %refs_14_.1), channel_id=1, source_target_pairs={{0,5},{1,4},{2,7},{3,6},{4,1},{5,0},{6,3},{7,2},{8,13},{9,12},{10,... | collective-permute-start | bytes 110600 | tf_op jit(solution)/shard_map/ppermute | solution.py:583
  6.5 4.6 %collective-permute-start.3 = (bf16[3,48,128]{2,1,0:T(8,128)(2,1)}, bf16[3,48,128]{2,1,0:T(8,128)(2,1)S(1)}, u32[]{:S(2)}, u32[]{:S(2)}) collective-permute-start(bf16[3,48,128]{2,1,0:T(8,128)(2,1)} %refs_14_.1), channel_id=1, source_target_pairs={{0,3},{1,2},{2,1},{3,0},{4,7},{5,6},{6,5},{7,4},{8,11},{9,10},{10,... | collective-permute-start | bytes 110600 | tf_op jit(solution)/shard_map/ppermute | solution.py:583
  6.7 5.3 %collective-permute-start.4 = (bf16[3,48,128]{2,1,0:T(8,128)(2,1)S(1)}, bf16[3,48,128]{2,1,0:T(8,128)(2,1)S(1)}, u32[]{:S(2)}, u32[]{:S(2)}) collective-permute-start(bf16[3,48,128]{2,1,0:T(8,128)(2,1)S(1)} %collective-permute-done.refs_1_.refs_3_), channel_id=1, source_target_pairs={{0,6},{1,7},{2,4},{3,5},{4,2},{5,3},{6,0},{7,1},{8,14},{9,15},{10,... | collective-permute-start | bytes 110600 | tf_op jit(solution)/shard_map/ppermute | solution.py:583
  9.2 3.4 %collective-permute-start.5 = (bf16[3,48,128]{2,1,0:T(8,128)(2,1)S(1)}, bf16[3,48,128]{2,1,0:T(8,128)(2,1)S(1)}, u32[]{:S(2)}, u32[]{:S(2)}) collective-permute-start(bf16[3,48,128]{2,1,0:T(8,128)(2,1)S(1)} %collective-permute-done.refs_1_.refs_3_), channel_id=1, source_target_pairs={{0,5},{1,4},{2,7},{3,6},{4,1},{5,0},{6,3},{7,2},{8,13},{9,12},{10,... | collective-permute-start | bytes 110600 | tf_op jit(solution)/shard_map/ppermute | solution.py:583
  9.4 3.4 %collective-permute-start.6 = (bf16[3,48,128]{2,1,0:T(8,128)(2,1)S(1)}, bf16[3,48,128]{2,1,0:T(8,128)(2,1)S(1)}, u32[]{:S(2)}, u32[]{:S(2)}) collective-permute-start(bf16[3,48,128]{2,1,0:T(8,128)(2,1)S(1)} %collective-permute-done.refs_1_.refs_3_), channel_id=1, source_target_pairs={{0,3},{1,2},{2,1},{3,0},{4,7},{5,6},{6,5},{7,4},{8,11},{9,10},{10,... | collective-permute-start | bytes 110600 | tf_op jit(solution)/shard_map/ppermute | solution.py:583
  13.2 1.8 %collective-permute-start.7 = (bf16[1152,128]{1,0:T(8,128)(2,1)S(1)}, bf16[1152,128]{1,0:T(8,128)(2,1)S(1)}, u32[]{:S(2)}, u32[]{:S(2)}) collective-permute-start(bf16[1152,128]{1,0:T(8,128)(2,1)S(1)} %get-tuple-element.47.right_ref), channel_id=1, source_target_pairs={{0,1},{1,0},{2,3},{3,2},{4,5},{5,4},{6,7},{7,6},{8,9},{9,8},{10,11... | collective-permute-start | bytes 884744 | tf_op jit(solution)/shard_map/ppermute | solution.py:583
  16.9 1.6 %collective-permute-start.8 = (bf16[1152,128]{1,0:T(8,128)(2,1)S(1)}, bf16[1152,128]{1,0:T(8,128)(2,1)S(1)}, u32[]{:S(2)}, u32[]{:S(2)}) collective-permute-start(bf16[1152,128]{1,0:T(8,128)(2,1)S(1)} %get-tuple-element.59.own_ref), channel_id=1, source_target_pairs={{0,1},{1,0},{2,3},{3,2},{4,5},{5,4},{6,7},{7,6},{8,9},{9,8},{10,11... | collective-permute-start | bytes 884744 | tf_op jit(solution)/shard_map/ppermute | solution.py:583
